TPU v7x, 512 devices: a whole 4x8x8 slice. The times are simulated.
512 devices in a mesh: dp: 32 (over z, y_lo), tensor: 4 (over x), precond: 4 (over y_hi, core).
Axes of the slice: x: 4, y: 8 (y_hi: 2, y_lo: 4; y = y_hi * 4 + y_lo), z: 8, core: 2. Of those that a mesh axis runs over, the one named last changes fastest.
Arguments:
- x_in: bfloat16 [4096, 2048], P('dp', 'precond'), may hold values from -12 to 12
- grad_out: bfloat16 [4096, 2048], P('dp', 'tensor'), may hold values from -12 to 12
- weight: bfloat16 [2048, 2048], P('precond', 'tensor'), may hold values from -0.125 to 0.125
Outputs:
- layer_out: bfloat16 [4096, 2048], P('dp', 'tensor')
- grad_in: bfloat16 [4096, 2048], P('dp', 'precond')
- left_root: float32 [4, 512, 2048], P('precond', 'dp', 'tensor')
- right_root: float32 [4, 512, 2048], P('precond', 'dp', 'tensor')
All inputs are finite; a program needn't handle non-finite values.
Results may differ from a plain program's by a relative error of at most 0.013.
Values may be sent and summed in bfloat16 or wider, within the bound.
No kernel may reach another device: no remote copies, remote signals or barrier semaphores. Data moves between devices by JAX's collectives and lax.ppermute only.
A program may use at most 64 MiB of HBM per device.

v0:
```python
import jax
import jax.numpy as jnp
from jax import lax
from jax.sharding import PartitionSpec as P

ITERS = 6


def batched(left, right):
    return jnp.einsum(
        "bij,bjk->bik",
        left,
        right,
        preferred_element_type=jnp.float32,
        precision=lax.Precision.HIGHEST,
    )


def gather_moment(moment_rows):
    return lax.all_gather(moment_rows.astype(jnp.bfloat16), "dp", axis=1, tiled=True).astype(
        moment_rows.dtype
    )


def shards(x_in, grad_out, weight):
    extent = weight.shape[0]
    groups = lax.axis_size("dp")
    slab = extent // groups
    tokens_all = x_in.shape[0] * groups
    layer_terms = jnp.dot(x_in, weight, preferred_element_type=jnp.float32)
    layer_out = lax.psum(layer_terms.astype(jnp.bfloat16), "precond")
    input_terms = lax.dot_general(
        grad_out, weight, (((1,), (1,)), ((), ())), preferred_element_type=jnp.float32
    )
    grad_in = lax.psum(input_terms.astype(jnp.bfloat16), "tensor")
    grad_slab = lax.psum_scatter(
        (
            lax.dot_general(
                x_in, grad_out, (((0,), (0,)), ((), ())), preferred_element_type=jnp.float32
            )
            / tokens_all
        ).astype(jnp.bfloat16),
        "dp",
        scatter_dimension=0,
        tiled=True,
    )
    grad_low = lax.all_gather(grad_slab, "dp", axis=0, tiled=True)
    identity = jnp.eye(extent, dtype=jnp.float32)
    left_stat = lax.dot_general(
        grad_low, grad_low, (((1,), (1,)), ((), ())), preferred_element_type=jnp.float32
    )
    right_stat = lax.dot_general(
        grad_low, grad_low, (((0,), (0,)), ((), ())), preferred_element_type=jnp.float32
    )
    statistic = jnp.stack([left_stat, right_stat]) + 1e-06 * identity
    scaling = 0.4 * jnp.sqrt(jnp.sum(statistic * statistic, axis=(1, 2), keepdims=True) + 1e-06)
    moment = statistic / scaling
    first_row = lax.axis_index("dp") * slab
    row_ids = first_row + lax.broadcasted_iota(jnp.int32, (slab, extent), 0)
    column_ids = lax.broadcasted_iota(jnp.int32, (slab, extent), 1)
    own_identity = jnp.where(row_ids == column_ids, 1.0, 0.0).astype(jnp.float32)
    inverse = own_identity[None] * scaling ** (-0.25)
    for iteration in range(ITERS):
        factor = (5.0 * identity - moment) / 4.0
        inverse = batched(inverse, factor)
        if iteration + 1 < ITERS:
            moment_rows = lax.dynamic_slice_in_dim(moment, first_row, slab, 1)
            for power in range(4):
                moment_rows = batched(moment_rows, factor)
            moment = gather_moment(moment_rows)
    return (layer_out, grad_in, inverse[0][None], inverse[1][None])


def solution(mesh):
    in_specs = (P("dp", "precond"), P("dp", "tensor"), P("precond", "tensor"))
    out_specs = (
        P("dp", "tensor"),
        P("dp", "precond"),
        P("precond", "dp", "tensor"),
        P("precond", "dp", "tensor"),
    )
    return jax.shard_map(shards, mesh=mesh, in_specs=in_specs, out_specs=out_specs, check_vma=False)
```

profile of v0, /device:TPU:6, one launch (start us, length us, event | category | flops | bytes accessed | tf_op | source)
XLA Modules:
  0.0 1074.1 jit_solution(16199245505458368972)
XLA Ops:
  8.1 2.2 fusion.25
  11.5 166.5 %reduce-scatter.2.cloned.1.call-done = bf16[16,512]{1,0:T(8,128)(2,1)} async-done(((bf16[512,512]{1,0:T(8,128)(2,1)}), bf16[16,512]{1,0:T(8,128)(2,1)}) %reduce-scatter.2.cloned.1.call-update) | async-done | bytes 16400 | tf_op jit(solution)/shard_map/reduce_scatter | solution.py:36
  178.0 78.1 %all_gather.18 = bf16[512,512]{1,0:T(8,128)(2,1)S(1)} all-gather(bf16[16,512]{1,0:T(8,128)(2,1)} %reduce-scatter.2.cloned.1.call-done), channel_id=1, replica_groups=mesh['dp'=32,'tensor'=4,'precond'=4] {'dp'}, dimensions={0}, use_global_device_ids=true | all-gather | bytes 540672 | tf_op jit(solution)/shard_map/all_gather | solution.py:47
  262.3 1.9 convolution_convert_fusion.2
  264.3 153.6 %all-gather.6.cloned.1.call-done = bf16[2,512,512]{2,1,0:T(8,128)(2,1)} async-done(((bf16[2,16,512]{2,1,0:T(8,128)(2,1)}), bf16[2,512,512]{2,1,0:T(8,128)(2,1)}) %all-gather.6.cloned.1.call-update) | async-done | bytes 1048592 | tf_op jit(solution)/shard_map/all_gather | solution.py:20
  417.9 2.3 fusion.22
  420.3 1.3 fusion.21
  421.6 1.3 fusion.20
  422.9 1.9 fusion.26
  425.0 153.3 %all-gather.8.cloned.1.call-done = bf16[2,512,512]{2,1,0:T(8,128)(2,1)} async-done(((bf16[2,16,512]{2,1,0:T(8,128)(2,1)}), bf16[2,512,512]{2,1,0:T(8,128)(2,1)}) %all-gather.8.cloned.1.call-update) | async-done | bytes 1048592 | tf_op jit(solution)/shard_map/all_gather | solution.py:20
  578.4 2.3 fusion.17
  580.7 1.3 fusion.16
  582.0 1.3 fusion.15
  583.3 1.9 fusion.27
  585.3 153.5 %all-gather.10.cloned.1.call-done = bf16[2,512,512]{2,1,0:T(8,128)(2,1)} async-done(((bf16[2,16,512]{2,1,0:T(8,128)(2,1)}), bf16[2,512,512]{2,1,0:T(8,128)(2,1)}) %all-gather.10.cloned.1.call-update) | async-done | bytes 1048592 | tf_op jit(solution)/shard_map/all_gather | solution.py:20
  738.8 2.3 fusion.12
  741.2 1.3 fusion.11
  742.5 1.3 fusion.10
  743.8 1.9 fusion.28
  746.0 153.3 %all-gather.12.cloned.1.call-done = bf16[2,512,512]{2,1,0:T(8,128)(2,1)} async-done(((bf16[2,16,512]{2,1,0:T(8,128)(2,1)}), bf16[2,512,512]{2,1,0:T(8,128)(2,1)}) %all-gather.12.cloned.1.call-update) | async-done | bytes 1048592 | tf_op jit(solution)/shard_map/all_gather | solution.py:20
  899.3 2.3 fusion.7
  903.0 1.3 fusion.5
  904.3 1.9 fusion.29
  908.3 2.9 fusion.33
  911.2 1.3 fusion.23
  912.6 1.3 fusion.18
  913.9 1.3 fusion.13
  915.2 1.3 fusion.8
  916.5 143.9 %all-gather.14.cloned.1.call-done = bf16[2,512,512]{2,1,0:T(8,128)(2,1)} async-done(((bf16[2,16,512]{2,1,0:T(8,128)(2,1)}), bf16[2,512,512]{2,1,0:T(8,128)(2,1)}) %all-gather.14.cloned.1.call-update) | async-done | bytes 1048592 | tf_op jit(solution)/shard_map/all_gather | solution.py:20
  1060.4 2.5 fusion
  1063.5 1.6 copy.9
  1065.1 1.6 copy.10
  (58 shorter events, 12.2 us)
Async XLA Ops:
  8.0 898.3 %copy-start = (bf16[512,512]{1,0:T(8,128)(2,1)S(1)}, bf16[512,512]{1,0:T(8,128)(2,1)}, u32[]{:S(2)}) copy-start(bf16[512,512]{1,0:T(8,128)(2,1)} %param.5) | copy-start | bytes 1572868
  8.0 170.0 %reduce-scatter.2.cloned.1.call-start = ((), (), s32[]{:S(2)}) async-start(), calls=%async_computation.3 | async-start | bytes 540672 | tf_op jit(solution)/shard_map/reduce_scatter | solution.py:36
  10.2 407.7 %all-gather.6.cloned.1.call-start = ((), (), s32[]{:S(2)}) async-start(), calls=%async_computation.4 | async-start | bytes 1081344 | tf_op jit(solution)/shard_map/all_gather | solution.py:20
  256.1 1.2 copy-start.9
  258.4 3.9 copy-start.1
  264.2 314.2 %all-gather.8.cloned.1.call-start = ((), (), s32[]{:S(2)}) async-start(), calls=%async_computation.5 | async-start | bytes 1081344 | tf_op jit(solution)/shard_map/all_gather | solution.py:20
  417.9 2.4 copy-start.2
  424.8 314.0 %all-gather.10.cloned.1.call-start = ((), (), s32[]{:S(2)}) async-start(), calls=%async_computation.6 | async-start | bytes 1081344 | tf_op jit(solution)/shard_map/all_gather | solution.py:20
  578.4 2.4 copy-start.3
  585.3 314.0 %all-gather.12.cloned.1.call-start = ((), (), s32[]{:S(2)}) async-start(), calls=%async_computation.7 | async-start | bytes 1081344 | tf_op jit(solution)/shard_map/all_gather | solution.py:20
  738.8 2.4 copy-start.5
  745.7 314.6 %all-gather.14.cloned.1.call-start = ((), (), s32[]{:S(2)}) async-start(), calls=%async_computation.8 | async-start | bytes 1081344 | tf_op jit(solution)/shard_map/all_gather | solution.py:20
  899.3 2.4 copy-start.7
  903.0 3.3 copy-start.10
  904.3 3.0 copy-start.11
  906.2 157.3 %all-reduce.3.cloned.1.call-start = ((), (), s32[]{:S(2)}) async-start(), calls=%async_computation.1 | async-start | bytes 262144 | tf_op jit(solution)/shard_map/psum | solution.py:31
  907.2 156.3 %all-reduce.5.cloned.1.call-start = ((), (), s32[]{:S(2)}) async-start(), calls=%async_computation.2 | async-start | bytes 262144 | tf_op jit(solution)/shard_map/psum | solution.py:35
  908.3 4.2 copy-start.4
  911.2 2.6 copy-start.6
  912.5 2.6 copy-start.8
Sparse Core Ops, SparseCore 0:
  11.6 166.3 reduce-scatter.1
  264.3 153.5 all-gather.5
  424.9 153.4 all-gather.7
  585.4 153.4 all-gather.9
  745.8 153.4 all-gather.11
  906.3 154.0 all-gather.13
Sparse Core Ops, SparseCore 1:
  910.1 57.8 all-reduce.2
  970.9 47.5 all-reduce.4
where the time goes:
time: 1070 us
  waiting for transfers between devices  924 us (86%)
  blocking collectives  78.1 us (7%)
  matrix products  48.7 us (5%)
  between operations  15.7 us (1%)
    all_gather x5, waiting for transfers between devices, gather_moment(): lax.all_gather(moment_rows.astype(jnp.bfloat16), 'dp', axis=1, tiled=True)  758 us
    reduce_scatter x1, waiting for transfers between devices, shards(): lax.psum_scatter((lax.dot_general(x_in, grad_out, (((0,), (0,)), ((), ())...  166 us
    all_gather x1, blocking collectives, shards(): grad_low = lax.all_gather(grad_slab, 'dp', axis=0, tiled=True)  78.1 us
    dot_general x26, matrix products, batched(): jnp.einsum('bij,bjk->bik', left, right, preferred_element_type=jnp.float3...  43.8 us
  transfers between devices with their start and end apart: 8, of which 6 were waited for; matrix products, arithmetic and copies ran while one was open for 1% of the time, Pallas kernels for 0%

commit v1 on v0

v1 whole, which is shorter than its diff:
```python
import functools

import jax
import jax.numpy as jnp
from jax import lax
from jax.experimental import pallas as pl
from jax.experimental.pallas import tpu as pltpu
from jax.sharding import PartitionSpec as P

ITERS = 6
Y_LO = 4
VMEM = pl.BlockSpec(memory_space=pltpu.VMEM)
SMEM = pl.BlockSpec(memory_space=pltpu.SMEM)
F32 = jnp.float32
BF16 = jnp.bfloat16


def mm(left, right, dims=((1,), (0,))):
    return lax.dot_general(left, right, (dims, ((), ())), preferred_element_type=F32)


def grad_kernel(tokens_all, x_ref, g_ref, grad_ref):
    grad = mm(x_ref[...], g_ref[...], ((0,), (0,)))
    grad_ref[...] = (grad * (1.0 / tokens_all)).astype(BF16)


def sum_kernel(parts_ref, out_ref):
    groups, slab = parts_ref.shape[0] // out_ref.shape[0], out_ref.shape[0]
    total = parts_ref[:slab, :].astype(F32)
    for k in range(1, groups):
        total = total + parts_ref[k * slab : (k + 1) * slab, :].astype(F32)
    out_ref[...] = total.astype(BF16)


def outputs_kernel(place_ref, x_ref, g_ref, w_ref, *rest):
    parts = (len(rest) - 2) // 2
    layer_refs, input_refs, (layer_all, input_all) = rest[:parts], rest[parts : 2 * parts], rest[2 * parts :]
    layer_all[...] = mm(x_ref[...], w_ref[...]).astype(BF16)
    input_all[...] = mm(g_ref[...], w_ref[...], ((1,), (1,))).astype(BF16)
    chunk = x_ref.shape[0] // parts
    for d in range(parts):
        for refs, whole, own in ((layer_refs, layer_all, place_ref[0]), (input_refs, input_all, place_ref[1])):
            start = pl.multiple_of(lax.rem(own + d, parts) * chunk, chunk)
            refs[d][...] = whole[pl.ds(start, chunk), :]


def place_kernel(place_ref, *refs):
    parts = (len(refs) - 2) // 2
    for which in range(2):
        out = refs[2 * parts + which]
        chunk = out.shape[0] // parts
        for d in range(parts):
            start = pl.multiple_of(lax.rem(place_ref[which] + parts - d, parts) * chunk, chunk)
            out[pl.ds(start, chunk), :] = refs[which * parts + d][...]


def newton_kernel(slab, place_ref, *refs):
    groups = len(refs) - 5
    chunk_refs = refs[:groups]
    left_ref, right_ref, block, wide, low = refs[groups:]
    extent = block.shape[0]
    z, y = place_ref[0], place_ref[1]
    for d in range(groups):
        base = lax.rem(z + groups - d, groups) * (Y_LO * slab)
        for e in range(Y_LO):
            start = pl.multiple_of(base + lax.rem(y + Y_LO - e, Y_LO) * slab, slab)
            block[pl.ds(start, slab), :] = chunk_refs[d][e * slab : (e + 1) * slab, :]
    first_row = pl.multiple_of((z * Y_LO + y) * slab, slab)
    row_ids = lax.broadcasted_iota(jnp.int32, (extent, extent), 0)
    column_ids = lax.broadcasted_iota(jnp.int32, (extent, extent), 1)
    own_rows = first_row + lax.broadcasted_iota(jnp.int32, (slab, extent), 0)
    own_columns = lax.broadcasted_iota(jnp.int32, (slab, extent), 1)
    b = block[...]
    rows = []
    for which in range(2):
        stat = mm(b, b, ((1,), (1,))) if which == 0 else mm(b, b, ((0,), (0,)))
        stat = jnp.where(row_ids == column_ids, stat + 1e-06, stat)
        square = jnp.sum(jnp.sum(stat * stat, axis=0, keepdims=True), axis=1, keepdims=True)
        scaling = 0.4 * jnp.sqrt(square + 1e-06)
        quarter = stat * (0.25 / scaling)
        wide[which] = quarter
        low[which] = quarter.astype(BF16)
        start = 1.0 / jnp.sqrt(jnp.sqrt(scaling))
        eye = jnp.where(own_rows == own_columns, 1.25, 0.0)
        rows.append(start * (eye - wide[which, pl.ds(first_row, slab), :]))

    def step(_, rows):
        new = []
        for which in range(2):
            n_low = low[which]
            n_wide = wide[which]
            c = mm(n_low, n_low) - 2.5 * n_wide
            c_low = c.astype(BF16)
            h = (3.125 * c + mm(c_low, c_low)).astype(BF16)
            n_new = 2.44140625 * n_wide + mm(h, n_low)
            wide[which] = n_new
            new_low = n_new.astype(BF16)
            low[which] = new_low
            new.append(1.25 * rows[which] - mm(rows[which].astype(BF16), new_low))
        return tuple(new)

    rows = lax.fori_loop(0, ITERS - 2, step, tuple(rows))
    ends = list(rows)
    for _ in range(4):
        for which in range(2):
            ends[which] = 1.25 * ends[which] - mm(ends[which].astype(BF16), low[which])
    for which, out in ((0, left_ref), (1, right_ref)):
        out[0] = 1.25 * rows[which] - mm(ends[which].astype(BF16), low[which])


def shifted(values, axis, pairs):
    return lax.ppermute(values, axis, pairs)


def exchange_reduce(pieces, axis):
    parts = len(pieces)
    got = [
        shifted(pieces[d], axis, [(i, (i + d) % parts) for i in range(parts)]) for d in range(1, parts)
    ]
    total = pieces[0].astype(F32)
    for piece in got:
        total = total + piece.astype(F32)
    return total.astype(BF16)


def exchange_gather(piece, axis, parts):
    return [piece] + [
        shifted(piece, axis, [(i, (i + d) % parts) for i in range(parts)]) for d in range(1, parts)
    ]


def shards(x_in, grad_out, weight):
    extent = weight.shape[0]
    tokens = x_in.shape[0]
    groups = lax.axis_size("dp")
    slab = extent // groups
    z_size = groups // Y_LO
    tensor, precond = lax.axis_size("tensor"), lax.axis_size("precond")
    parts = tensor
    place = jnp.stack([lax.axis_index("precond"), lax.axis_index("tensor")]).astype(jnp.int32)
    me = lax.axis_index("dp")
    block_place = jnp.stack([lax.div(me, Y_LO), lax.rem(me, Y_LO)]).astype(jnp.int32)

    grad_part = pl.pallas_call(
        functools.partial(grad_kernel, tokens * groups),
        out_shape=jax.ShapeDtypeStruct((extent, extent), BF16),
        in_specs=[VMEM, VMEM],
        out_specs=VMEM,
        compiler_params=pltpu.CompilerParams(vmem_limit_bytes=32 * 2**20),
        cost_estimate=pl.CostEstimate(flops=2 * tokens * extent * extent, bytes_accessed=2**20, transcendentals=0),
        name="grad_part",
    )(x_in, grad_out)
    received = lax.all_to_all(grad_part, "dp", 0, 0, tiled=True)
    mine = pl.pallas_call(
        sum_kernel,
        out_shape=jax.ShapeDtypeStruct((slab, extent), BF16),
        in_specs=[VMEM],
        out_specs=VMEM,
        cost_estimate=pl.CostEstimate(flops=extent * extent, bytes_accessed=2**19, transcendentals=0),
        name="grad_sum",
    )(received)

    piece = jax.ShapeDtypeStruct((tokens // parts, extent), BF16)
    pieces = pl.pallas_call(
        outputs_kernel,
        out_shape=[piece] * (2 * parts),
        in_specs=[SMEM, VMEM, VMEM, VMEM],
        out_specs=[VMEM] * (2 * parts),
        scratch_shapes=[pltpu.VMEM((tokens, extent), BF16)] * 2,
        compiler_params=pltpu.CompilerParams(vmem_limit_bytes=32 * 2**20),
        cost_estimate=pl.CostEstimate(flops=4 * tokens * extent * extent, bytes_accessed=2**21, transcendentals=0),
        name="outputs_part",
    )(place, x_in, grad_out, weight)
    layer_mine = exchange_reduce(pieces[:parts], "precond")
    input_mine = exchange_reduce(pieces[parts:], "tensor")
    outputs_in = exchange_gather(layer_mine, "precond", parts) + exchange_gather(input_mine, "tensor", parts)

    near = [mine]
    for d in range(1, Y_LO):
        pairs = [(z * Y_LO + y, z * Y_LO + (y + d) % Y_LO) for z in range(z_size) for y in range(Y_LO)]
        near.append(shifted(mine, "dp", pairs))
    near = jnp.concatenate(near, axis=0)
    chunks = [near]
    for d in range(1, z_size):
        pairs = [(z * Y_LO + y, ((z + d) % z_size) * Y_LO + y) for z in range(z_size) for y in range(Y_LO)]
        chunks.append(shifted(near, "dp", pairs))

    whole = jax.ShapeDtypeStruct((tokens, extent), BF16)
    layer_out, grad_in = pl.pallas_call(
        place_kernel,
        out_shape=[whole, whole],
        in_specs=[SMEM] + [VMEM] * (2 * parts),
        out_specs=[VMEM, VMEM],
        cost_estimate=pl.CostEstimate(flops=0, bytes_accessed=2**19, transcendentals=0),
        name="place",
    )(place, *outputs_in)

    root = jax.ShapeDtypeStruct((1, slab, extent), F32)
    left_root, right_root = pl.pallas_call(
        functools.partial(newton_kernel, slab),
        out_shape=[root, root],
        in_specs=[SMEM] + [VMEM] * z_size,
        out_specs=[VMEM, VMEM],
        scratch_shapes=[
            pltpu.VMEM((extent, extent), BF16),
            pltpu.VMEM((2, extent, extent), F32),
            pltpu.VMEM((2, extent, extent), BF16),
        ],
        compiler_params=pltpu.CompilerParams(vmem_limit_bytes=48 * 2**20),
        cost_estimate=pl.CostEstimate(flops=60 * extent**3, bytes_accessed=2**20, transcendentals=0),
        name="newton",
    )(block_place, *chunks)
    return layer_out, grad_in, left_root, right_root


def solution(mesh):
    in_specs = (P("dp", "precond"), P("dp", "tensor"), P("precond", "tensor"))
    out_specs = (
        P("dp", "tensor"),
        P("dp", "precond"),
        P("precond", "dp", "tensor"),
        P("precond", "dp", "tensor"),
    )
    return jax.shard_map(shards, mesh=mesh, in_specs=in_specs, out_specs=out_specs, check_vma=False)
```

time: 1070 us -> 127 us (0.12)
  waiting for transfers between devices: 924 us -> 1.6 us
  starting transfers between devices: 0.74 us -> 103 us
  blocking collectives: 78.1 us -> 0 us
  matrix products: 48.7 us -> 0 us
  Pallas kernels: 0 us -> 17.5 us
  between operations: 15.7 us -> 1.14 us
    all_gather x5 -> x0, waiting for transfers between devices: 758 us -> none  [gather_moment(): lax.all_gather(moment_rows.astype(jnp.bfloat16), 'dp', axis=1, tiled=True)]
    reduce_scatter x1 -> x0, waiting for transfers between devices: 166 us -> none  [shards(): lax.psum_scatter((lax.dot_general(x_in, grad_out, (((0,), (0,)), ((), ())...]
    ppermute x0 -> x22, starting transfers between devices: none -> 88.9 us  [shifted(): return lax.ppermute(values, axis, pairs)]
    all_gather x1 -> x0, blocking collectives: 78.1 us -> none  [shards(): grad_low = lax.all_gather(grad_slab, 'dp', axis=0, tiled=True)]
    dot_general x31 -> x0, matrix products: 48.7 us -> none  [the longest x26 43.8 us: batched(): jnp.einsum('bij,bjk->bik', left, right, preferred_element_type=jnp.float3...]
    pallas_call x0 -> x5, Pallas kernels: none -> 17.5 us  [the longest x1 12.1 us: shards(): pl.pallas_call(functools.partial(newton_kernel, slab), out_shape=[root, r...]
    all_to_all x0 -> x1, starting transfers between devices: none -> 13.9 us  [shards(): received = lax.all_to_all(grad_part, 'dp', 0, 0, tiled=True)]
  transfers between devices with their start and end apart: 8 -> 23, of which waited for: 6 -> 2; matrix products, arithmetic and copies ran while one was open for 1% -> 0% of each run, Pallas kernels for 0% -> 3%
where the time goes in v1:
time: 127 us; the launch traced here: 126 us
  starting transfers between devices  103 us (81%)
  Pallas kernels  17.5 us (14%)
  local copies, waits for them, and re-layouts  2.64 us (2%)
  waiting for transfers between devices  1.6 us (1%)
    ppermute x22, starting transfers between devices, shifted(): return lax.ppermute(values, axis, pairs)  88.9 us
    all_to_all x1, starting transfers between devices, shards(): received = lax.all_to_all(grad_part, 'dp', 0, 0, tiled=True)  13.9 us
    pallas_call x1, Pallas kernels, shards(): pl.pallas_call(functools.partial(newton_kernel, slab), out_shape=[root, r...  12.1 us
    unnamed x32, local copies, waits for them, and re-layouts  2.64 us
  transfers between devices with their start and end apart: 23, of which 2 were waited for; matrix products, arithmetic and copies ran while one was open for 0% of the time, Pallas kernels for 3%

profile of v1, /device:TPU:6, one launch (start us, length us, event | category | flops | bytes accessed | tf_op | source)
XLA Modules:
  0.0 125.9 jit_solution(14223140199951159985)
XLA Ops:
  0.6 0.9 copy-done.1
  1.5 0.9 copy-done.3
  2.4 1.1 grad_part.1
  3.5 13.9 %all-to-all-start = ((bf16[32,16,512]{2,1,0:T(8,128)(2,1)}), bf16[32,16,512]{2,1,0:T(8,128)(2,1)S(1)}, u32[]{:S(2)}, u32[]{:S(2)}) async-start(bf16[32,16,512]{2,1,0:T(8,128)(2,1)} %bitcast.4), calls=%async_computation | async-start | bytes 1048576 | tf_op jit(solution)/shard_map/all_to_all | solution.py:153
  17.5 1.0 outputs_part.1
  18.5 2.4 %collective-permute-start.6 = (bf16[32,512]{1,0:T(8,128)(2,1)S(1)}, bf16[32,512]{1,0:T(8,128)(2,1)S(1)}, u32[]{:S(2)}, u32[]{:S(2)}) collective-permute-start(bf16[32,512]{1,0:T(8,128)(2,1)S(1)} %get-tuple-element.21), channel_id=1, source_target_pairs={{0,4},{4,8},{8,12},{12,0},{1,5},{5,9},{9,13},{13,1},{2,6},{6,10},{... | collective-permute-start | bytes 98312 | tf_op jit(solution)/shard_map/ppermute | solution.py:112
  20.9 4.3 %collective-permute-start.7 = (bf16[32,512]{1,0:T(8,128)(2,1)S(1)}, bf16[32,512]{1,0:T(8,128)(2,1)S(1)}, u32[]{:S(2)}, u32[]{:S(2)}) collective-permute-start(bf16[32,512]{1,0:T(8,128)(2,1)S(1)} %get-tuple-element.22), channel_id=1, source_target_pairs={{0,8},{4,12},{8,0},{12,4},{1,9},{5,13},{9,1},{13,5},{2,10},{6,14},... | collective-permute-start | bytes 98312 | tf_op jit(solution)/shard_map/ppermute | solution.py:112
  25.2 1.9 %collective-permute-start.8 = (bf16[32,512]{1,0:T(8,128)(2,1)S(1)}, bf16[32,512]{1,0:T(8,128)(2,1)S(1)}, u32[]{:S(2)}, u32[]{:S(2)}) collective-permute-start(bf16[32,512]{1,0:T(8,128)(2,1)S(1)} %get-tuple-element.23), channel_id=1, source_target_pairs={{0,12},{4,0},{8,4},{12,8},{1,13},{5,1},{9,5},{13,9},{2,14},{6,2},{... | collective-permute-start | bytes 98312 | tf_op jit(solution)/shard_map/ppermute | solution.py:112
  27.2 1.9 %collective-permute-start = (bf16[32,512]{1,0:T(8,128)(2,1)S(1)}, bf16[32,512]{1,0:T(8,128)(2,1)S(1)}, u32[]{:S(2)}, u32[]{:S(2)}) collective-permute-start(bf16[32,512]{1,0:T(8,128)(2,1)S(1)} %get-tuple-element.17), channel_id=1, source_target_pairs={{0,1},{1,2},{2,3},{3,0},{4,5},{5,6},{6,7},{7,4},{8,9},{9,10},{10,1... | collective-permute-start | bytes 98312 | tf_op jit(solution)/shard_map/ppermute | solution.py:112
  29.1 5.0 %collective-permute-start.1 = (bf16[32,512]{1,0:T(8,128)(2,1)S(1)}, bf16[32,512]{1,0:T(8,128)(2,1)S(1)}, u32[]{:S(2)}, u32[]{:S(2)}) collective-permute-start(bf16[32,512]{1,0:T(8,128)(2,1)S(1)} %get-tuple-element.18), channel_id=1, source_target_pairs={{0,2},{1,3},{2,0},{3,1},{4,6},{5,7},{6,4},{7,5},{8,10},{9,11},{10,... | collective-permute-start | bytes 98312 | tf_op jit(solution)/shard_map/ppermute | solution.py:112
  34.6 0.8 copy-done.6
  35.4 1.7 %grad_sum.1 = bf16[16,512]{1,0:T(8,128)(2,1)} custom-call(bf16[512,512]{1,0:T(8,128)(2,1)} %bitcast.6), custom_call_target="tpu_custom_call" | custom-call | flops 262144 | bytes 524288 | tf_op jit(solution)/shard_map/grad_sum/pallas_call | solution.py:154
  37.1 3.4 %collective-permute-start.12 = (bf16[16,512]{1,0:T(8,128)(2,1)}, bf16[16,512]{1,0:T(8,128)(2,1)S(1)}, u32[]{:S(2)}, u32[]{:S(2)}) collective-permute-start(bf16[16,512]{1,0:T(8,128)(2,1)} %grad_sum.1), channel_id=1, source_target_pairs={{0,16},{16,32},{32,48},{48,0},{64,80},{80,96},{96,112},{112,64},{1... | collective-permute-start | bytes 49160 | tf_op jit(solution)/shard_map/ppermute | solution.py:112
  40.5 4.1 %collective-permute-start.13 = (bf16[16,512]{1,0:T(8,128)(2,1)}, bf16[16,512]{1,0:T(8,128)(2,1)S(1)}, u32[]{:S(2)}, u32[]{:S(2)}) collective-permute-start(bf16[16,512]{1,0:T(8,128)(2,1)} %grad_sum.1), channel_id=1, source_target_pairs={{0,32},{16,48},{32,0},{48,16},{64,96},{80,112},{96,64},{112,80},{1... | collective-permute-start | bytes 49160 | tf_op jit(solution)/shard_map/ppermute | solution.py:112
  44.6 3.4 %collective-permute-start.14 = (bf16[16,512]{1,0:T(8,128)(2,1)}, bf16[16,512]{1,0:T(8,128)(2,1)S(1)}, u32[]{:S(2)}, u32[]{:S(2)}) collective-permute-start(bf16[16,512]{1,0:T(8,128)(2,1)} %grad_sum.1), channel_id=1, source_target_pairs={{0,48},{16,0},{32,16},{48,32},{64,112},{80,64},{96,80},{112,96},{1... | collective-permute-start | bytes 49160 | tf_op jit(solution)/shard_map/ppermute | solution.py:112
  48.1 6.4 %collective-permute-start.2 = (bf16[32,512]{1,0:T(8,128)(2,1)S(1)}, bf16[32,512]{1,0:T(8,128)(2,1)S(1)}, u32[]{:S(2)}, u32[]{:S(2)}) collective-permute-start(bf16[32,512]{1,0:T(8,128)(2,1)S(1)} %get-tuple-element.19), channel_id=1, source_target_pairs={{0,3},{1,0},{2,1},{3,2},{4,7},{5,4},{6,5},{7,6},{8,11},{9,8},{10,9... | collective-permute-start | bytes 98312 | tf_op jit(solution)/shard_map/ppermute | solution.py:112
  54.5 5.2 %collective-permute-start.10 = (bf16[32,512]{1,0:T(8,128)(2,1)S(1)}, bf16[32,512]{1,0:T(8,128)(2,1)S(1)}, u32[]{:S(2)}, u32[]{:S(2)}) collective-permute-start(bf16[32,512]{1,0:T(8,128)(2,1)S(1)} %add_convert_fusion.refs_4_), channel_id=1, source_target_pairs={{0,8},{4,12},{8,0},{12,4},{1,9},{5,13},{9,1},{13,5},{2,10},{6,14},... | collective-permute-start | bytes 98312 | tf_op jit(solution)/shard_map/ppermute | solution.py:112
  59.7 2.7 %collective-permute-start.11 = (bf16[32,512]{1,0:T(8,128)(2,1)S(1)}, bf16[32,512]{1,0:T(8,128)(2,1)S(1)}, u32[]{:S(2)}, u32[]{:S(2)}) collective-permute-start(bf16[32,512]{1,0:T(8,128)(2,1)S(1)} %add_convert_fusion.refs_4_), channel_id=1, source_target_pairs={{0,12},{4,0},{8,4},{12,8},{1,13},{5,1},{9,5},{13,9},{2,14},{6,2},{... | collective-permute-start | bytes 98312 | tf_op jit(solution)/shard_map/ppermute | solution.py:112
  62.5 4.3 %collective-permute-start.9 = (bf16[32,512]{1,0:T(8,128)(2,1)S(1)}, bf16[32,512]{1,0:T(8,128)(2,1)S(1)}, u32[]{:S(2)}, u32[]{:S(2)}) collective-permute-start(bf16[32,512]{1,0:T(8,128)(2,1)S(1)} %add_convert_fusion.refs_4_), channel_id=1, source_target_pairs={{0,4},{4,8},{8,12},{12,0},{1,5},{5,9},{9,13},{13,1},{2,6},{6,10},{... | collective-permute-start | bytes 98312 | tf_op jit(solution)/shard_map/ppermute | solution.py:112
  66.8 3.4 %collective-permute-start.15 = (bf16[64,512]{1,0:T(8,128)(2,1)S(1)}, bf16[64,512]{1,0:T(8,128)(2,1)S(1)}, u32[]{:S(2)}, u32[]{:S(2)}) collective-permute-start(bf16[64,512]{1,0:T(8,128)(2,1)S(1)} %pad_maximum_fusion.refs_0_), channel_id=1, source_target_pairs={{0,64},{16,80},{32,96},{48,112},{64,128},{80,144},{96,160},{112,17... | collective-permute-start | bytes 196616 | tf_op jit(solution)/shard_map/ppermute | solution.py:112
  70.2 4.3 %collective-permute-start.16 = (bf16[64,512]{1,0:T(8,128)(2,1)S(1)}, bf16[64,512]{1,0:T(8,128)(2,1)S(1)}, u32[]{:S(2)}, u32[]{:S(2)}) collective-permute-start(bf16[64,512]{1,0:T(8,128)(2,1)S(1)} %pad_maximum_fusion.refs_0_), channel_id=1, source_target_pairs={{0,128},{16,144},{32,160},{48,176},{64,192},{80,208},{96,224},{112... | collective-permute-start | bytes 196616 | tf_op jit(solution)/shard_map/ppermute | solution.py:112
  74.6 1.9 %collective-permute-start.3 = (bf16[32,512]{1,0:T(8,128)(2,1)S(1)}, bf16[32,512]{1,0:T(8,128)(2,1)S(1)}, u32[]{:S(2)}, u32[]{:S(2)}) collective-permute-start(bf16[32,512]{1,0:T(8,128)(2,1)S(1)} %add_convert_fusion.1.refs_0_), channel_id=1, source_target_pairs={{0,1},{1,2},{2,3},{3,0},{4,5},{5,6},{6,7},{7,4},{8,9},{9,10},{10,1... | collective-permute-start | bytes 98312 | tf_op jit(solution)/shard_map/ppermute | solution.py:112
  76.5 4.7 %collective-permute-start.4 = (bf16[32,512]{1,0:T(8,128)(2,1)S(1)}, bf16[32,512]{1,0:T(8,128)(2,1)S(1)}, u32[]{:S(2)}, u32[]{:S(2)}) collective-permute-start(bf16[32,512]{1,0:T(8,128)(2,1)S(1)} %add_convert_fusion.1.refs_0_), channel_id=1, source_target_pairs={{0,2},{1,3},{2,0},{3,1},{4,6},{5,7},{6,4},{7,5},{8,10},{9,11},{10,... | collective-permute-start | bytes 98312 | tf_op jit(solution)/shard_map/ppermute | solution.py:112
  81.3 7.3 %collective-permute-start.5 = (bf16[32,512]{1,0:T(8,128)(2,1)S(1)}, bf16[32,512]{1,0:T(8,128)(2,1)S(1)}, u32[]{:S(2)}, u32[]{:S(2)}) collective-permute-start(bf16[32,512]{1,0:T(8,128)(2,1)S(1)} %add_convert_fusion.1.refs_0_), channel_id=1, source_target_pairs={{0,3},{1,0},{2,1},{3,2},{4,7},{5,4},{6,5},{7,6},{8,11},{9,8},{10,9... | collective-permute-start | bytes 98312 | tf_op jit(solution)/shard_map/ppermute | solution.py:112
  88.6 4.6 %collective-permute-start.17 = (bf16[64,512]{1,0:T(8,128)(2,1)S(1)}, bf16[64,512]{1,0:T(8,128)(2,1)S(1)}, u32[]{:S(2)}, u32[]{:S(2)}) collective-permute-start(bf16[64,512]{1,0:T(8,128)(2,1)S(1)} %pad_maximum_fusion.refs_0_), channel_id=1, source_target_pairs={{0,192},{16,208},{32,224},{48,240},{64,256},{80,272},{96,288},{112... | collective-permute-start | bytes 196616 | tf_op jit(solution)/shard_map/ppermute | solution.py:112
  93.2 4.2 %collective-permute-start.18 = (bf16[64,512]{1,0:T(8,128)(2,1)S(1)}, bf16[64,512]{1,0:T(8,128)(2,1)S(1)}, u32[]{:S(2)}, u32[]{:S(2)}) collective-permute-start(bf16[64,512]{1,0:T(8,128)(2,1)S(1)} %pad_maximum_fusion.refs_0_), channel_id=1, source_target_pairs={{0,256},{16,272},{32,288},{48,304},{64,320},{80,336},{96,352},{112... | collective-permute-start | bytes 196616 | tf_op jit(solution)/shard_map/ppermute | solution.py:112
  97.5 4.7 %collective-permute-start.19 = (bf16[64,512]{1,0:T(8,128)(2,1)S(1)}, bf16[64,512]{1,0:T(8,128)(2,1)S(1)}, u32[]{:S(2)}, u32[]{:S(2)}) collective-permute-start(bf16[64,512]{1,0:T(8,128)(2,1)S(1)} %pad_maximum_fusion.refs_0_), channel_id=1, source_target_pairs={{0,320},{16,336},{32,352},{48,368},{64,384},{80,400},{96,416},{112... | collective-permute-start | bytes 196616 | tf_op jit(solution)/shard_map/ppermute | solution.py:112
  102.2 5.4 %collective-permute-start.20 = (bf16[64,512]{1,0:T(8,128)(2,1)S(1)}, bf16[64,512]{1,0:T(8,128)(2,1)S(1)}, u32[]{:S(2)}, u32[]{:S(2)}) collective-permute-start(bf16[64,512]{1,0:T(8,128)(2,1)S(1)} %pad_maximum_fusion.refs_0_), channel_id=1, source_target_pairs={{0,384},{16,400},{32,416},{48,432},{64,448},{80,464},{96,480},{112... | collective-permute-start | bytes 196616 | tf_op jit(solution)/shard_map/ppermute | solution.py:112
  107.6 3.4 %collective-permute-start.21 = (bf16[64,512]{1,0:T(8,128)(2,1)S(1)}, bf16[64,512]{1,0:T(8,128)(2,1)S(1)}, u32[]{:S(2)}, u32[]{:S(2)}) collective-permute-start(bf16[64,512]{1,0:T(8,128)(2,1)S(1)} %pad_maximum_fusion.refs_0_), channel_id=1, source_target_pairs={{0,448},{16,464},{32,480},{48,496},{64,0},{80,16},{96,32},{112,48}... | collective-permute-start | bytes 196616 | tf_op jit(solution)/shard_map/ppermute | solution.py:112
  111.1 1.6 %place.1 = (bf16[128,512]{1,0:T(8,128)(2,1)}, bf16[128,512]{1,0:T(8,128)(2,1)}) custom-call(s32[2]{0:T(128)} %copy-done.5, bf16[32,512]{1,0:T(8,128)(2,1)} %copy-done.8, bf16[32,512]{1,0:T(8,128)(2,1)} %copy-done.13, bf16[32,512]{1,0:T(8,128)(2,1)} %copy-done.14, bf16[32,512]{1,0:T(8,128)(2,1)} %copy-done.15, bf16[32,512]{1,0:T(8,128)(2,1)} %copy-done.7, ...), custom_call_target="tpu_custom_call" | custom-call | bytes 524288 | tf_op jit(solution)/shard_map/place/pallas_call | solution.py:189
  112.7 1.0 collective-permute-done.21.refs_7_
  113.8 12.1 %newton.1 = (f32[1,16,512]{2,1,0:T(8,128)}, f32[1,16,512]{2,1,0:T(8,128)}) custom-call(s32[2]{0:T(128)S(1)} %pad_add_fusion.1.place_ref, bf16[64,512]{1,0:T(8,128)(2,1)S(1)} %pad_maximum_fusion.refs_0_, bf16[64,512]{1,0:T(8,128)(2,1)S(1)} %collective-permute-done.15.refs_1_, bf16[64,512]{1,0:T(8,128)(2,1)S(1)} %collective-permute-done.16.refs_2_, ...), custom_call_target="tpu_custom_call" | custom-call | flops 8053063680 | bytes 1048576 | tf_op jit(solution)/shard_map/newton/pallas_call | solution.py:199
  (56 shorter events, 0.8 us)
Async XLA Ops:
  3.5 14.0 %copy-start.4 = (bf16[128,512]{1,0:T(8,128)(2,1)S(1)}, bf16[128,512]{1,0:T(8,128)(2,1)}, u32[]{:S(2)}) copy-start(bf16[128,512]{1,0:T(8,128)(2,1)} %g_ref.3) | copy-start | bytes 393220
  3.5 31.1 %all-to-all-start = ((bf16[32,16,512]{2,1,0:T(8,128)(2,1)}), bf16[32,16,512]{2,1,0:T(8,128)(2,1)S(1)}, u32[]{:S(2)}, u32[]{:S(2)}) async-start(bf16[32,16,512]{2,1,0:T(8,128)(2,1)} %bitcast.4), calls=%async_computation | async-start | bytes 1048576 | tf_op jit(solution)/shard_map/all_to_all | solution.py:153
  18.5 18.6 %collective-permute-start.6 = (bf16[32,512]{1,0:T(8,128)(2,1)S(1)}, bf16[32,512]{1,0:T(8,128)(2,1)S(1)}, u32[]{:S(2)}, u32[]{:S(2)}) collective-permute-start(bf16[32,512]{1,0:T(8,128)(2,1)S(1)} %get-tuple-element.21), channel_id=1, source_target_pairs={{0,4},{4,8},{8,12},{12,0},{1,5},{5,9},{9,13},{13,1},{2,6},{6,10},{... | collective-permute-start | bytes 98312 | tf_op jit(solution)/shard_map/ppermute | solution.py:112
  20.9 19.6 %collective-permute-start.7 = (bf16[32,512]{1,0:T(8,128)(2,1)S(1)}, bf16[32,512]{1,0:T(8,128)(2,1)S(1)}, u32[]{:S(2)}, u32[]{:S(2)}) collective-permute-start(bf16[32,512]{1,0:T(8,128)(2,1)S(1)} %get-tuple-element.22), channel_id=1, source_target_pairs={{0,8},{4,12},{8,0},{12,4},{1,9},{5,13},{9,1},{13,5},{2,10},{6,14},... | collective-permute-start | bytes 98312 | tf_op jit(solution)/shard_map/ppermute | solution.py:112
  25.2 19.4 %collective-permute-start.8 = (bf16[32,512]{1,0:T(8,128)(2,1)S(1)}, bf16[32,512]{1,0:T(8,128)(2,1)S(1)}, u32[]{:S(2)}, u32[]{:S(2)}) collective-permute-start(bf16[32,512]{1,0:T(8,128)(2,1)S(1)} %get-tuple-element.23), channel_id=1, source_target_pairs={{0,12},{4,0},{8,4},{12,8},{1,13},{5,1},{9,5},{13,9},{2,14},{6,2},{... | collective-permute-start | bytes 98312 | tf_op jit(solution)/shard_map/ppermute | solution.py:112
  27.2 35.3 %collective-permute-start = (bf16[32,512]{1,0:T(8,128)(2,1)S(1)}, bf16[32,512]{1,0:T(8,128)(2,1)S(1)}, u32[]{:S(2)}, u32[]{:S(2)}) collective-permute-start(bf16[32,512]{1,0:T(8,128)(2,1)S(1)} %get-tuple-element.17), channel_id=1, source_target_pairs={{0,1},{1,2},{2,3},{3,0},{4,5},{5,6},{6,7},{7,4},{8,9},{9,10},{10,1... | collective-permute-start | bytes 98312 | tf_op jit(solution)/shard_map/ppermute | solution.py:112
  29.1 37.7 %collective-permute-start.1 = (bf16[32,512]{1,0:T(8,128)(2,1)S(1)}, bf16[32,512]{1,0:T(8,128)(2,1)S(1)}, u32[]{:S(2)}, u32[]{:S(2)}) collective-permute-start(bf16[32,512]{1,0:T(8,128)(2,1)S(1)} %get-tuple-element.18), channel_id=1, source_target_pairs={{0,2},{1,3},{2,0},{3,1},{4,6},{5,7},{6,4},{7,5},{8,10},{9,11},{10,... | collective-permute-start | bytes 98312 | tf_op jit(solution)/shard_map/ppermute | solution.py:112
  37.1 10.9 %collective-permute-start.12 = (bf16[16,512]{1,0:T(8,128)(2,1)}, bf16[16,512]{1,0:T(8,128)(2,1)S(1)}, u32[]{:S(2)}, u32[]{:S(2)}) collective-permute-start(bf16[16,512]{1,0:T(8,128)(2,1)} %grad_sum.1), channel_id=1, source_target_pairs={{0,16},{16,32},{32,48},{48,0},{64,80},{80,96},{96,112},{112,64},{1... | collective-permute-start | bytes 49160 | tf_op jit(solution)/shard_map/ppermute | solution.py:112
  40.5 14.0 %collective-permute-start.13 = (bf16[16,512]{1,0:T(8,128)(2,1)}, bf16[16,512]{1,0:T(8,128)(2,1)S(1)}, u32[]{:S(2)}, u32[]{:S(2)}) collective-permute-start(bf16[16,512]{1,0:T(8,128)(2,1)} %grad_sum.1), channel_id=1, source_target_pairs={{0,32},{16,48},{32,0},{48,16},{64,96},{80,112},{96,64},{112,80},{1... | collective-permute-start | bytes 49160 | tf_op jit(solution)/shard_map/ppermute | solution.py:112
  44.6 15.1 %collective-permute-start.14 = (bf16[16,512]{1,0:T(8,128)(2,1)}, bf16[16,512]{1,0:T(8,128)(2,1)S(1)}, u32[]{:S(2)}, u32[]{:S(2)}) collective-permute-start(bf16[16,512]{1,0:T(8,128)(2,1)} %grad_sum.1), channel_id=1, source_target_pairs={{0,48},{16,0},{32,16},{48,32},{64,112},{80,64},{96,80},{112,96},{1... | collective-permute-start | bytes 49160 | tf_op jit(solution)/shard_map/ppermute | solution.py:112
  48.0 14.4 %copy-start.9 = (bf16[16,512]{1,0:T(8,128)(2,1)S(1)}, bf16[16,512]{1,0:T(8,128)(2,1)}, u32[]{:S(2)}) copy-start(bf16[16,512]{1,0:T(8,128)(2,1)} %grad_sum.1) | copy-start | bytes 49156
  48.1 14.4 %copy-start.7 = (bf16[32,512]{1,0:T(8,128)(2,1)}, bf16[32,512]{1,0:T(8,128)(2,1)S(1)}, u32[]{:S(2)}) copy-start(bf16[32,512]{1,0:T(8,128)(2,1)S(1)} %add_convert_fusion.refs_4_) | copy-start | bytes 98308
  48.1 22.1 %collective-permute-start.2 = (bf16[32,512]{1,0:T(8,128)(2,1)S(1)}, bf16[32,512]{1,0:T(8,128)(2,1)S(1)}, u32[]{:S(2)}, u32[]{:S(2)}) collective-permute-start(bf16[32,512]{1,0:T(8,128)(2,1)S(1)} %get-tuple-element.19), channel_id=1, source_target_pairs={{0,3},{1,0},{2,1},{3,2},{4,7},{5,4},{6,5},{7,6},{8,11},{9,8},{10,9... | collective-permute-start | bytes 98312 | tf_op jit(solution)/shard_map/ppermute | solution.py:112
  54.5 20.0 %collective-permute-start.10 = (bf16[32,512]{1,0:T(8,128)(2,1)S(1)}, bf16[32,512]{1,0:T(8,128)(2,1)S(1)}, u32[]{:S(2)}, u32[]{:S(2)}) collective-permute-start(bf16[32,512]{1,0:T(8,128)(2,1)S(1)} %add_convert_fusion.refs_4_), channel_id=1, source_target_pairs={{0,8},{4,12},{8,0},{12,4},{1,9},{5,13},{9,1},{13,5},{2,10},{6,14},... | collective-permute-start | bytes 98312 | tf_op jit(solution)/shard_map/ppermute | solution.py:112
  59.7 16.8 %collective-permute-start.11 = (bf16[32,512]{1,0:T(8,128)(2,1)S(1)}, bf16[32,512]{1,0:T(8,128)(2,1)S(1)}, u32[]{:S(2)}, u32[]{:S(2)}) collective-permute-start(bf16[32,512]{1,0:T(8,128)(2,1)S(1)} %add_convert_fusion.refs_4_), channel_id=1, source_target_pairs={{0,12},{4,0},{8,4},{12,8},{1,13},{5,1},{9,5},{13,9},{2,14},{6,2},{... | collective-permute-start | bytes 98312 | tf_op jit(solution)/shard_map/ppermute | solution.py:112
  62.5 18.7 %collective-permute-start.9 = (bf16[32,512]{1,0:T(8,128)(2,1)S(1)}, bf16[32,512]{1,0:T(8,128)(2,1)S(1)}, u32[]{:S(2)}, u32[]{:S(2)}) collective-permute-start(bf16[32,512]{1,0:T(8,128)(2,1)S(1)} %add_convert_fusion.refs_4_), channel_id=1, source_target_pairs={{0,4},{4,8},{8,12},{12,0},{1,5},{5,9},{9,13},{13,1},{2,6},{6,10},{... | collective-permute-start | bytes 98312 | tf_op jit(solution)/shard_map/ppermute | solution.py:112
  66.8 35.3 %collective-permute-start.15 = (bf16[64,512]{1,0:T(8,128)(2,1)S(1)}, bf16[64,512]{1,0:T(8,128)(2,1)S(1)}, u32[]{:S(2)}, u32[]{:S(2)}) collective-permute-start(bf16[64,512]{1,0:T(8,128)(2,1)S(1)} %pad_maximum_fusion.refs_0_), channel_id=1, source_target_pairs={{0,64},{16,80},{32,96},{48,112},{64,128},{80,144},{96,160},{112,17... | collective-permute-start | bytes 196616 | tf_op jit(solution)/shard_map/ppermute | solution.py:112
  70.2 37.4 %collective-permute-start.16 = (bf16[64,512]{1,0:T(8,128)(2,1)S(1)}, bf16[64,512]{1,0:T(8,128)(2,1)S(1)}, u32[]{:S(2)}, u32[]{:S(2)}) collective-permute-start(bf16[64,512]{1,0:T(8,128)(2,1)S(1)} %pad_maximum_fusion.refs_0_), channel_id=1, source_target_pairs={{0,128},{16,144},{32,160},{48,176},{64,192},{80,208},{96,224},{112... | collective-permute-start | bytes 196616 | tf_op jit(solution)/shard_map/ppermute | solution.py:112
  74.5 36.5 %copy-start.8 = (bf16[32,512]{1,0:T(8,128)(2,1)}, bf16[32,512]{1,0:T(8,128)(2,1)S(1)}, u32[]{:S(2)}) copy-start(bf16[32,512]{1,0:T(8,128)(2,1)S(1)} %add_convert_fusion.1.refs_0_) | copy-start | bytes 98308
  74.6 36.5 %copy-start.10 = (bf16[32,512]{1,0:T(8,128)(2,1)}, bf16[32,512]{1,0:T(8,128)(2,1)S(1)}, u32[]{:S(2)}) copy-start(bf16[32,512]{1,0:T(8,128)(2,1)S(1)} %collective-permute-done.10.refs_6_) | copy-start | bytes 98308
  74.6 14.0 %collective-permute-start.3 = (bf16[32,512]{1,0:T(8,128)(2,1)S(1)}, bf16[32,512]{1,0:T(8,128)(2,1)S(1)}, u32[]{:S(2)}, u32[]{:S(2)}) collective-permute-start(bf16[32,512]{1,0:T(8,128)(2,1)S(1)} %add_convert_fusion.1.refs_0_), channel_id=1, source_target_pairs={{0,1},{1,2},{2,3},{3,0},{4,5},{5,6},{6,7},{7,4},{8,9},{9,10},{10,1... | collective-permute-start | bytes 98312 | tf_op jit(solution)/shard_map/ppermute | solution.py:112
  76.5 34.5 %copy-start.11 = (bf16[32,512]{1,0:T(8,128)(2,1)}, bf16[32,512]{1,0:T(8,128)(2,1)S(1)}, u32[]{:S(2)}) copy-start(bf16[32,512]{1,0:T(8,128)(2,1)S(1)} %collective-permute-done.11.refs_7_) | copy-start | bytes 98308
  76.5 16.7 %collective-permute-start.4 = (bf16[32,512]{1,0:T(8,128)(2,1)S(1)}, bf16[32,512]{1,0:T(8,128)(2,1)S(1)}, u32[]{:S(2)}, u32[]{:S(2)}) collective-permute-start(bf16[32,512]{1,0:T(8,128)(2,1)S(1)} %add_convert_fusion.1.refs_0_), channel_id=1, source_target_pairs={{0,2},{1,3},{2,0},{3,1},{4,6},{5,7},{6,4},{7,5},{8,10},{9,11},{10,... | collective-permute-start | bytes 98312 | tf_op jit(solution)/shard_map/ppermute | solution.py:112
  81.2 29.8 %copy-start.12 = (bf16[32,512]{1,0:T(8,128)(2,1)}, bf16[32,512]{1,0:T(8,128)(2,1)S(1)}, u32[]{:S(2)}) copy-start(bf16[32,512]{1,0:T(8,128)(2,1)S(1)} %collective-permute-done.9.refs_5_) | copy-start | bytes 98308
  81.3 16.2 %collective-permute-start.5 = (bf16[32,512]{1,0:T(8,128)(2,1)S(1)}, bf16[32,512]{1,0:T(8,128)(2,1)S(1)}, u32[]{:S(2)}, u32[]{:S(2)}) collective-permute-start(bf16[32,512]{1,0:T(8,128)(2,1)S(1)} %add_convert_fusion.1.refs_0_), channel_id=1, source_target_pairs={{0,3},{1,0},{2,1},{3,2},{4,7},{5,4},{6,5},{7,6},{8,11},{9,8},{10,9... | collective-permute-start | bytes 98312 | tf_op jit(solution)/shard_map/ppermute | solution.py:112
  88.6 22.5 %copy-start.13 = (bf16[32,512]{1,0:T(8,128)(2,1)}, bf16[32,512]{1,0:T(8,128)(2,1)S(1)}, u32[]{:S(2)}) copy-start(bf16[32,512]{1,0:T(8,128)(2,1)S(1)} %collective-permute-done.3.refs_1_) | copy-start | bytes 98308
  88.6 24.1 %collective-permute-start.17 = (bf16[64,512]{1,0:T(8,128)(2,1)S(1)}, bf16[64,512]{1,0:T(8,128)(2,1)S(1)}, u32[]{:S(2)}, u32[]{:S(2)}) collective-permute-start(bf16[64,512]{1,0:T(8,128)(2,1)S(1)} %pad_maximum_fusion.refs_0_), channel_id=1, source_target_pairs={{0,192},{16,208},{32,224},{48,240},{64,256},{80,272},{96,288},{112... | collective-permute-start | bytes 196616 | tf_op jit(solution)/shard_map/ppermute | solution.py:112
  93.2 17.8 %copy-start.14 = (bf16[32,512]{1,0:T(8,128)(2,1)}, bf16[32,512]{1,0:T(8,128)(2,1)S(1)}, u32[]{:S(2)}) copy-start(bf16[32,512]{1,0:T(8,128)(2,1)S(1)} %collective-permute-done.4.refs_2_) | copy-start | bytes 98308
  93.2 19.5 %collective-permute-start.18 = (bf16[64,512]{1,0:T(8,128)(2,1)S(1)}, bf16[64,512]{1,0:T(8,128)(2,1)S(1)}, u32[]{:S(2)}, u32[]{:S(2)}) collective-permute-start(bf16[64,512]{1,0:T(8,128)(2,1)S(1)} %pad_maximum_fusion.refs_0_), channel_id=1, source_target_pairs={{0,256},{16,272},{32,288},{48,304},{64,320},{80,336},{96,352},{112... | collective-permute-start | bytes 196616 | tf_op jit(solution)/shard_map/ppermute | solution.py:112
  97.5 15.2 %collective-permute-start.19 = (bf16[64,512]{1,0:T(8,128)(2,1)S(1)}, bf16[64,512]{1,0:T(8,128)(2,1)S(1)}, u32[]{:S(2)}, u32[]{:S(2)}) collective-permute-start(bf16[64,512]{1,0:T(8,128)(2,1)S(1)} %pad_maximum_fusion.refs_0_), channel_id=1, source_target_pairs={{0,320},{16,336},{32,352},{48,368},{64,384},{80,400},{96,416},{112... | collective-permute-start | bytes 196616 | tf_op jit(solution)/shard_map/ppermute | solution.py:112
  102.2 10.6 %collective-permute-start.20 = (bf16[64,512]{1,0:T(8,128)(2,1)S(1)}, bf16[64,512]{1,0:T(8,128)(2,1)S(1)}, u32[]{:S(2)}, u32[]{:S(2)}) collective-permute-start(bf16[64,512]{1,0:T(8,128)(2,1)S(1)} %pad_maximum_fusion.refs_0_), channel_id=1, source_target_pairs={{0,384},{16,400},{32,416},{48,432},{64,448},{80,464},{96,480},{112... | collective-permute-start | bytes 196616 | tf_op jit(solution)/shard_map/ppermute | solution.py:112
  107.6 6.2 %collective-permute-start.21 = (bf16[64,512]{1,0:T(8,128)(2,1)S(1)}, bf16[64,512]{1,0:T(8,128)(2,1)S(1)}, u32[]{:S(2)}, u32[]{:S(2)}) collective-permute-start(bf16[64,512]{1,0:T(8,128)(2,1)S(1)} %pad_maximum_fusion.refs_0_), channel_id=1, source_target_pairs={{0,448},{16,464},{32,480},{48,496},{64,0},{80,16},{96,32},{112,48}... | collective-permute-start | bytes 196616 | tf_op jit(solution)/shard_map/ppermute | solution.py:112
  (7 other events, 45.1 us)

commit v2 on v1

v2 whole, which is shorter than its diff:
```python
import functools

import jax
import jax.numpy as jnp
from jax import lax
from jax.experimental import pallas as pl
from jax.experimental.pallas import tpu as pltpu
from jax.sharding import PartitionSpec as P

ITERS = 6
VMEM = pl.BlockSpec(memory_space=pltpu.VMEM)
ANY = pl.BlockSpec(memory_space=pl.ANY)
SMEM = pl.BlockSpec(memory_space=pltpu.SMEM)
F32 = jnp.float32
BF16 = jnp.bfloat16


def mm(left, right, dims=((1,), (0,))):
    return lax.dot_general(left, right, (dims, ((), ())), preferred_element_type=F32)


def fetch(sources, targets, sems):
    copies = [pltpu.make_async_copy(src, dst, sems.at[k]) for k, (src, dst) in enumerate(zip(sources, targets))]
    for copy in copies:
        copy.start()
    for copy in copies:
        copy.wait()


def grad_kernel(tokens_all, x_any, g_any, grad_ref, x_ref, g_ref, sems):
    fetch((x_any, g_any), (x_ref, g_ref), sems)
    grad = mm(x_ref[...], g_ref[...], ((0,), (0,)))
    grad_ref[...] = (grad * (1.0 / tokens_all)).astype(BF16)


def pair_sum(left_ref, right_ref):
    return (left_ref[...].astype(F32) + right_ref[...].astype(F32)).astype(BF16)


def sum_kernel(copies, parts_ref, layer_ref, layer_other, input_ref, input_other, out_ref, layer_sum, input_sum):
    slab = parts_ref.shape[0] // copies
    total = parts_ref[:slab, :].astype(F32)
    for k in range(1, copies):
        total = total + parts_ref[k * slab : (k + 1) * slab, :].astype(F32)
    total = total.astype(BF16)
    for k in range(copies):
        out_ref[k * slab : (k + 1) * slab, :] = total
    layer_sum[...] = pair_sum(layer_ref, layer_other)
    input_sum[...] = pair_sum(input_ref, input_other)


def outputs_kernel(x_any, g_any, w_any, after_any, layer_ref, input_ref, x_ref, g_ref, w_ref, sems):
    fetch((x_any, g_any, w_any), (x_ref, g_ref, w_ref), sems)
    layer_ref[...] = mm(x_ref[...], w_ref[...]).astype(BF16)
    input_ref[...] = mm(g_ref[...], w_ref[...], ((1,), (1,))).astype(BF16)


def newton_kernel(
    slab,
    place_ref,
    block_ref,
    layer_ref,
    layer_other,
    input_ref,
    input_other,
    layer_out,
    input_out,
    left_ref,
    right_ref,
    wide,
    low,
):
    layer_out[...] = pair_sum(layer_ref, layer_other)
    input_out[...] = pair_sum(input_ref, input_other)
    extent = block_ref.shape[0]
    first_row = pl.multiple_of(place_ref[0] * slab, slab)
    row_ids = lax.broadcasted_iota(jnp.int32, (extent, extent), 0)
    column_ids = lax.broadcasted_iota(jnp.int32, (extent, extent), 1)
    own_rows = first_row + lax.broadcasted_iota(jnp.int32, (slab, extent), 0)
    own_columns = lax.broadcasted_iota(jnp.int32, (slab, extent), 1)
    b = block_ref[...]
    rows = []
    for which in range(2):
        stat = mm(b, b, ((1,), (1,))) if which == 0 else mm(b, b, ((0,), (0,)))
        stat = jnp.where(row_ids == column_ids, stat + 1e-06, stat)
        square = jnp.sum(jnp.sum(stat * stat, axis=0, keepdims=True), axis=1, keepdims=True)
        scaling = 0.4 * jnp.sqrt(square + 1e-06)
        quarter = stat * (0.25 / scaling)
        wide[which] = quarter
        low[which] = quarter.astype(BF16)
        start = 1.0 / jnp.sqrt(jnp.sqrt(scaling))
        eye = jnp.where(own_rows == own_columns, 1.25, 0.0)
        rows.append(start * (eye - wide[which, pl.ds(first_row, slab), :]))

    def step(_, rows):
        new = []
        for which in range(2):
            n_low = low[which]
            n_wide = wide[which]
            c = mm(n_low, n_low) - 2.5 * n_wide
            c_low = c.astype(BF16)
            h = (3.125 * c + mm(c_low, c_low)).astype(BF16)
            n_new = 2.44140625 * n_wide + mm(h, n_low)
            wide[which] = n_new
            new_low = n_new.astype(BF16)
            low[which] = new_low
            new.append(1.25 * rows[which] - mm(rows[which].astype(BF16), new_low))
        return tuple(new)

    rows = lax.fori_loop(0, ITERS - 2, step, tuple(rows))
    ends = list(rows)
    for _ in range(4):
        for which in range(2):
            ends[which] = 1.25 * ends[which] - mm(ends[which].astype(BF16), low[which])
    for which, out in ((0, left_ref), (1, right_ref)):
        out[0] = 1.25 * rows[which] - mm(ends[which].astype(BF16), low[which])


def exchange(values, axis):
    return lax.all_to_all(values, axis, 0, 0, tiled=True)


def partner(values, axis, flip):
    return lax.ppermute(values, axis, [(i, i ^ flip) for i in range(4)])


def shards(x_in, grad_out, weight):
    extent = weight.shape[0]
    tokens = x_in.shape[0]
    groups = lax.axis_size("dp")
    slab = extent // groups
    place = lax.axis_index("dp").astype(jnp.int32).reshape(1)
    block = jax.ShapeDtypeStruct((extent, extent), BF16)
    whole = jax.ShapeDtypeStruct((tokens, extent), BF16)
    tokens_vmem = pltpu.VMEM((tokens, extent), BF16)

    grad_part = pl.pallas_call(
        functools.partial(grad_kernel, tokens * groups),
        out_shape=block,
        in_specs=[ANY, ANY],
        out_specs=VMEM,
        scratch_shapes=[tokens_vmem, tokens_vmem, pltpu.SemaphoreType.DMA((2,))],
        compiler_params=pltpu.CompilerParams(vmem_limit_bytes=32 * 2**20),
        cost_estimate=pl.CostEstimate(flops=2 * tokens * extent * extent, bytes_accessed=2**20, transcendentals=0),
        name="grad_part",
    )(x_in, grad_out)
    received = exchange(grad_part, "dp")
    layer_part, input_part = pl.pallas_call(
        outputs_kernel,
        out_shape=[whole, whole],
        in_specs=[ANY, ANY, ANY, ANY],
        out_specs=[VMEM, VMEM],
        scratch_shapes=[
            tokens_vmem,
            tokens_vmem,
            pltpu.VMEM((extent, extent), BF16),
            pltpu.SemaphoreType.DMA((3,)),
        ],
        compiler_params=pltpu.CompilerParams(vmem_limit_bytes=32 * 2**20),
        cost_estimate=pl.CostEstimate(flops=4 * tokens * extent * extent, bytes_accessed=2**20, transcendentals=0),
        name="outputs_part",
    )(x_in, grad_out, weight, grad_part)
    copies, layer_sum, input_sum = pl.pallas_call(
        functools.partial(sum_kernel, groups),
        out_shape=[block, whole, whole],
        in_specs=[VMEM] * 5,
        out_specs=[VMEM] * 3,
        cost_estimate=pl.CostEstimate(flops=extent * extent, bytes_accessed=2**20, transcendentals=0),
        name="sums",
    )(received, layer_part, partner(layer_part, "precond", 1), input_part, partner(input_part, "tensor", 1))
    grad_low = exchange(copies, "dp")

    root = jax.ShapeDtypeStruct((1, slab, extent), F32)
    return pl.pallas_call(
        functools.partial(newton_kernel, slab),
        out_shape=[whole, whole, root, root],
        in_specs=[SMEM] + [VMEM] * 5,
        out_specs=[VMEM] * 4,
        scratch_shapes=[
            pltpu.VMEM((2, extent, extent), F32),
            pltpu.VMEM((2, extent, extent), BF16),
        ],
        compiler_params=pltpu.CompilerParams(vmem_limit_bytes=48 * 2**20),
        cost_estimate=pl.CostEstimate(flops=60 * extent**3, bytes_accessed=2**20, transcendentals=0),
        name="newton",
    )(place, grad_low, layer_sum, partner(layer_sum, "precond", 2), input_sum, partner(input_sum, "tensor", 2))


def solution(mesh):
    in_specs = (P("dp", "precond"), P("dp", "tensor"), P("precond", "tensor"))
    out_specs = (
        P("dp", "tensor"),
        P("dp", "precond"),
        P("precond", "dp", "tensor"),
        P("precond", "dp", "tensor"),
    )
    return jax.shard_map(shards, mesh=mesh, in_specs=in_specs, out_specs=out_specs, check_vma=False)
```

time: 127 us -> 77.7 us (0.61)
  starting transfers between devices: 103 us -> 31.9 us
  waiting for transfers between devices: 1.6 us -> 25.8 us
  Pallas kernels: 17.5 us -> 16.1 us
    ppermute x22 -> x4, starting transfers between devices: 88.9 us -> 13 us  [partner(): return lax.ppermute(values, axis, [(i, i ^ flip) for i in range(4)])]
    ppermute x22 -> x4, waiting for transfers between devices: 1.09 us -> 13.9 us  [partner(): return lax.ppermute(values, axis, [(i, i ^ flip) for i in range(4)])]
    all_to_all x1 -> x2, waiting for transfers between devices: 0.51 us -> 11.9 us  [exchange(): return lax.all_to_all(values, axis, 0, 0, tiled=True)]
    all_to_all x1 -> x2, starting transfers between devices: 13.9 us -> 18.9 us  [exchange(): return lax.all_to_all(values, axis, 0, 0, tiled=True)]
    pallas_call x4 -> x3, Pallas kernels: 16.4 us -> 14.6 us  [the longest x1 11.6 us: shards(): pl.pallas_call(functools.partial(newton_kernel, slab), out_shape=[whole,...]
    unnamed x32 -> x24, local copies, waits for them, and re-layouts: 2.64 us -> 2.62 us
  transfers between devices with their start and end apart: 23 -> 6, of which waited for: 2 -> 4; matrix products, arithmetic and copies ran while one was open for 0% -> 0% of each run, Pallas kernels for 3% -> 1%
where the time goes in v2:
time: 77.7 us; the launch traced here: 77.3 us
  starting transfers between devices  31.9 us (41%)
  waiting for transfers between devices  25.8 us (33%)
  Pallas kernels  16.1 us (21%)
  local copies, waits for them, and re-layouts  2.62 us (3%)
  between operations  0.82 us (1%)
    all_to_all x2, starting transfers between devices, exchange(): return lax.all_to_all(values, axis, 0, 0, tiled=True)  18.9 us
    ppermute x4, waiting for transfers between devices, partner(): return lax.ppermute(values, axis, [(i, i ^ flip) for i in range(4)])  13.9 us
    ppermute x4, starting transfers between devices, partner(): return lax.ppermute(values, axis, [(i, i ^ flip) for i in range(4)])  13 us
    all_to_all x2, waiting for transfers between devices, exchange(): return lax.all_to_all(values, axis, 0, 0, tiled=True)  11.9 us
    pallas_call x1, Pallas kernels, shards(): pl.pallas_call(functools.partial(newton_kernel, slab), out_shape=[whole,...  11.6 us
    unnamed x24, local copies, waits for them, and re-layouts  2.62 us
    pallas_call x1, Pallas kernels, shards(): pl.pallas_call(functools.partial(sum_kernel, groups), out_shape=[block, w...  2.23 us
  transfers between devices with their start and end apart: 6, of which 4 were waited for; matrix products, arithmetic and copies ran while one was open for 0% of the time, Pallas kernels for 1%

profile of v2, /device:TPU:6, one launch (start us, length us, event | category | flops | bytes accessed | tf_op | source)
XLA Modules:
  0.0 77.3 jit_solution(6528184125646478672)
XLA Ops:
  0.6 0.0 copy-start.1
  0.6 0.9 %copy-done.1 = bf16[128,512]{1,0:T(8,128)(2,1)S(1)} copy-done((bf16[128,512]{1,0:T(8,128)(2,1)S(1)}, bf16[128,512]{1,0:T(8,128)(2,1)}, u32[]{:S(2)}) %copy-start.1) | copy-done | bytes 131096
  1.5 0.9 %copy-done.3 = bf16[128,512]{1,0:T(8,128)(2,1)S(1)} copy-done((bf16[128,512]{1,0:T(8,128)(2,1)S(1)}, bf16[128,512]{1,0:T(8,128)(2,1)}, u32[]{:S(2)}) %copy-start.3) | copy-done | bytes 131096
  2.4 1.4 %grad_part.1.after_any = bf16[512,512]{1,0:T(8,128)(2,1)} custom-call(bf16[128,512]{1,0:T(8,128)(2,1)S(1)} %copy-done.1, bf16[128,512]{1,0:T(8,128)(2,1)S(1)} %copy-done.3), custom_call_target="tpu_custom_call" | custom-call | flops 67108864 | bytes 1048576 | tf_op jit(solution)/shard_map/grad_part/pallas_call | solution.py:137
  3.9 0.0 copy-start
  3.9 0.0 copy-start.2
  3.9 0.0 copy-start.4
  3.9 13.9 %all-to-all-start = ((bf16[32,16,512]{2,1,0:T(8,128)(2,1)}), bf16[32,16,512]{2,1,0:T(8,128)(2,1)S(1)}, u32[]{:S(2)}, u32[]{:S(2)}) async-start(bf16[32,16,512]{2,1,0:T(8,128)(2,1)} %bitcast.1), calls=%async_computation | async-start | bytes 1048576 | tf_op jit(solution)/shard_map/all_to_all | solution.py:120
  17.8 0.0 copy-done
  17.8 0.0 copy-done.2
  17.9 0.0 copy-done.4
  17.9 0.8 %outputs_part.1 = (bf16[128,512]{1,0:T(8,128)(2,1)S(1)}, bf16[128,512]{1,0:T(8,128)(2,1)S(1)}) custom-call(bf16[128,512]{1,0:T(8,128)(2,1)S(1)} %copy-done.2, bf16[128,512]{1,0:T(8,128)(2,1)S(1)} %copy-done.4, bf16[512,512]{1,0:T(8,128)(2,1)S(1)} %copy-done, bf16[512,512]{1,0:T(8,128)(2,1)} %grad_part.1.after_any), custom_call_target="tpu_custom_call" | custom-call | flops 134217728 | bytes 1048576 | tf_op jit(solution)/shard_map/outputs_part/pallas_call | solution.py:148
  18.7 0.0 copy-start.5
  18.7 0.0 copy-start.6
  18.7 1.9 %collective-permute-start = (bf16[128,512]{1,0:T(8,128)(2,1)S(1)}, bf16[128,512]{1,0:T(8,128)(2,1)S(1)}, u32[]{:S(2)}, u32[]{:S(2)}) collective-permute-start(bf16[128,512]{1,0:T(8,128)(2,1)S(1)} %get-tuple-element.9.layer_ref), channel_id=1, source_target_pairs={{0,1},{1,0},{2,3},{3,2},{4,5},{5,4},{6,7},{7,6},{8,9},{9,8},{10,11... | collective-permute-start | bytes 393224 | tf_op jit(solution)/shard_map/ppermute | solution.py:124
  20.6 2.7 %collective-permute-start.1 = (bf16[128,512]{1,0:T(8,128)(2,1)S(1)}, bf16[128,512]{1,0:T(8,128)(2,1)S(1)}, u32[]{:S(2)}, u32[]{:S(2)}) collective-permute-start(bf16[128,512]{1,0:T(8,128)(2,1)S(1)} %get-tuple-element.10.input_ref), channel_id=1, source_target_pairs={{0,4},{4,0},{8,12},{12,8},{1,5},{5,1},{9,13},{13,9},{2,6},{6,2},{1... | collective-permute-start | bytes 393224 | tf_op jit(solution)/shard_map/ppermute | solution.py:124
  23.4 0.0 collective-permute-done.layer_other
  23.4 0.0 copy-start.10
  23.4 5.0 %collective-permute-done.1.input_other = bf16[128,512]{1,0:T(8,128)(2,1)S(1)} collective-permute-done((bf16[128,512]{1,0:T(8,128)(2,1)S(1)}, bf16[128,512]{1,0:T(8,128)(2,1)S(1)}, u32[]{:S(2)}, u32[]{:S(2)}) %collective-permute-start.1) | collective-permute-done | bytes 131104 | tf_op jit(solution)/shard_map/ppermute | solution.py:124
  28.4 6.6 %all-to-all-done = bf16[32,16,512]{2,1,0:T(8,128)(2,1)S(1)} async-done(((bf16[32,16,512]{2,1,0:T(8,128)(2,1)}), bf16[32,16,512]{2,1,0:T(8,128)(2,1)S(1)}, u32[]{:S(2)}, u32[]{:S(2)}) %all-to-all-start) | async-done | bytes 524320 | tf_op jit(solution)/shard_map/all_to_all | solution.py:120
  35.0 0.0 copy-done.5
  35.0 0.0 copy-done.6
  35.1 0.8 copy-done.9
  35.8 2.2 %sums.1 = (bf16[512,512]{1,0:T(8,128)(2,1)}, bf16[128,512]{1,0:T(8,128)(2,1)}, bf16[128,512]{1,0:T(8,128)(2,1)}) custom-call(bf16[512,512]{1,0:T(8,128)(2,1)} %bitcast.6, bf16[128,512]{1,0:T(8,128)(2,1)} %copy-done.5, bf16[128,512]{1,0:T(8,128)(2,1)} %copy-done.10, bf16[128,512]{1,0:T(8,128)(2,1)} %copy-done.6, bf16[128,512]{1,0:T(8,128)(2,1)} %copy-done.11), custom_call_target="tpu_custom_call" | custom-call | flops 262144 | bytes 1048576 | tf_op jit(solution)/shard_map/sums/pallas_call | solution.py:163
  38.1 5.0 %all-to-all-start.1 = ((bf16[32,16,512]{2,1,0:T(8,128)(2,1)}), bf16[32,16,512]{2,1,0:T(8,128)(2,1)S(1)}, u32[]{:S(2)}, u32[]{:S(2)}) async-start(bf16[32,16,512]{2,1,0:T(8,128)(2,1)} %bitcast.7), calls=%async_computation.1 | async-start | bytes 1048576 | tf_op jit(solution)/shard_map/all_to_all | solution.py:120
  43.1 0.0 copy-done.7
  43.1 5.0 %collective-permute-start.2 = (bf16[128,512]{1,0:T(8,128)(2,1)S(1)}, bf16[128,512]{1,0:T(8,128)(2,1)S(1)}, u32[]{:S(2)}, u32[]{:S(2)}) collective-permute-start(bf16[128,512]{1,0:T(8,128)(2,1)S(1)} %copy-done.7), channel_id=1, source_target_pairs={{0,2},{1,3},{2,0},{3,1},{4,6},{5,7},{6,4},{7,5},{8,10},{9,11},{10,... | collective-permute-start | bytes 393224 | tf_op jit(solution)/shard_map/ppermute | solution.py:124
  48.2 3.3 %collective-permute-start.3 = (bf16[128,512]{1,0:T(8,128)(2,1)S(1)}, bf16[128,512]{1,0:T(8,128)(2,1)S(1)}, u32[]{:S(2)}, u32[]{:S(2)}) collective-permute-start(bf16[128,512]{1,0:T(8,128)(2,1)S(1)} %copy-done.8), channel_id=1, source_target_pairs={{0,8},{4,12},{8,0},{12,4},{1,9},{5,13},{9,1},{13,5},{2,10},{6,14},... | collective-permute-start | bytes 393224 | tf_op jit(solution)/shard_map/ppermute | solution.py:124
  51.5 8.9 %collective-permute-done.2.layer_other = bf16[128,512]{1,0:T(8,128)(2,1)S(1)} collective-permute-done((bf16[128,512]{1,0:T(8,128)(2,1)S(1)}, bf16[128,512]{1,0:T(8,128)(2,1)S(1)}, u32[]{:S(2)}, u32[]{:S(2)}) %collective-permute-start.2) | collective-permute-done | bytes 131104 | tf_op jit(solution)/shard_map/ppermute | solution.py:124
  60.4 0.0 collective-permute-done.3.input_other
  60.4 5.3 %all-to-all-done.1 = bf16[32,16,512]{2,1,0:T(8,128)(2,1)S(1)} async-done(((bf16[32,16,512]{2,1,0:T(8,128)(2,1)}), bf16[32,16,512]{2,1,0:T(8,128)(2,1)S(1)}, u32[]{:S(2)}, u32[]{:S(2)}) %all-to-all-start.1) | async-done | bytes 524320 | tf_op jit(solution)/shard_map/all_to_all | solution.py:120
  65.7 11.6 %newton.1 = (bf16[128,512]{1,0:T(8,128)(2,1)}, bf16[128,512]{1,0:T(8,128)(2,1)}, f32[1,16,512]{2,1,0:T(8,128)}, f32[1,16,512]{2,1,0:T(8,128)}) custom-call(s32[1]{0:T(128)} %bitcast.place_ref, bf16[512,512]{1,0:T(8,128)(2,1)S(1)} %bitcast.5, bf16[128,512]{1,0:T(8,128)(2,1)S(1)} %copy-done.7, bf16[128,512]{1,0:T(8,128)(2,1)S(1)} %collective-permute-done.2.layer_other, ...), custom_call_target="tpu_custom_call" | custom-call | flops 8053063680 | bytes 1048576 | tf_op jit(solution)/shard_map/newton/pallas_call | solution.py:174
  (8 shorter events, 0.0 us)
Async XLA Ops:
  0.6 0.9 %copy-start.1 = (bf16[128,512]{1,0:T(8,128)(2,1)S(1)}, bf16[128,512]{1,0:T(8,128)(2,1)}, u32[]{:S(2)}) copy-start(bf16[128,512]{1,0:T(8,128)(2,1)} %x_any.3) | copy-start | bytes 393220
  1.5 0.9 %copy-start.3 = (bf16[128,512]{1,0:T(8,128)(2,1)S(1)}, bf16[128,512]{1,0:T(8,128)(2,1)}, u32[]{:S(2)}) copy-start(bf16[128,512]{1,0:T(8,128)(2,1)} %g_any.3) | copy-start | bytes 393220
  3.9 13.9 %copy-start = (bf16[512,512]{1,0:T(8,128)(2,1)S(1)}, bf16[512,512]{1,0:T(8,128)(2,1)}, u32[]{:S(2)}) copy-start(bf16[512,512]{1,0:T(8,128)(2,1)} %w_any.1) | copy-start | bytes 1572868
  3.9 13.9 %copy-start.2 = (bf16[128,512]{1,0:T(8,128)(2,1)S(1)}, bf16[128,512]{1,0:T(8,128)(2,1)}, u32[]{:S(2)}) copy-start(bf16[128,512]{1,0:T(8,128)(2,1)} %x_any.3) | copy-start | bytes 393220
  3.9 13.9 %copy-start.4 = (bf16[128,512]{1,0:T(8,128)(2,1)S(1)}, bf16[128,512]{1,0:T(8,128)(2,1)}, u32[]{:S(2)}) copy-start(bf16[128,512]{1,0:T(8,128)(2,1)} %g_any.3) | copy-start | bytes 393220
  3.9 31.1 %all-to-all-start = ((bf16[32,16,512]{2,1,0:T(8,128)(2,1)}), bf16[32,16,512]{2,1,0:T(8,128)(2,1)S(1)}, u32[]{:S(2)}, u32[]{:S(2)}) async-start(bf16[32,16,512]{2,1,0:T(8,128)(2,1)} %bitcast.1), calls=%async_computation | async-start | bytes 1048576 | tf_op jit(solution)/shard_map/all_to_all | solution.py:120
  18.7 16.4 %copy-start.5 = (bf16[128,512]{1,0:T(8,128)(2,1)}, bf16[128,512]{1,0:T(8,128)(2,1)S(1)}, u32[]{:S(2)}) copy-start(bf16[128,512]{1,0:T(8,128)(2,1)S(1)} %get-tuple-element.9.layer_ref) | copy-start | bytes 393220
  18.7 16.4 %copy-start.6 = (bf16[128,512]{1,0:T(8,128)(2,1)}, bf16[128,512]{1,0:T(8,128)(2,1)S(1)}, u32[]{:S(2)}) copy-start(bf16[128,512]{1,0:T(8,128)(2,1)S(1)} %get-tuple-element.10.input_ref) | copy-start | bytes 393220
  18.7 4.7 %collective-permute-start = (bf16[128,512]{1,0:T(8,128)(2,1)S(1)}, bf16[128,512]{1,0:T(8,128)(2,1)S(1)}, u32[]{:S(2)}, u32[]{:S(2)}) collective-permute-start(bf16[128,512]{1,0:T(8,128)(2,1)S(1)} %get-tuple-element.9.layer_ref), channel_id=1, source_target_pairs={{0,1},{1,0},{2,3},{3,2},{4,5},{5,4},{6,7},{7,6},{8,9},{9,8},{10,11... | collective-permute-start | bytes 393224 | tf_op jit(solution)/shard_map/ppermute | solution.py:124
  20.6 7.8 %collective-permute-start.1 = (bf16[128,512]{1,0:T(8,128)(2,1)S(1)}, bf16[128,512]{1,0:T(8,128)(2,1)S(1)}, u32[]{:S(2)}, u32[]{:S(2)}) collective-permute-start(bf16[128,512]{1,0:T(8,128)(2,1)S(1)} %get-tuple-element.10.input_ref), channel_id=1, source_target_pairs={{0,4},{4,0},{8,12},{12,8},{1,5},{5,1},{9,13},{13,9},{2,6},{6,2},{1... | collective-permute-start | bytes 393224 | tf_op jit(solution)/shard_map/ppermute | solution.py:124
  23.4 11.7 %copy-start.10 = (bf16[128,512]{1,0:T(8,128)(2,1)}, bf16[128,512]{1,0:T(8,128)(2,1)S(1)}, u32[]{:S(2)}) copy-start(bf16[128,512]{1,0:T(8,128)(2,1)S(1)} %collective-permute-done.layer_other) | copy-start | bytes 393220
  28.4 6.6 %copy-start.11 = (bf16[128,512]{1,0:T(8,128)(2,1)}, bf16[128,512]{1,0:T(8,128)(2,1)S(1)}, u32[]{:S(2)}) copy-start(bf16[128,512]{1,0:T(8,128)(2,1)S(1)} %collective-permute-done.1.input_other) | copy-start | bytes 393220
  35.0 0.8 %copy-start.9 = (bf16[32,16,512]{2,1,0:T(8,128)(2,1)}, bf16[32,16,512]{2,1,0:T(8,128)(2,1)S(1)}, u32[]{:S(2)}) copy-start(bf16[32,16,512]{2,1,0:T(8,128)(2,1)S(1)} %all-to-all-done) | copy-start | bytes 1572868
  38.1 5.0 %copy-start.7 = (bf16[128,512]{1,0:T(8,128)(2,1)S(1)}, bf16[128,512]{1,0:T(8,128)(2,1)}, u32[]{:S(2)}) copy-start(bf16[128,512]{1,0:T(8,128)(2,1)} %get-tuple-element.12.layer_ref) | copy-start | bytes 393220
  38.1 10.1 %copy-start.8 = (bf16[128,512]{1,0:T(8,128)(2,1)S(1)}, bf16[128,512]{1,0:T(8,128)(2,1)}, u32[]{:S(2)}) copy-start(bf16[128,512]{1,0:T(8,128)(2,1)} %get-tuple-element.13.input_ref) | copy-start | bytes 393220
  38.1 27.6 %all-to-all-start.1 = ((bf16[32,16,512]{2,1,0:T(8,128)(2,1)}), bf16[32,16,512]{2,1,0:T(8,128)(2,1)S(1)}, u32[]{:S(2)}, u32[]{:S(2)}) async-start(bf16[32,16,512]{2,1,0:T(8,128)(2,1)} %bitcast.7), calls=%async_computation.1 | async-start | bytes 1048576 | tf_op jit(solution)/shard_map/all_to_all | solution.py:120
  43.1 17.3 %collective-permute-start.2 = (bf16[128,512]{1,0:T(8,128)(2,1)S(1)}, bf16[128,512]{1,0:T(8,128)(2,1)S(1)}, u32[]{:S(2)}, u32[]{:S(2)}) collective-permute-start(bf16[128,512]{1,0:T(8,128)(2,1)S(1)} %copy-done.7), channel_id=1, source_target_pairs={{0,2},{1,3},{2,0},{3,1},{4,6},{5,7},{6,4},{7,5},{8,10},{9,11},{10,... | collective-permute-start | bytes 393224 | tf_op jit(solution)/shard_map/ppermute | solution.py:124
  48.2 12.2 %collective-permute-start.3 = (bf16[128,512]{1,0:T(8,128)(2,1)S(1)}, bf16[128,512]{1,0:T(8,128)(2,1)S(1)}, u32[]{:S(2)}, u32[]{:S(2)}) collective-permute-start(bf16[128,512]{1,0:T(8,128)(2,1)S(1)} %copy-done.8), channel_id=1, source_target_pairs={{0,8},{4,12},{8,0},{12,4},{1,9},{5,13},{9,1},{13,5},{2,10},{6,14},... | collective-permute-start | bytes 393224 | tf_op jit(solution)/shard_map/ppermute | solution.py:124

commit v3 on v2

v3 whole, which is shorter than its diff:
```python
import functools

import jax
import jax.numpy as jnp
from jax import lax
from jax.experimental import pallas as pl
from jax.experimental.pallas import tpu as pltpu
from jax.sharding import PartitionSpec as P

ITERS = 6
VMEM = pl.BlockSpec(memory_space=pltpu.VMEM)
HBM = pl.BlockSpec(memory_space=pltpu.HBM)
ANY = pl.BlockSpec(memory_space=pl.ANY)
SMEM = pl.BlockSpec(memory_space=pltpu.SMEM)
F32 = jnp.float32
BF16 = jnp.bfloat16


def mm(left, right, dims=((1,), (0,))):
    return lax.dot_general(left, right, (dims, ((), ())), preferred_element_type=F32)


def fetch(sources, targets, sems):
    copies = [pltpu.make_async_copy(src, dst, sems.at[k]) for k, (src, dst) in enumerate(zip(sources, targets))]
    for copy in copies:
        copy.start()
    for copy in copies:
        copy.wait()


def grad_kernel(tokens_all, x_any, g_any, grad_ref, x_ref, g_ref, sems):
    fetch((x_any, g_any), (x_ref, g_ref), sems)
    grad = mm(x_ref[...], g_ref[...], ((0,), (0,)))
    grad_ref[...] = (grad * (1.0 / tokens_all)).astype(BF16)


def pair_sum(left_ref, right_ref):
    return (left_ref[...].astype(F32) + right_ref[...].astype(F32)).astype(BF16)


def sum_kernel(copies, parts_ref, layer_ref, layer_other, input_ref, input_other, out_ref, layer_sum, input_sum):
    slab = parts_ref.shape[0] // copies
    total = parts_ref[:slab, :].astype(F32)
    for k in range(1, copies):
        total = total + parts_ref[k * slab : (k + 1) * slab, :].astype(F32)
    total = total.astype(BF16)
    for k in range(copies):
        out_ref[k * slab : (k + 1) * slab, :] = total
    layer_sum[...] = pair_sum(layer_ref, layer_other)
    input_sum[...] = pair_sum(input_ref, input_other)


def outputs_kernel(x_any, g_any, w_any, after_any, layer_ref, input_ref, x_ref, g_ref, w_ref, sems):
    fetch((x_any, g_any, w_any), (x_ref, g_ref, w_ref), sems)
    layer_ref[...] = mm(x_ref[...], w_ref[...]).astype(BF16)
    input_ref[...] = mm(g_ref[...], w_ref[...], ((1,), (1,))).astype(BF16)


def middle_kernel(input_ref, input_other, layer_ref, input_out, layer_copy):
    input_out[...] = pair_sum(input_ref, input_other)
    layer_copy[...] = layer_ref[...]


def last_kernel(layer_ref, layer_other, after_any, layer_out):
    layer_out[...] = pair_sum(layer_ref, layer_other)


def staged(units):
    waiting = None
    for product, use in units:
        result = product()
        if waiting is not None:
            waiting[0](waiting[1])
        waiting = (use, result)
    waiting[0](waiting[1])


def newton_kernel(slab, place_ref, block_ref, left_ref, right_ref, wide, n_low, c_low, h_low, row):
    extent = block_ref.shape[0]
    half = extent // 2
    cuts = (slice(0, half), slice(half, extent))
    sides = ((0, cuts[0]), (0, cuts[1]), (1, cuts[0]), (1, cuts[1]))
    first_row = pl.multiple_of(place_ref[0] * slab, slab)
    outs = (left_ref, right_ref)
    turned = h_low.at[1]
    turned[...] = block_ref[...].T
    on_diagonal = lax.broadcasted_iota(jnp.int32, (half, half), 0) == lax.broadcasted_iota(jnp.int32, (half, half), 1)
    own = first_row + lax.broadcasted_iota(jnp.int32, (slab, extent), 0)
    eye = jnp.where(own == lax.broadcasted_iota(jnp.int32, (slab, extent), 1), 1.25, 0.0)
    squares = [0.0, 0.0]
    quarters = [None, None]

    def gram(side, cut):
        if side == 0:
            return mm(block_ref[...], turned[:, cut])
        return mm(turned[...], block_ref[:, cut])

    def keep_gram(side, cut, product):
        for rows in cuts:
            stat = product[rows]
            if rows == cut:
                stat = jnp.where(on_diagonal, stat + 1e-06, stat)
            wide[side, rows, cut] = stat
            squares[side] = squares[side] + jnp.sum(stat * stat, axis=0, keepdims=True)
        if cut.stop == extent:
            scaling = 0.4 * jnp.sqrt(jnp.sum(squares[side], axis=1, keepdims=True) + 1e-06)
            quarter = 0.25 / scaling
            quarters[side] = quarter
            n_low[side, 0, :extent, :] = (wide[side] * quarter).astype(BF16)
            start = 1.0 / jnp.sqrt(jnp.sqrt(scaling))
            first = start * (eye - quarter * wide[side, pl.ds(first_row, slab), :])
            row[side] = first
            n_low[side, 1, extent:, :] = first.astype(BF16)

    def unit(do, use, side, cut):
        return (lambda: do(side, cut)), (lambda product: use(side, cut, product))

    units = [unit(gram, keep_gram, *at) for at in sides]

    def square_n(now, riders, side, cut):
        return mm(n_low[side, now, : extent + riders, :], n_low[side, now, :extent, cut])

    def keep_c(now, riders, side, cut, product):
        scale = 2.5 * quarters[side] if now == 0 and riders == 0 else 2.5
        c_low[side, :, cut] = (product[:extent] - scale * wide[side, :, cut]).astype(BF16)
        if riders:
            new = 1.25 * row[side, :, cut] - product[extent:]
            row[side, :, cut] = new
            n_low[side, 1 - now, extent:, cut] = new.astype(BF16)

    def square_c(side, cut):
        return mm(c_low[side], c_low[side, :, cut])

    def keep_h(side, cut, product):
        h_low[side, :, cut] = (3.125 * c_low[side, :, cut].astype(F32) + product).astype(BF16)

    def next_n(now, side, cut):
        return mm(h_low[side], n_low[side, now, :extent, cut])

    def keep_n(now, first, side, cut, product):
        scale = 2.44140625 * quarters[side] if first else 2.44140625
        n = scale * wide[side, :, cut] + product
        wide[side, :, cut] = n
        n_low[side, 1 - now, :extent, cut] = n.astype(BF16)

    for k in range(ITERS - 2):
        now, riders = k % 2, (slab if k else 0)
        part = functools.partial
        units += [unit(part(square_n, now, riders), part(keep_c, now, riders), *at) for at in sides]
        units += [unit(square_c, keep_h, *at) for at in sides]
        units += [unit(part(next_n, now), part(keep_n, now, k == 0), *at) for at in sides]
    staged(units)

    now = (ITERS - 2) % 2
    firsts = [1.25 * row[side] - mm(n_low[side, now, extent:, :], n_low[side, now, :extent, :]) for side in range(2)]
    ends = list(firsts)
    for _ in range(4):
        for side in range(2):
            ends[side] = 1.25 * ends[side] - mm(ends[side].astype(BF16), n_low[side, now, :extent, :])
    for side in range(2):
        outs[side][0] = 1.25 * firsts[side] - mm(ends[side].astype(BF16), n_low[side, now, :extent, :])


def limit(mebibytes):
    return pltpu.CompilerParams(vmem_limit_bytes=mebibytes * 2**20)


def exchange(values, axis):
    return lax.all_to_all(values, axis, 0, 0, tiled=True)


def partner(values, axis, flip):
    return lax.ppermute(values, axis, [(i, i ^ flip) for i in range(4)])


def shards(x_in, grad_out, weight):
    extent = weight.shape[0]
    tokens = x_in.shape[0]
    groups = lax.axis_size("dp")
    slab = extent // groups
    place = lax.axis_index("dp").astype(jnp.int32).reshape(1)
    block = jax.ShapeDtypeStruct((extent, extent), BF16)
    whole = jax.ShapeDtypeStruct((tokens, extent), BF16)
    tokens_vmem = pltpu.VMEM((tokens, extent), BF16)

    grad_part = pl.pallas_call(
        functools.partial(grad_kernel, tokens * groups),
        out_shape=block,
        in_specs=[HBM, HBM],
        out_specs=VMEM,
        scratch_shapes=[tokens_vmem, tokens_vmem, pltpu.SemaphoreType.DMA((2,))],
        compiler_params=limit(63),
        cost_estimate=pl.CostEstimate(flops=2 * tokens * extent * extent, bytes_accessed=2**20, transcendentals=0),
        name="grad_part",
    )(x_in, grad_out)
    received = exchange(grad_part, "dp")
    layer_part, input_part = pl.pallas_call(
        outputs_kernel,
        out_shape=[whole, whole],
        in_specs=[HBM, HBM, HBM, ANY],
        out_specs=[VMEM, VMEM],
        scratch_shapes=[
            tokens_vmem,
            tokens_vmem,
            pltpu.VMEM((extent, extent), BF16),
            pltpu.SemaphoreType.DMA((3,)),
        ],
        compiler_params=limit(8),
        cost_estimate=pl.CostEstimate(flops=4 * tokens * extent * extent, bytes_accessed=2**20, transcendentals=0),
        name="outputs_part",
    )(x_in, grad_out, weight, grad_part)
    copies, layer_sum, input_sum = pl.pallas_call(
        functools.partial(sum_kernel, groups),
        out_shape=[block, whole, whole],
        in_specs=[VMEM] * 5,
        out_specs=[VMEM] * 3,
        compiler_params=limit(8),
        cost_estimate=pl.CostEstimate(flops=extent * extent, bytes_accessed=2**20, transcendentals=0),
        name="sums",
    )(received, layer_part, partner(layer_part, "precond", 1), input_part, partner(input_part, "tensor", 1))
    grad_low = exchange(copies, "dp")

    grad_in, layer_copy = pl.pallas_call(
        middle_kernel,
        out_shape=[whole, whole],
        in_specs=[VMEM] * 3,
        out_specs=[VMEM] * 2,
        compiler_params=limit(8),
        cost_estimate=pl.CostEstimate(flops=0, bytes_accessed=2**19, transcendentals=0),
        name="middle",
    )(input_sum, partner(input_sum, "tensor", 2), layer_sum)
    layer_other = partner(layer_copy, "precond", 2)

    root = jax.ShapeDtypeStruct((1, slab, extent), F32)
    left_root, right_root = pl.pallas_call(
        functools.partial(newton_kernel, slab),
        out_shape=[root, root],
        in_specs=[SMEM, VMEM],
        out_specs=[VMEM] * 2,
        scratch_shapes=[
            pltpu.VMEM((2, extent, extent), F32),
            pltpu.VMEM((2, 2, extent + slab, extent), BF16),
            pltpu.VMEM((2, extent, extent), BF16),
            pltpu.VMEM((2, extent, extent), BF16),
            pltpu.VMEM((2, slab, extent), F32),
        ],
        compiler_params=limit(24),
        cost_estimate=pl.CostEstimate(flops=0, bytes_accessed=2**16, transcendentals=0),
        name="newton",
    )(place, grad_low)
    layer_out = pl.pallas_call(
        last_kernel,
        out_shape=whole,
        in_specs=[VMEM, VMEM, ANY],
        out_specs=VMEM,
        compiler_params=limit(8),
        cost_estimate=pl.CostEstimate(flops=0, bytes_accessed=2**18, transcendentals=0),
        name="last",
    )(layer_copy, layer_other, left_root)
    return layer_out, grad_in, left_root, right_root


def solution(mesh):
    in_specs = (P("dp", "precond"), P("dp", "tensor"), P("precond", "tensor"))
    out_specs = (
        P("dp", "tensor"),
        P("dp", "precond"),
        P("precond", "dp", "tensor"),
        P("precond", "dp", "tensor"),
    )
    return jax.shard_map(shards, mesh=mesh, in_specs=in_specs, out_specs=out_specs, check_vma=False)
```

time: 77.7 us -> 67.8 us (0.87)
  waiting for transfers between devices: 25.8 us -> 19.6 us
  local copies, waits for them, and re-layouts: 2.62 us -> 0.78 us
  Pallas kernels: 16.1 us -> 14.4 us
    ppermute x4, waiting for transfers between devices: 13.9 us -> 10.1 us  [partner(): return lax.ppermute(values, axis, [(i, i ^ flip) for i in range(4)])]
    all_to_all x2, waiting for transfers between devices: 11.9 us -> 9.47 us  [exchange(): return lax.all_to_all(values, axis, 0, 0, tiled=True)]
    unnamed x24 -> x10, local copies, waits for them, and re-layouts: 2.62 us -> 0.78 us
    pallas_call x1, Pallas kernels: 2.23 us -> 0.93 us  [shards(): pl.pallas_call(functools.partial(sum_kernel, groups), out_shape=[block, w...]
    pallas_call x2 -> x4, Pallas kernels: 12.4 us -> 11.4 us  [the longest x1 9.2 us: shards(): pl.pallas_call(functools.partial(newton_kernel, slab), out_shape=[root, r...]
  transfers between devices with their start and end apart: 6 -> 6, of which waited for: 4 -> 4; matrix products, arithmetic and copies ran while one was open for 0% -> 0% of each run, Pallas kernels for 1% -> 16%
where the time goes in v3:
time: 67.8 us; the launch traced here: 67.3 us
  starting transfers between devices  31.8 us (47%)
  waiting for transfers between devices  19.6 us (29%)
  Pallas kernels  14.4 us (21%)
  local copies, waits for them, and re-layouts  0.78 us (1%)
  between operations  0.77 us (1%)
    all_to_all x2, starting transfers between devices, exchange(): return lax.all_to_all(values, axis, 0, 0, tiled=True)  18.8 us
    ppermute x4, starting transfers between devices, partner(): return lax.ppermute(values, axis, [(i, i ^ flip) for i in range(4)])  13 us
    ppermute x4, waiting for transfers between devices, partner(): return lax.ppermute(values, axis, [(i, i ^ flip) for i in range(4)])  10.1 us
    all_to_all x2, waiting for transfers between devices, exchange(): return lax.all_to_all(values, axis, 0, 0, tiled=True)  9.47 us
    pallas_call x1, Pallas kernels, shards(): pl.pallas_call(functools.partial(newton_kernel, slab), out_shape=[root, r...  9.2 us
    pallas_call x1, Pallas kernels, shards(): pl.pallas_call(functools.partial(grad_kernel, tokens * groups), out_shape...  2.14 us
  transfers between devices with their start and end apart: 6, of which 4 were waited for; matrix products, arithmetic and copies ran while one was open for 0% of the time, Pallas kernels for 16%

profile of v3, /device:TPU:6, one launch (start us, length us, event | category | flops | bytes accessed | tf_op | source)
XLA Modules:
  0.0 67.3 jit_solution(10775538698616849103)
XLA Ops:
  0.6 0.0 copy-start.2
  0.6 0.0 copy-start.3
  0.7 2.1 %grad_part.1.after_any = bf16[512,512]{1,0:T(8,128)(2,1)} custom-call(bf16[128,512]{1,0:T(8,128)(2,1)} %x_any.3, bf16[128,512]{1,0:T(8,128)(2,1)} %g_any.3), custom_call_target="tpu_custom_call" | custom-call | flops 67108864 | bytes 1048576 | tf_op jit(solution)/shard_map/grad_part/pallas_call | solution.py:186
  2.8 0.0 copy-start
  2.8 0.0 copy-start.1
  2.8 13.9 %all-to-all-start = ((bf16[32,16,512]{2,1,0:T(8,128)(2,1)}), bf16[32,16,512]{2,1,0:T(8,128)(2,1)S(1)}, u32[]{:S(2)}, u32[]{:S(2)}) async-start(bf16[32,16,512]{2,1,0:T(8,128)(2,1)} %bitcast.5), calls=%async_computation | async-start | bytes 1048576 | tf_op jit(solution)/shard_map/all_to_all | solution.py:169
  16.7 0.0 copy-done.2
  16.7 0.0 copy-done.3
  16.7 0.0 copy-done
  16.7 0.0 copy-done.1
  16.8 0.8 %outputs_part.1 = (bf16[128,512]{1,0:T(8,128)(2,1)S(1)}, bf16[128,512]{1,0:T(8,128)(2,1)S(1)}) custom-call(bf16[128,512]{1,0:T(8,128)(2,1)S(1)} %copy-done.2, bf16[128,512]{1,0:T(8,128)(2,1)S(1)} %copy-done.3, bf16[512,512]{1,0:T(8,128)(2,1)S(1)} %copy-done.1, bf16[512,512]{1,0:T(8,128)(2,1)S(1)} %copy-done), custom_call_target="tpu_custom_call" | custom-call | flops 134217728 | bytes 1048576 | tf_op jit(solution)/shard_map/outputs_part/pallas_call | solution.py:197
  17.6 1.9 %collective-permute-start = (bf16[128,512]{1,0:T(8,128)(2,1)S(1)}, bf16[128,512]{1,0:T(8,128)(2,1)S(1)}, u32[]{:S(2)}, u32[]{:S(2)}) collective-permute-start(bf16[128,512]{1,0:T(8,128)(2,1)S(1)} %get-tuple-element.13.layer_ref), channel_id=1, source_target_pairs={{0,1},{1,0},{2,3},{3,2},{4,5},{5,4},{6,7},{7,6},{8,9},{9,8},{10,11... | collective-permute-start | bytes 393224 | tf_op jit(solution)/shard_map/ppermute | solution.py:173
  19.5 2.7 %collective-permute-start.1 = (bf16[128,512]{1,0:T(8,128)(2,1)S(1)}, bf16[128,512]{1,0:T(8,128)(2,1)S(1)}, u32[]{:S(2)}, u32[]{:S(2)}) collective-permute-start(bf16[128,512]{1,0:T(8,128)(2,1)S(1)} %get-tuple-element.14.input_ref), channel_id=1, source_target_pairs={{0,4},{4,0},{8,12},{12,8},{1,5},{5,1},{9,13},{13,9},{2,6},{6,2},{1... | collective-permute-start | bytes 393224 | tf_op jit(solution)/shard_map/ppermute | solution.py:173
  22.2 0.0 collective-permute-done.layer_other
  22.2 5.0 %collective-permute-done.1.input_other = bf16[128,512]{1,0:T(8,128)(2,1)S(1)} collective-permute-done((bf16[128,512]{1,0:T(8,128)(2,1)S(1)}, bf16[128,512]{1,0:T(8,128)(2,1)S(1)}, u32[]{:S(2)}, u32[]{:S(2)}) %collective-permute-start.1) | collective-permute-done | bytes 131104 | tf_op jit(solution)/shard_map/ppermute | solution.py:173
  27.3 6.6 %all-to-all-done = bf16[32,16,512]{2,1,0:T(8,128)(2,1)S(1)} async-done(((bf16[32,16,512]{2,1,0:T(8,128)(2,1)}), bf16[32,16,512]{2,1,0:T(8,128)(2,1)S(1)}, u32[]{:S(2)}, u32[]{:S(2)}) %all-to-all-start) | async-done | bytes 524320 | tf_op jit(solution)/shard_map/all_to_all | solution.py:169
  33.9 0.9 %sums.1 = (bf16[512,512]{1,0:T(8,128)(2,1)}, bf16[128,512]{1,0:T(8,128)(2,1)S(1)}, bf16[128,512]{1,0:T(8,128)(2,1)S(1)}) custom-call(bf16[512,512]{1,0:T(8,128)(2,1)S(1)} %bitcast.7, bf16[128,512]{1,0:T(8,128)(2,1)S(1)} %get-tuple-element.13.layer_ref, bf16[128,512]{1,0:T(8,128)(2,1)S(1)} %collective-permute-done.layer_other, ...), custom_call_target="tpu_custom_call" | custom-call | flops 262144 | bytes 1048576 | tf_op jit(solution)/shard_map/sums/pallas_call | solution.py:212
  34.8 4.9 %all-to-all-start.1 = ((bf16[32,16,512]{2,1,0:T(8,128)(2,1)}), bf16[32,16,512]{2,1,0:T(8,128)(2,1)S(1)}, u32[]{:S(2)}, u32[]{:S(2)}) async-start(bf16[32,16,512]{2,1,0:T(8,128)(2,1)} %bitcast.3), calls=%async_computation.1 | async-start | bytes 1048576 | tf_op jit(solution)/shard_map/all_to_all | solution.py:169
  39.8 3.3 %collective-permute-start.2 = (bf16[128,512]{1,0:T(8,128)(2,1)S(1)}, bf16[128,512]{1,0:T(8,128)(2,1)S(1)}, u32[]{:S(2)}, u32[]{:S(2)}) collective-permute-start(bf16[128,512]{1,0:T(8,128)(2,1)S(1)} %get-tuple-element.15.input_ref), channel_id=1, source_target_pairs={{0,8},{4,12},{8,0},{12,4},{1,9},{5,13},{9,1},{13,5},{2,10},{6,14},... | collective-permute-start | bytes 393224 | tf_op jit(solution)/shard_map/ppermute | solution.py:173
  43.1 5.0 %collective-permute-done.2.input_other = bf16[128,512]{1,0:T(8,128)(2,1)S(1)} collective-permute-done((bf16[128,512]{1,0:T(8,128)(2,1)S(1)}, bf16[128,512]{1,0:T(8,128)(2,1)S(1)}, u32[]{:S(2)}, u32[]{:S(2)}) %collective-permute-start.2) | collective-permute-done | bytes 131104 | tf_op jit(solution)/shard_map/ppermute | solution.py:173
  48.1 0.7 %middle.1 = (bf16[128,512]{1,0:T(8,128)(2,1)}, bf16[128,512]{1,0:T(8,128)(2,1)S(1)}) custom-call(bf16[128,512]{1,0:T(8,128)(2,1)S(1)} %get-tuple-element.15.input_ref, bf16[128,512]{1,0:T(8,128)(2,1)S(1)} %collective-permute-done.2.input_other, bf16[128,512]{1,0:T(8,128)(2,1)S(1)} %get-tuple-element.16.layer_ref), custom_call_target="tpu_custom_call" | custom-call | bytes 524288 | tf_op jit(solution)/shard_map/middle/pallas_call | solution.py:223
  48.8 5.0 %collective-permute-start.3 = (bf16[128,512]{1,0:T(8,128)(2,1)S(1)}, bf16[128,512]{1,0:T(8,128)(2,1)S(1)}, u32[]{:S(2)}, u32[]{:S(2)}) collective-permute-start(bf16[128,512]{1,0:T(8,128)(2,1)S(1)} %get-tuple-element.17.layer_ref), channel_id=1, source_target_pairs={{0,2},{1,3},{2,0},{3,1},{4,6},{5,7},{6,4},{7,5},{8,10},{9,11},{10,... | collective-permute-start | bytes 393224 | tf_op jit(solution)/shard_map/ppermute | solution.py:173
  53.8 2.8 %all-to-all-done.1 = bf16[32,16,512]{2,1,0:T(8,128)(2,1)S(1)} async-done(((bf16[32,16,512]{2,1,0:T(8,128)(2,1)}), bf16[32,16,512]{2,1,0:T(8,128)(2,1)S(1)}, u32[]{:S(2)}, u32[]{:S(2)}) %all-to-all-start.1) | async-done | bytes 524320 | tf_op jit(solution)/shard_map/all_to_all | solution.py:169
  56.7 9.2 %newton.1 = (f32[1,16,512]{2,1,0:T(8,128)}, f32[1,16,512]{2,1,0:T(8,128)}) custom-call(s32[1]{0:T(128)} %bitcast.2.place_ref, bf16[512,512]{1,0:T(8,128)(2,1)S(1)} %bitcast.6), custom_call_target="tpu_custom_call" | custom-call | bytes 65536 | tf_op jit(solution)/shard_map/newton/pallas_call | solution.py:235
  65.9 0.0 collective-permute-done.3.layer_other
  65.9 0.0 copy-start.4
  65.9 0.8 %copy-done.4 = f32[1,16,512]{2,1,0:T(8,128)S(1)} copy-done((f32[1,16,512]{2,1,0:T(8,128)S(1)}, f32[1,16,512]{2,1,0:T(8,128)}, u32[]{:S(2)}) %copy-start.4) | copy-done | bytes 32792
  66.7 0.7 %last.1 = bf16[128,512]{1,0:T(8,128)(2,1)} custom-call(bf16[128,512]{1,0:T(8,128)(2,1)S(1)} %get-tuple-element.17.layer_ref, bf16[128,512]{1,0:T(8,128)(2,1)S(1)} %collective-permute-done.3.layer_other, f32[1,16,512]{2,1,0:T(8,128)S(1)} %copy-done.4), custom_call_target="tpu_custom_call" | custom-call | bytes 262144 | tf_op jit(solution)/shard_map/last/pallas_call | solution.py:251
Async XLA Ops:
  0.6 16.1 %copy-start.2 = (bf16[128,512]{1,0:T(8,128)(2,1)S(1)}, bf16[128,512]{1,0:T(8,128)(2,1)}, u32[]{:S(2)}) copy-start(bf16[128,512]{1,0:T(8,128)(2,1)} %x_any.3) | copy-start | bytes 393220
  0.6 16.1 %copy-start.3 = (bf16[128,512]{1,0:T(8,128)(2,1)S(1)}, bf16[128,512]{1,0:T(8,128)(2,1)}, u32[]{:S(2)}) copy-start(bf16[128,512]{1,0:T(8,128)(2,1)} %g_any.3) | copy-start | bytes 393220
  2.8 13.9 %copy-start = (bf16[512,512]{1,0:T(8,128)(2,1)S(1)}, bf16[512,512]{1,0:T(8,128)(2,1)}, u32[]{:S(2)}) copy-start(bf16[512,512]{1,0:T(8,128)(2,1)} %grad_part.1.after_any) | copy-start | bytes 1572868
  2.8 13.9 %copy-start.1 = (bf16[512,512]{1,0:T(8,128)(2,1)S(1)}, bf16[512,512]{1,0:T(8,128)(2,1)}, u32[]{:S(2)}) copy-start(bf16[512,512]{1,0:T(8,128)(2,1)} %w_any.1) | copy-start | bytes 1572868
  2.8 31.1 %all-to-all-start = ((bf16[32,16,512]{2,1,0:T(8,128)(2,1)}), bf16[32,16,512]{2,1,0:T(8,128)(2,1)S(1)}, u32[]{:S(2)}, u32[]{:S(2)}) async-start(bf16[32,16,512]{2,1,0:T(8,128)(2,1)} %bitcast.5), calls=%async_computation | async-start | bytes 1048576 | tf_op jit(solution)/shard_map/all_to_all | solution.py:169
  17.6 4.7 %collective-permute-start = (bf16[128,512]{1,0:T(8,128)(2,1)S(1)}, bf16[128,512]{1,0:T(8,128)(2,1)S(1)}, u32[]{:S(2)}, u32[]{:S(2)}) collective-permute-start(bf16[128,512]{1,0:T(8,128)(2,1)S(1)} %get-tuple-element.13.layer_ref), channel_id=1, source_target_pairs={{0,1},{1,0},{2,3},{3,2},{4,5},{5,4},{6,7},{7,6},{8,9},{9,8},{10,11... | collective-permute-start | bytes 393224 | tf_op jit(solution)/shard_map/ppermute | solution.py:173
  19.5 7.8 %collective-permute-start.1 = (bf16[128,512]{1,0:T(8,128)(2,1)S(1)}, bf16[128,512]{1,0:T(8,128)(2,1)S(1)}, u32[]{:S(2)}, u32[]{:S(2)}) collective-permute-start(bf16[128,512]{1,0:T(8,128)(2,1)S(1)} %get-tuple-element.14.input_ref), channel_id=1, source_target_pairs={{0,4},{4,0},{8,12},{12,8},{1,5},{5,1},{9,13},{13,9},{2,6},{6,2},{1... | collective-permute-start | bytes 393224 | tf_op jit(solution)/shard_map/ppermute | solution.py:173
  34.8 21.8 %all-to-all-start.1 = ((bf16[32,16,512]{2,1,0:T(8,128)(2,1)}), bf16[32,16,512]{2,1,0:T(8,128)(2,1)S(1)}, u32[]{:S(2)}, u32[]{:S(2)}) async-start(bf16[32,16,512]{2,1,0:T(8,128)(2,1)} %bitcast.3), calls=%async_computation.1 | async-start | bytes 1048576 | tf_op jit(solution)/shard_map/all_to_all | solution.py:169
  39.8 8.4 %collective-permute-start.2 = (bf16[128,512]{1,0:T(8,128)(2,1)S(1)}, bf16[128,512]{1,0:T(8,128)(2,1)S(1)}, u32[]{:S(2)}, u32[]{:S(2)}) collective-permute-start(bf16[128,512]{1,0:T(8,128)(2,1)S(1)} %get-tuple-element.15.input_ref), channel_id=1, source_target_pairs={{0,8},{4,12},{8,0},{12,4},{1,9},{5,13},{9,1},{13,5},{2,10},{6,14},... | collective-permute-start | bytes 393224 | tf_op jit(solution)/shard_map/ppermute | solution.py:173
  48.8 17.1 %collective-permute-start.3 = (bf16[128,512]{1,0:T(8,128)(2,1)S(1)}, bf16[128,512]{1,0:T(8,128)(2,1)S(1)}, u32[]{:S(2)}, u32[]{:S(2)}) collective-permute-start(bf16[128,512]{1,0:T(8,128)(2,1)S(1)} %get-tuple-element.17.layer_ref), channel_id=1, source_target_pairs={{0,2},{1,3},{2,0},{3,1},{4,6},{5,7},{6,4},{7,5},{8,10},{9,11},{10,... | collective-permute-start | bytes 393224 | tf_op jit(solution)/shard_map/ppermute | solution.py:173
  65.9 0.8 %copy-start.4 = (f32[1,16,512]{2,1,0:T(8,128)S(1)}, f32[1,16,512]{2,1,0:T(8,128)}, u32[]{:S(2)}) copy-start(f32[1,16,512]{2,1,0:T(8,128)} %get-tuple-element.11.after_any) | copy-start | bytes 98308

commit v4 on v3

v4 whole, which is shorter than its diff:
```python
import functools

import jax
import jax.numpy as jnp
from jax import lax
from jax.experimental import pallas as pl
from jax.experimental.pallas import tpu as pltpu
from jax.sharding import PartitionSpec as P

ITERS = 6
CHUNKS = 2
VMEM = pl.BlockSpec(memory_space=pltpu.VMEM)
HBM = pl.BlockSpec(memory_space=pltpu.HBM)
ANY = pl.BlockSpec(memory_space=pl.ANY)
SMEM = pl.BlockSpec(memory_space=pltpu.SMEM)
F32 = jnp.float32
BF16 = jnp.bfloat16


def mm(left, right, dims=((1,), (0,))):
    return lax.dot_general(left, right, (dims, ((), ())), preferred_element_type=F32)


def fetch(sources, targets, sems):
    copies = [pltpu.make_async_copy(src, dst, sems.at[k]) for k, (src, dst) in enumerate(zip(sources, targets))]
    for copy in copies:
        copy.start()
    for copy in copies:
        copy.wait()


def grad_kernel(tokens_all, x_any, g_any, grad_any, x_ref, g_ref, grad_ref, sems, out_sems):
    fetch((x_any, g_any), (x_ref, g_ref), sems)
    copies = []
    chunk = grad_ref.shape[0] // CHUNKS
    for k in range(CHUNKS):
        rows = slice(k * chunk, (k + 1) * chunk)
        grad = mm(x_ref[:, rows], g_ref[...], ((0,), (0,)))
        grad_ref[rows, :] = (grad * (1.0 / tokens_all)).astype(BF16)
        copies.append(pltpu.make_async_copy(grad_ref.at[rows, :], grad_any.at[rows, :], out_sems.at[k]))
        copies[k].start()
    for copy in copies:
        copy.wait()


def pair_sum(left_ref, right_ref):
    return (left_ref[...].astype(F32) + right_ref[...].astype(F32)).astype(BF16)


def sum_kernel(copies, parts_ref, input_ref, input_other, layer_any, out_ref, input_sum):
    slab = parts_ref.shape[0] // copies
    total = parts_ref[:slab, :].astype(F32)
    for k in range(1, copies):
        total = total + parts_ref[k * slab : (k + 1) * slab, :].astype(F32)
    total = total.astype(BF16)
    for k in range(copies):
        out_ref[k * slab : (k + 1) * slab, :] = total
    input_sum[...] = pair_sum(input_ref, input_other)


def outputs_kernel(x_any, g_any, w_any, after_any, layer_ref, input_ref, x_ref, g_ref, w_ref, sems):
    fetch((x_any, g_any, w_any), (x_ref, g_ref, w_ref), sems)
    layer_ref[...] = mm(x_ref[...], w_ref[...]).astype(BF16)
    input_ref[...] = mm(g_ref[...], w_ref[...], ((1,), (1,))).astype(BF16)


def middle_kernel(input_ref, input_other, layer_ref, layer_other, input_out, layer_sum):
    layer_sum[...] = pair_sum(layer_ref, layer_other)
    input_out[...] = pair_sum(input_ref, input_other)


def last_kernel(layer_ref, layer_other, done_ref, layer_out):
    layer_out[...] = pair_sum(layer_ref, layer_other)


def staged(units):
    waiting = None
    for product, use in units:
        result = product()
        if waiting is not None:
            waiting[0](waiting[1])
        waiting = (use, result)
    waiting[0](waiting[1])


def newton_kernel(slab, place_ref, block_ref, left_ref, right_ref, done_ref, wide, n_low, c_low, h_low, row):
    extent = block_ref.shape[0]
    half = extent // 2
    top, low = slice(0, half), slice(half, extent)
    sides = ((0, top), (0, low), (1, top), (1, low))
    first_row = pl.multiple_of(place_ref[0] * slab, slab)
    outs = (left_ref, right_ref)
    turned = h_low.at[1]
    turned[...] = block_ref[...].T
    on_diagonal = lax.broadcasted_iota(jnp.int32, (half, half), 0) == lax.broadcasted_iota(jnp.int32, (half, half), 1)
    own = first_row + lax.broadcasted_iota(jnp.int32, (slab, extent), 0)
    eye = jnp.where(own == lax.broadcasted_iota(jnp.int32, (slab, extent), 1), 1.25, 0.0)
    squares = [None, None]
    quarters = [None, None]

    def keep(ref, cut, values):
        values = values.astype(BF16)
        ref[cut.start : extent, cut] = values
        if cut == top:
            ref[top, low] = values[half:].T

    def gram(side, cut):
        left, right = (block_ref, turned) if side == 0 else (turned, block_ref)
        return mm(left[cut.start :, :], right[:, cut])

    def keep_gram(side, cut, product):
        corner = jnp.where(on_diagonal, product[:half] + 1e-06, product[:half])
        wide[side, cut, cut] = corner
        square = jnp.sum(corner * corner, axis=0, keepdims=True)
        if cut == top:
            below = product[half:]
            wide[side, low, top] = below
            wide[side, top, low] = below.T
            squares[side] = square + 2.0 * jnp.sum(below * below, axis=0, keepdims=True)
            return
        total = jnp.sum(squares[side] + square, axis=1, keepdims=True)
        scaling = 0.4 * jnp.sqrt(total + 1e-06)
        quarter = 0.25 / scaling
        quarters[side] = quarter
        n_low[side, 0, :extent, :] = (wide[side] * quarter).astype(BF16)
        start = 1.0 / jnp.sqrt(jnp.sqrt(scaling))
        first = start * (eye - quarter * wide[side, pl.ds(first_row, slab), :])
        row[side] = first
        n_low[side, 1, extent:, :] = first.astype(BF16)

    def unit(do, use, side, cut):
        return (lambda: do(side, cut)), (lambda product: use(side, cut, product))

    units = [unit(gram, keep_gram, *at) for at in sides]

    def square_n(now, riders, side, cut):
        return mm(n_low[side, now, cut.start : extent + riders, :], n_low[side, now, :extent, cut])

    def keep_c(now, riders, side, cut, product):
        scale = 2.5 * quarters[side] if now == 0 and riders == 0 else 2.5
        size = extent - cut.start
        keep(c_low.at[side], cut, product[:size] - scale * wide[side, cut.start :, cut])
        if riders:
            new = 1.25 * row[side, :, cut] - product[size:]
            row[side, :, cut] = new
            n_low[side, 1 - now, extent:, cut] = new.astype(BF16)

    def square_c(side, cut):
        return mm(c_low[side, cut.start :, :], c_low[side, :, cut])

    def keep_h(side, cut, product):
        keep(h_low.at[side], cut, 3.125 * c_low[side, cut.start :, cut].astype(F32) + product)

    def next_n(now, side, cut):
        return mm(h_low[side, cut.start :, :], n_low[side, now, :extent, cut])

    def keep_n(now, first, side, cut, product):
        scale = 2.44140625 * quarters[side] if first else 2.44140625
        n = scale * wide[side, cut.start :, cut] + product
        wide[side, cut.start :, cut] = n
        keep(n_low.at[side, 1 - now], cut, n)

    for k in range(ITERS - 2):
        now, riders = k % 2, (slab if k else 0)
        part = functools.partial
        units += [unit(part(square_n, now, riders), part(keep_c, now, riders), *at) for at in sides]
        units += [unit(square_c, keep_h, *at) for at in sides]
        units += [unit(part(next_n, now), part(keep_n, now, k == 0), *at) for at in sides]
    staged(units)

    now = (ITERS - 2) % 2
    firsts = [1.25 * row[side] - mm(n_low[side, now, extent:, :], n_low[side, now, :extent, :]) for side in range(2)]
    ends = list(firsts)
    for _ in range(4):
        for side in range(2):
            ends[side] = 1.25 * ends[side] - mm(ends[side].astype(BF16), n_low[side, now, :extent, :])
    for side in range(2):
        outs[side][0] = 1.25 * firsts[side] - mm(ends[side].astype(BF16), n_low[side, now, :extent, :])
    done_ref[...] = jnp.zeros_like(done_ref)


def limit(mebibytes):
    return pltpu.CompilerParams(vmem_limit_bytes=mebibytes * 2**20)


def exchange(values, axis):
    return lax.all_to_all(values, axis, 0, 0, tiled=True)


def partner(values, axis, flip):
    return lax.ppermute(values, axis, [(i, i ^ flip) for i in range(4)])


def shards(x_in, grad_out, weight):
    extent = weight.shape[0]
    tokens = x_in.shape[0]
    groups = lax.axis_size("dp")
    slab = extent // groups
    place = lax.axis_index("dp").astype(jnp.int32).reshape(1)
    block = jax.ShapeDtypeStruct((extent, extent), BF16)
    whole = jax.ShapeDtypeStruct((tokens, extent), BF16)
    tokens_vmem = pltpu.VMEM((tokens, extent), BF16)

    grad_part = pl.pallas_call(
        functools.partial(grad_kernel, tokens * groups),
        out_shape=block,
        in_specs=[HBM, HBM],
        out_specs=HBM,
        scratch_shapes=[
            tokens_vmem,
            tokens_vmem,
            pltpu.VMEM((extent, extent), BF16),
            pltpu.SemaphoreType.DMA((2,)),
            pltpu.SemaphoreType.DMA((CHUNKS,)),
        ],
        compiler_params=limit(63),
        cost_estimate=pl.CostEstimate(flops=2 * tokens * extent * extent, bytes_accessed=2**20, transcendentals=0),
        name="grad_part",
    )(x_in, grad_out)
    received = exchange(grad_part, "dp")
    layer_part, input_part = pl.pallas_call(
        outputs_kernel,
        out_shape=[whole, whole],
        in_specs=[HBM, HBM, HBM, ANY],
        out_specs=[VMEM, VMEM],
        scratch_shapes=[
            tokens_vmem,
            tokens_vmem,
            pltpu.VMEM((extent, extent), BF16),
            pltpu.SemaphoreType.DMA((3,)),
        ],
        compiler_params=limit(8),
        cost_estimate=pl.CostEstimate(flops=4 * tokens * extent * extent, bytes_accessed=2**20, transcendentals=0),
        name="outputs_part",
    )(x_in, grad_out, weight, grad_part)
    layer_near = partner(layer_part, "precond", 1)
    copies, input_sum = pl.pallas_call(
        functools.partial(sum_kernel, groups),
        out_shape=[block, whole],
        in_specs=[VMEM, VMEM, VMEM, ANY],
        out_specs=[VMEM] * 2,
        compiler_params=limit(8),
        cost_estimate=pl.CostEstimate(flops=extent * extent, bytes_accessed=2**20, transcendentals=0),
        name="sums",
    )(received, input_part, partner(input_part, "tensor", 1), layer_near)
    grad_low = exchange(copies, "dp")

    grad_in, layer_sum = pl.pallas_call(
        middle_kernel,
        out_shape=[whole, whole],
        in_specs=[VMEM] * 4,
        out_specs=[VMEM] * 2,
        compiler_params=limit(8),
        cost_estimate=pl.CostEstimate(flops=0, bytes_accessed=2**19, transcendentals=0),
        name="middle",
    )(input_sum, partner(input_sum, "tensor", 2), layer_part, layer_near)
    layer_other = partner(layer_sum, "precond", 2)

    root = jax.ShapeDtypeStruct((1, slab, extent), F32)
    left_root, right_root, done = pl.pallas_call(
        functools.partial(newton_kernel, slab),
        out_shape=[root, root, jax.ShapeDtypeStruct((8, 128), F32)],
        in_specs=[SMEM, VMEM],
        out_specs=[VMEM] * 3,
        scratch_shapes=[
            pltpu.VMEM((2, extent, extent), F32),
            pltpu.VMEM((2, 2, extent + slab, extent), BF16),
            pltpu.VMEM((2, extent, extent), BF16),
            pltpu.VMEM((2, extent, extent), BF16),
            pltpu.VMEM((2, slab, extent), F32),
        ],
        compiler_params=limit(24),
        cost_estimate=pl.CostEstimate(flops=0, bytes_accessed=2**16, transcendentals=0),
        name="newton",
    )(place, grad_low)
    layer_out = pl.pallas_call(
        last_kernel,
        out_shape=whole,
        in_specs=[VMEM, VMEM, VMEM],
        out_specs=VMEM,
        compiler_params=limit(8),
        cost_estimate=pl.CostEstimate(flops=0, bytes_accessed=2**18, transcendentals=0),
        name="last",
    )(layer_sum, layer_other, done)
    return layer_out, grad_in, left_root, right_root


def solution(mesh):
    in_specs = (P("dp", "precond"), P("dp", "tensor"), P("precond", "tensor"))
    out_specs = (
        P("dp", "tensor"),
        P("dp", "precond"),
        P("precond", "dp", "tensor"),
        P("precond", "dp", "tensor"),
    )
    return jax.shard_map(shards, mesh=mesh, in_specs=in_specs, out_specs=out_specs, check_vma=False)
```

time: 67.8 us -> 65.3 us (0.963)
  Pallas kernels: 14.4 us -> 12.7 us
  local copies, waits for them, and re-layouts: 0.78 us -> 0.02 us
    pallas_call x1, Pallas kernels: 9.2 us -> 7.5 us  [shards(): pl.pallas_call(functools.partial(newton_kernel, slab), out_shape=[root, r...]
    unnamed x10 -> x8, local copies, waits for them, and re-layouts: 0.78 us -> 0.02 us
  transfers between devices with their start and end apart: 6 -> 6, of which waited for: 4 -> 4; matrix products, arithmetic and copies ran while one was open for 0% -> 0% of each run, Pallas kernels for 16% -> 14%
where the time goes in v4:
time: 65.3 us; the launch traced here: 64.8 us
  starting transfers between devices  31.8 us (49%)
  waiting for transfers between devices  19.6 us (30%)
  Pallas kernels  12.7 us (19%)
  between operations  0.77 us (1%)
    all_to_all x2, starting transfers between devices, exchange(): return lax.all_to_all(values, axis, 0, 0, tiled=True)  18.8 us
    ppermute x4, starting transfers between devices, partner(): return lax.ppermute(values, axis, [(i, i ^ flip) for i in range(4)])  13 us
    ppermute x4, waiting for transfers between devices, partner(): return lax.ppermute(values, axis, [(i, i ^ flip) for i in range(4)])  10.1 us
    all_to_all x2, waiting for transfers between devices, exchange(): return lax.all_to_all(values, axis, 0, 0, tiled=True)  9.47 us
    pallas_call x1, Pallas kernels, shards(): pl.pallas_call(functools.partial(newton_kernel, slab), out_shape=[root, r...  7.5 us
    pallas_call x1, Pallas kernels, shards(): pl.pallas_call(functools.partial(grad_kernel, tokens * groups), out_shape...  2.08 us
  transfers between devices with their start and end apart: 6, of which 4 were waited for; matrix products, arithmetic and copies ran while one was open for 0% of the time, Pallas kernels for 14%

profile of v4, /device:TPU:6, one launch (start us, length us, event | category | flops | bytes accessed | tf_op | source)
XLA Modules:
  0.0 64.8 jit_solution(11711531612202772761)
XLA Ops:
  0.6 0.0 copy-start.2
  0.6 0.0 copy-start.3
  0.7 2.1 %grad_part.1.after_any = bf16[512,512]{1,0:T(8,128)(2,1)} custom-call(bf16[128,512]{1,0:T(8,128)(2,1)} %x_any.3, bf16[128,512]{1,0:T(8,128)(2,1)} %g_any.3), custom_call_target="tpu_custom_call" | custom-call | flops 67108864 | bytes 1048576 | tf_op jit(solution)/shard_map/grad_part/pallas_call | solution.py:204
  2.7 0.0 copy-start
  2.7 0.0 copy-start.1
  2.8 13.9 %all-to-all-start = ((bf16[32,16,512]{2,1,0:T(8,128)(2,1)}), bf16[32,16,512]{2,1,0:T(8,128)(2,1)S(1)}, u32[]{:S(2)}, u32[]{:S(2)}) async-start(bf16[32,16,512]{2,1,0:T(8,128)(2,1)} %bitcast.5), calls=%async_computation | async-start | bytes 1048576 | tf_op jit(solution)/shard_map/all_to_all | solution.py:187
  16.7 0.0 copy-done.2
  16.7 0.0 copy-done.3
  16.7 0.0 copy-done
  16.7 0.0 copy-done.1
  16.7 0.8 %outputs_part.1 = (bf16[128,512]{1,0:T(8,128)(2,1)S(1)}, bf16[128,512]{1,0:T(8,128)(2,1)S(1)}) custom-call(bf16[128,512]{1,0:T(8,128)(2,1)S(1)} %copy-done.2, bf16[128,512]{1,0:T(8,128)(2,1)S(1)} %copy-done.3, bf16[512,512]{1,0:T(8,128)(2,1)S(1)} %copy-done.1, bf16[512,512]{1,0:T(8,128)(2,1)S(1)} %copy-done), custom_call_target="tpu_custom_call" | custom-call | flops 134217728 | bytes 1048576 | tf_op jit(solution)/shard_map/outputs_part/pallas_call | solution.py:221
  17.5 1.9 %collective-permute-start.1 = (bf16[128,512]{1,0:T(8,128)(2,1)S(1)}, bf16[128,512]{1,0:T(8,128)(2,1)S(1)}, u32[]{:S(2)}, u32[]{:S(2)}) collective-permute-start(bf16[128,512]{1,0:T(8,128)(2,1)S(1)} %get-tuple-element.14.layer_ref), channel_id=1, source_target_pairs={{0,1},{1,0},{2,3},{3,2},{4,5},{5,4},{6,7},{7,6},{8,9},{9,8},{10,11... | collective-permute-start | bytes 393224 | tf_op jit(solution)/shard_map/ppermute | solution.py:191
  19.4 2.7 %collective-permute-start = (bf16[128,512]{1,0:T(8,128)(2,1)S(1)}, bf16[128,512]{1,0:T(8,128)(2,1)S(1)}, u32[]{:S(2)}, u32[]{:S(2)}) collective-permute-start(bf16[128,512]{1,0:T(8,128)(2,1)S(1)} %get-tuple-element.13.input_ref), channel_id=1, source_target_pairs={{0,4},{4,0},{8,12},{12,8},{1,5},{5,1},{9,13},{13,9},{2,6},{6,2},{1... | collective-permute-start | bytes 393224 | tf_op jit(solution)/shard_map/ppermute | solution.py:191
  22.2 0.0 collective-permute-done.1.layer_any.layer_other
  22.2 5.0 %collective-permute-done.input_other = bf16[128,512]{1,0:T(8,128)(2,1)S(1)} collective-permute-done((bf16[128,512]{1,0:T(8,128)(2,1)S(1)}, bf16[128,512]{1,0:T(8,128)(2,1)S(1)}, u32[]{:S(2)}, u32[]{:S(2)}) %collective-permute-start) | collective-permute-done | bytes 131104 | tf_op jit(solution)/shard_map/ppermute | solution.py:191
  27.2 6.6 %all-to-all-done = bf16[32,16,512]{2,1,0:T(8,128)(2,1)S(1)} async-done(((bf16[32,16,512]{2,1,0:T(8,128)(2,1)}), bf16[32,16,512]{2,1,0:T(8,128)(2,1)S(1)}, u32[]{:S(2)}, u32[]{:S(2)}) %all-to-all-start) | async-done | bytes 524320 | tf_op jit(solution)/shard_map/all_to_all | solution.py:187
  33.9 0.9 %sums.1 = (bf16[512,512]{1,0:T(8,128)(2,1)}, bf16[128,512]{1,0:T(8,128)(2,1)S(1)}) custom-call(bf16[512,512]{1,0:T(8,128)(2,1)S(1)} %bitcast.6, bf16[128,512]{1,0:T(8,128)(2,1)S(1)} %get-tuple-element.13.input_ref, bf16[128,512]{1,0:T(8,128)(2,1)S(1)} %collective-permute-done.input_other, bf16[128,512]{1,0:T(8,128)(2,1)S(1)} %collective-permute-done.1.layer_any.layer_other), custom_call_target="tpu_custom_call" | custom-call | flops 262144 | bytes 1048576 | tf_op jit(solution)/shard_map/sums/pallas_call | solution.py:237
  34.8 4.9 %all-to-all-start.1 = ((bf16[32,16,512]{2,1,0:T(8,128)(2,1)}), bf16[32,16,512]{2,1,0:T(8,128)(2,1)S(1)}, u32[]{:S(2)}, u32[]{:S(2)}) async-start(bf16[32,16,512]{2,1,0:T(8,128)(2,1)} %bitcast.3), calls=%async_computation.1 | async-start | bytes 1048576 | tf_op jit(solution)/shard_map/all_to_all | solution.py:187
  39.7 3.3 %collective-permute-start.2 = (bf16[128,512]{1,0:T(8,128)(2,1)S(1)}, bf16[128,512]{1,0:T(8,128)(2,1)S(1)}, u32[]{:S(2)}, u32[]{:S(2)}) collective-permute-start(bf16[128,512]{1,0:T(8,128)(2,1)S(1)} %get-tuple-element.15.input_ref), channel_id=1, source_target_pairs={{0,8},{4,12},{8,0},{12,4},{1,9},{5,13},{9,1},{13,5},{2,10},{6,14},... | collective-permute-start | bytes 393224 | tf_op jit(solution)/shard_map/ppermute | solution.py:191
  43.0 5.0 %collective-permute-done.2.input_other = bf16[128,512]{1,0:T(8,128)(2,1)S(1)} collective-permute-done((bf16[128,512]{1,0:T(8,128)(2,1)S(1)}, bf16[128,512]{1,0:T(8,128)(2,1)S(1)}, u32[]{:S(2)}, u32[]{:S(2)}) %collective-permute-start.2) | collective-permute-done | bytes 131104 | tf_op jit(solution)/shard_map/ppermute | solution.py:191
  48.1 0.7 %middle.1 = (bf16[128,512]{1,0:T(8,128)(2,1)}, bf16[128,512]{1,0:T(8,128)(2,1)S(1)}) custom-call(bf16[128,512]{1,0:T(8,128)(2,1)S(1)} %get-tuple-element.15.input_ref, bf16[128,512]{1,0:T(8,128)(2,1)S(1)} %collective-permute-done.2.input_other, bf16[128,512]{1,0:T(8,128)(2,1)S(1)} %get-tuple-element.14.layer_ref, ...), custom_call_target="tpu_custom_call" | custom-call | bytes 524288 | tf_op jit(solution)/shard_map/middle/pallas_call | solution.py:248
  48.8 5.0 %collective-permute-start.3 = (bf16[128,512]{1,0:T(8,128)(2,1)S(1)}, bf16[128,512]{1,0:T(8,128)(2,1)S(1)}, u32[]{:S(2)}, u32[]{:S(2)}) collective-permute-start(bf16[128,512]{1,0:T(8,128)(2,1)S(1)} %get-tuple-element.16.layer_ref), channel_id=1, source_target_pairs={{0,2},{1,3},{2,0},{3,1},{4,6},{5,7},{6,4},{7,5},{8,10},{9,11},{10,... | collective-permute-start | bytes 393224 | tf_op jit(solution)/shard_map/ppermute | solution.py:191
  53.8 2.8 %all-to-all-done.1 = bf16[32,16,512]{2,1,0:T(8,128)(2,1)S(1)} async-done(((bf16[32,16,512]{2,1,0:T(8,128)(2,1)}), bf16[32,16,512]{2,1,0:T(8,128)(2,1)S(1)}, u32[]{:S(2)}, u32[]{:S(2)}) %all-to-all-start.1) | async-done | bytes 524320 | tf_op jit(solution)/shard_map/all_to_all | solution.py:187
  56.6 7.5 %newton.1 = (f32[1,16,512]{2,1,0:T(8,128)}, f32[1,16,512]{2,1,0:T(8,128)}, f32[8,128]{1,0:T(8,128)S(1)}) custom-call(s32[1]{0:T(128)} %bitcast.2.place_ref, bf16[512,512]{1,0:T(8,128)(2,1)S(1)} %bitcast.7), custom_call_target="tpu_custom_call" | custom-call | bytes 65536 | tf_op jit(solution)/shard_map/newton/pallas_call | solution.py:260
  64.1 0.0 collective-permute-done.3.layer_other
  64.1 0.7 %last.1 = bf16[128,512]{1,0:T(8,128)(2,1)} custom-call(bf16[128,512]{1,0:T(8,128)(2,1)S(1)} %get-tuple-element.16.layer_ref, bf16[128,512]{1,0:T(8,128)(2,1)S(1)} %collective-permute-done.3.layer_other, f32[8,128]{1,0:T(8,128)S(1)} %get-tuple-element.18.done_ref), custom_call_target="tpu_custom_call" | custom-call | bytes 262144 | tf_op jit(solution)/shard_map/last/pallas_call | solution.py:276
Async XLA Ops:
  0.6 16.0 %copy-start.2 = (bf16[128,512]{1,0:T(8,128)(2,1)S(1)}, bf16[128,512]{1,0:T(8,128)(2,1)}, u32[]{:S(2)}) copy-start(bf16[128,512]{1,0:T(8,128)(2,1)} %x_any.3) | copy-start | bytes 393220
  0.6 16.0 %copy-start.3 = (bf16[128,512]{1,0:T(8,128)(2,1)S(1)}, bf16[128,512]{1,0:T(8,128)(2,1)}, u32[]{:S(2)}) copy-start(bf16[128,512]{1,0:T(8,128)(2,1)} %g_any.3) | copy-start | bytes 393220
  2.7 13.9 %copy-start = (bf16[512,512]{1,0:T(8,128)(2,1)S(1)}, bf16[512,512]{1,0:T(8,128)(2,1)}, u32[]{:S(2)}) copy-start(bf16[512,512]{1,0:T(8,128)(2,1)} %grad_part.1.after_any) | copy-start | bytes 1572868
  2.7 13.9 %copy-start.1 = (bf16[512,512]{1,0:T(8,128)(2,1)S(1)}, bf16[512,512]{1,0:T(8,128)(2,1)}, u32[]{:S(2)}) copy-start(bf16[512,512]{1,0:T(8,128)(2,1)} %w_any.1) | copy-start | bytes 1572868
  2.8 31.1 %all-to-all-start = ((bf16[32,16,512]{2,1,0:T(8,128)(2,1)}), bf16[32,16,512]{2,1,0:T(8,128)(2,1)S(1)}, u32[]{:S(2)}, u32[]{:S(2)}) async-start(bf16[32,16,512]{2,1,0:T(8,128)(2,1)} %bitcast.5), calls=%async_computation | async-start | bytes 1048576 | tf_op jit(solution)/shard_map/all_to_all | solution.py:187
  17.5 4.7 %collective-permute-start.1 = (bf16[128,512]{1,0:T(8,128)(2,1)S(1)}, bf16[128,512]{1,0:T(8,128)(2,1)S(1)}, u32[]{:S(2)}, u32[]{:S(2)}) collective-permute-start(bf16[128,512]{1,0:T(8,128)(2,1)S(1)} %get-tuple-element.14.layer_ref), channel_id=1, source_target_pairs={{0,1},{1,0},{2,3},{3,2},{4,5},{5,4},{6,7},{7,6},{8,9},{9,8},{10,11... | collective-permute-start | bytes 393224 | tf_op jit(solution)/shard_map/ppermute | solution.py:191
  19.4 7.8 %collective-permute-start = (bf16[128,512]{1,0:T(8,128)(2,1)S(1)}, bf16[128,512]{1,0:T(8,128)(2,1)S(1)}, u32[]{:S(2)}, u32[]{:S(2)}) collective-permute-start(bf16[128,512]{1,0:T(8,128)(2,1)S(1)} %get-tuple-element.13.input_ref), channel_id=1, source_target_pairs={{0,4},{4,0},{8,12},{12,8},{1,5},{5,1},{9,13},{13,9},{2,6},{6,2},{1... | collective-permute-start | bytes 393224 | tf_op jit(solution)/shard_map/ppermute | solution.py:191
  34.8 21.8 %all-to-all-start.1 = ((bf16[32,16,512]{2,1,0:T(8,128)(2,1)}), bf16[32,16,512]{2,1,0:T(8,128)(2,1)S(1)}, u32[]{:S(2)}, u32[]{:S(2)}) async-start(bf16[32,16,512]{2,1,0:T(8,128)(2,1)} %bitcast.3), calls=%async_computation.1 | async-start | bytes 1048576 | tf_op jit(solution)/shard_map/all_to_all | solution.py:187
  39.7 8.4 %collective-permute-start.2 = (bf16[128,512]{1,0:T(8,128)(2,1)S(1)}, bf16[128,512]{1,0:T(8,128)(2,1)S(1)}, u32[]{:S(2)}, u32[]{:S(2)}) collective-permute-start(bf16[128,512]{1,0:T(8,128)(2,1)S(1)} %get-tuple-element.15.input_ref), channel_id=1, source_target_pairs={{0,8},{4,12},{8,0},{12,4},{1,9},{5,13},{9,1},{13,5},{2,10},{6,14},... | collective-permute-start | bytes 393224 | tf_op jit(solution)/shard_map/ppermute | solution.py:191
  48.8 15.4 %collective-permute-start.3 = (bf16[128,512]{1,0:T(8,128)(2,1)S(1)}, bf16[128,512]{1,0:T(8,128)(2,1)S(1)}, u32[]{:S(2)}, u32[]{:S(2)}) collective-permute-start(bf16[128,512]{1,0:T(8,128)(2,1)S(1)} %get-tuple-element.16.layer_ref), channel_id=1, source_target_pairs={{0,2},{1,3},{2,0},{3,1},{4,6},{5,7},{6,4},{7,5},{8,10},{9,11},{10,... | collective-permute-start | bytes 393224 | tf_op jit(solution)/shard_map/ppermute | solution.py:191

commit v5 on v4

--- a/solution.py
+++ b/solution.py
@@ -8,7 +8,6 @@
 from jax.sharding import PartitionSpec as P
 
 ITERS = 6
-CHUNKS = 2
 VMEM = pl.BlockSpec(memory_space=pltpu.VMEM)
 HBM = pl.BlockSpec(memory_space=pltpu.HBM)
 ANY = pl.BlockSpec(memory_space=pl.ANY)
@@ -29,18 +28,10 @@
         copy.wait()
 
 
-def grad_kernel(tokens_all, x_any, g_any, grad_any, x_ref, g_ref, grad_ref, sems, out_sems):
+def grad_kernel(tokens_all, x_any, g_any, grad_ref, x_ref, g_ref, sems):
     fetch((x_any, g_any), (x_ref, g_ref), sems)
-    copies = []
-    chunk = grad_ref.shape[0] // CHUNKS
-    for k in range(CHUNKS):
-        rows = slice(k * chunk, (k + 1) * chunk)
-        grad = mm(x_ref[:, rows], g_ref[...], ((0,), (0,)))
-        grad_ref[rows, :] = (grad * (1.0 / tokens_all)).astype(BF16)
-        copies.append(pltpu.make_async_copy(grad_ref.at[rows, :], grad_any.at[rows, :], out_sems.at[k]))
-        copies[k].start()
-    for copy in copies:
-        copy.wait()
+    grad = mm(x_ref[...], g_ref[...], ((0,), (0,)))
+    grad_ref[...] = (grad * (1.0 / tokens_all)).astype(BF16)
 
 
 def pair_sum(left_ref, right_ref):
@@ -69,8 +60,10 @@
     input_out[...] = pair_sum(input_ref, input_other)
 
 
-def last_kernel(layer_ref, layer_other, done_ref, layer_out):
+def last_kernel(layer_ref, layer_other, left_ref, right_ref, layer_out, left_out, right_out):
     layer_out[...] = pair_sum(layer_ref, layer_other)
+    left_out[...] = left_ref[...]
+    right_out[...] = right_ref[...]
 
 
 def staged(units):
@@ -83,7 +76,7 @@
     waiting[0](waiting[1])
 
 
-def newton_kernel(slab, place_ref, block_ref, left_ref, right_ref, done_ref, wide, n_low, c_low, h_low, row):
+def newton_kernel(slab, place_ref, block_ref, left_ref, right_ref, wide, n_low, c_low, h_low, row):
     extent = block_ref.shape[0]
     half = extent // 2
     top, low = slice(0, half), slice(half, extent)
@@ -166,17 +159,20 @@
         units += [unit(part(square_n, now, riders), part(keep_c, now, riders), *at) for at in sides]
         units += [unit(square_c, keep_h, *at) for at in sides]
         units += [unit(part(next_n, now), part(keep_n, now, k == 0), *at) for at in sides]
+    now = (ITERS - 2) % 2
+    units += [unit(functools.partial(square_n, now, slab), functools.partial(keep_c, now, slab), *at) for at in sides]
     staged(units)
 
-    now = (ITERS - 2) % 2
-    firsts = [1.25 * row[side] - mm(n_low[side, now, extent:, :], n_low[side, now, :extent, :]) for side in range(2)]
-    ends = list(firsts)
-    for _ in range(4):
+    ends = [row[side] for side in range(2)]
+    for _ in range(2):
         for side in range(2):
-            ends[side] = 1.25 * ends[side] - mm(ends[side].astype(BF16), n_low[side, now, :extent, :])
+            ends[side] = 1.5625 * ends[side] + mm(ends[side].astype(BF16), c_low[side])
     for side in range(2):
-        outs[side][0] = 1.25 * firsts[side] - mm(ends[side].astype(BF16), n_low[side, now, :extent, :])
-    done_ref[...] = jnp.zeros_like(done_ref)
+        outs[side][0] = 1.25 * row[side] - mm(ends[side].astype(BF16), n_low[side, now, :extent, :])
+
+
+def in_hbm(values):
+    return pltpu.with_memory_space_constraint(values, pltpu.HBM)
 
 
 def limit(mebibytes):
@@ -197,7 +193,7 @@
     groups = lax.axis_size("dp")
     slab = extent // groups
     place = lax.axis_index("dp").astype(jnp.int32).reshape(1)
-    block = jax.ShapeDtypeStruct((extent, extent), BF16)
+    block = pltpu.VMEM((extent, extent), BF16)
     whole = jax.ShapeDtypeStruct((tokens, extent), BF16)
     tokens_vmem = pltpu.VMEM((tokens, extent), BF16)
 
@@ -205,18 +201,12 @@
         functools.partial(grad_kernel, tokens * groups),
         out_shape=block,
         in_specs=[HBM, HBM],
-        out_specs=HBM,
-        scratch_shapes=[
-            tokens_vmem,
-            tokens_vmem,
-            pltpu.VMEM((extent, extent), BF16),
-            pltpu.SemaphoreType.DMA((2,)),
-            pltpu.SemaphoreType.DMA((CHUNKS,)),
-        ],
-        compiler_params=limit(63),
+        out_specs=VMEM,
+        scratch_shapes=[tokens_vmem, tokens_vmem, pltpu.SemaphoreType.DMA((2,))],
+        compiler_params=limit(8),
         cost_estimate=pl.CostEstimate(flops=2 * tokens * extent * extent, bytes_accessed=2**20, transcendentals=0),
         name="grad_part",
-    )(x_in, grad_out)
+    )(in_hbm(x_in), in_hbm(grad_out))
     received = exchange(grad_part, "dp")
     layer_part, input_part = pl.pallas_call(
         outputs_kernel,
@@ -257,11 +247,11 @@
     layer_other = partner(layer_sum, "precond", 2)
 
     root = jax.ShapeDtypeStruct((1, slab, extent), F32)
-    left_root, right_root, done = pl.pallas_call(
+    left_near, right_near = pl.pallas_call(
         functools.partial(newton_kernel, slab),
-        out_shape=[root, root, jax.ShapeDtypeStruct((8, 128), F32)],
+        out_shape=[pltpu.VMEM((1, slab, extent), F32)] * 2,
         in_specs=[SMEM, VMEM],
-        out_specs=[VMEM] * 3,
+        out_specs=[VMEM] * 2,
         scratch_shapes=[
             pltpu.VMEM((2, extent, extent), F32),
             pltpu.VMEM((2, 2, extent + slab, extent), BF16),
@@ -273,15 +263,15 @@
         cost_estimate=pl.CostEstimate(flops=0, bytes_accessed=2**16, transcendentals=0),
         name="newton",
     )(place, grad_low)
-    layer_out = pl.pallas_call(
+    layer_out, left_root, right_root = pl.pallas_call(
         last_kernel,
-        out_shape=whole,
-        in_specs=[VMEM, VMEM, VMEM],
-        out_specs=VMEM,
+        out_shape=[whole, root, root],
+        in_specs=[VMEM] * 4,
+        out_specs=[VMEM] * 3,
         compiler_params=limit(8),
         cost_estimate=pl.CostEstimate(flops=0, bytes_accessed=2**18, transcendentals=0),
         name="last",
-    )(layer_sum, layer_other, done)
+    )(layer_sum, layer_other, left_near, right_near)
     return layer_out, grad_in, left_root, right_root
 
 

time: 65.3 us -> 64.7 us (level)
  transfers between devices with their start and end apart: 6 -> 6, of which waited for: 4 -> 4; matrix products, arithmetic and copies ran while one was open for 0% -> 0% of each run, Pallas kernels for 14% -> 13%
where the time goes in v5:
time: 64.7 us; the launch traced here: 64.2 us
  starting transfers between devices  31.8 us (49%)
  waiting for transfers between devices  19.6 us (30%)
  Pallas kernels  12.1 us (19%)
  between operations  0.76 us (1%)
    all_to_all x2, starting transfers between devices, exchange(): return lax.all_to_all(values, axis, 0, 0, tiled=True)  18.8 us
    ppermute x4, starting transfers between devices, partner(): return lax.ppermute(values, axis, [(i, i ^ flip) for i in range(4)])  13 us
    ppermute x4, waiting for transfers between devices, partner(): return lax.ppermute(values, axis, [(i, i ^ flip) for i in range(4)])  10.1 us
    all_to_all x2, waiting for transfers between devices, exchange(): return lax.all_to_all(values, axis, 0, 0, tiled=True)  9.49 us
    pallas_call x1, Pallas kernels, shards(): pl.pallas_call(functools.partial(newton_kernel, slab), out_shape=[pltpu.V...  6.87 us
    pallas_call x1, Pallas kernels, shards(): pl.pallas_call(functools.partial(grad_kernel, tokens * groups), out_shape...  2.09 us
  transfers between devices with their start and end apart: 6, of which 4 were waited for; matrix products, arithmetic and copies ran while one was open for 0% of the time, Pallas kernels for 13%

profile of v5, /device:TPU:6, one launch (start us, length us, event | category | flops | bytes accessed | tf_op | source)
XLA Modules:
  0.0 64.2 jit_solution(10781042795850984757)
XLA Ops:
  0.6 2.1 %grad_part.1.after_any = bf16[512,512]{1,0:T(8,128)(2,1)} custom-call(bf16[128,512]{1,0:T(8,128)(2,1)} %x_any.3, bf16[128,512]{1,0:T(8,128)(2,1)} %g_any.3), custom_call_target="tpu_custom_call" | custom-call | flops 67108864 | bytes 1048576 | tf_op jit(solution)/shard_map/grad_part/pallas_call | solution.py:200
  2.7 0.0 copy-start
  2.7 0.0 copy-start.1
  2.8 0.0 copy-start.2
  2.8 13.9 %all-to-all-start = ((bf16[32,16,512]{2,1,0:T(8,128)(2,1)}), bf16[32,16,512]{2,1,0:T(8,128)(2,1)S(1)}, u32[]{:S(2)}, u32[]{:S(2)}) async-start(bf16[32,16,512]{2,1,0:T(8,128)(2,1)} %bitcast), calls=%async_computation | async-start | bytes 1048576 | tf_op jit(solution)/shard_map/all_to_all | solution.py:183
  16.7 0.0 copy-done
  16.7 0.0 copy-done.1
  16.7 0.0 copy-done.2
  16.7 0.8 %outputs_part.1 = (bf16[128,512]{1,0:T(8,128)(2,1)S(1)}, bf16[128,512]{1,0:T(8,128)(2,1)S(1)}) custom-call(bf16[128,512]{1,0:T(8,128)(2,1)S(1)} %copy-done.1, bf16[128,512]{1,0:T(8,128)(2,1)S(1)} %copy-done.2, bf16[512,512]{1,0:T(8,128)(2,1)S(1)} %copy-done, bf16[512,512]{1,0:T(8,128)(2,1)} %grad_part.1.after_any), custom_call_target="tpu_custom_call" | custom-call | flops 134217728 | bytes 1048576 | tf_op jit(solution)/shard_map/outputs_part/pallas_call | solution.py:211
  17.5 1.9 %collective-permute-start.1 = (bf16[128,512]{1,0:T(8,128)(2,1)S(1)}, bf16[128,512]{1,0:T(8,128)(2,1)S(1)}, u32[]{:S(2)}, u32[]{:S(2)}) collective-permute-start(bf16[128,512]{1,0:T(8,128)(2,1)S(1)} %get-tuple-element.16.layer_ref), channel_id=1, source_target_pairs={{0,1},{1,0},{2,3},{3,2},{4,5},{5,4},{6,7},{7,6},{8,9},{9,8},{10,11... | collective-permute-start | bytes 393224 | tf_op jit(solution)/shard_map/ppermute | solution.py:187
  19.4 2.7 %collective-permute-start = (bf16[128,512]{1,0:T(8,128)(2,1)S(1)}, bf16[128,512]{1,0:T(8,128)(2,1)S(1)}, u32[]{:S(2)}, u32[]{:S(2)}) collective-permute-start(bf16[128,512]{1,0:T(8,128)(2,1)S(1)} %get-tuple-element.15.input_ref), channel_id=1, source_target_pairs={{0,4},{4,0},{8,12},{12,8},{1,5},{5,1},{9,13},{13,9},{2,6},{6,2},{1... | collective-permute-start | bytes 393224 | tf_op jit(solution)/shard_map/ppermute | solution.py:187
  22.2 0.0 collective-permute-done.1.layer_any.layer_other
  22.2 5.0 %collective-permute-done.input_other = bf16[128,512]{1,0:T(8,128)(2,1)S(1)} collective-permute-done((bf16[128,512]{1,0:T(8,128)(2,1)S(1)}, bf16[128,512]{1,0:T(8,128)(2,1)S(1)}, u32[]{:S(2)}, u32[]{:S(2)}) %collective-permute-start) | collective-permute-done | bytes 131104 | tf_op jit(solution)/shard_map/ppermute | solution.py:187
  27.2 6.6 %all-to-all-done = bf16[32,16,512]{2,1,0:T(8,128)(2,1)S(1)} async-done(((bf16[32,16,512]{2,1,0:T(8,128)(2,1)}), bf16[32,16,512]{2,1,0:T(8,128)(2,1)S(1)}, u32[]{:S(2)}, u32[]{:S(2)}) %all-to-all-start) | async-done | bytes 524320 | tf_op jit(solution)/shard_map/all_to_all | solution.py:183
  33.9 0.9 %sums.1 = (bf16[512,512]{1,0:T(8,128)(2,1)}, bf16[128,512]{1,0:T(8,128)(2,1)S(1)}) custom-call(bf16[512,512]{1,0:T(8,128)(2,1)S(1)} %bitcast.5, bf16[128,512]{1,0:T(8,128)(2,1)S(1)} %get-tuple-element.15.input_ref, bf16[128,512]{1,0:T(8,128)(2,1)S(1)} %collective-permute-done.input_other, bf16[128,512]{1,0:T(8,128)(2,1)S(1)} %collective-permute-done.1.layer_any.layer_other), custom_call_target="tpu_custom_call" | custom-call | flops 262144 | bytes 1048576 | tf_op jit(solution)/shard_map/sums/pallas_call | solution.py:227
  34.8 4.9 %all-to-all-start.1 = ((bf16[32,16,512]{2,1,0:T(8,128)(2,1)}), bf16[32,16,512]{2,1,0:T(8,128)(2,1)S(1)}, u32[]{:S(2)}, u32[]{:S(2)}) async-start(bf16[32,16,512]{2,1,0:T(8,128)(2,1)} %bitcast.3), calls=%async_computation.1 | async-start | bytes 1048576 | tf_op jit(solution)/shard_map/all_to_all | solution.py:183
  39.7 3.3 %collective-permute-start.2 = (bf16[128,512]{1,0:T(8,128)(2,1)S(1)}, bf16[128,512]{1,0:T(8,128)(2,1)S(1)}, u32[]{:S(2)}, u32[]{:S(2)}) collective-permute-start(bf16[128,512]{1,0:T(8,128)(2,1)S(1)} %get-tuple-element.17.input_ref), channel_id=1, source_target_pairs={{0,8},{4,12},{8,0},{12,4},{1,9},{5,13},{9,1},{13,5},{2,10},{6,14},... | collective-permute-start | bytes 393224 | tf_op jit(solution)/shard_map/ppermute | solution.py:187
  43.0 5.0 %collective-permute-done.2.input_other = bf16[128,512]{1,0:T(8,128)(2,1)S(1)} collective-permute-done((bf16[128,512]{1,0:T(8,128)(2,1)S(1)}, bf16[128,512]{1,0:T(8,128)(2,1)S(1)}, u32[]{:S(2)}, u32[]{:S(2)}) %collective-permute-start.2) | collective-permute-done | bytes 131104 | tf_op jit(solution)/shard_map/ppermute | solution.py:187
  48.1 0.7 %middle.1 = (bf16[128,512]{1,0:T(8,128)(2,1)}, bf16[128,512]{1,0:T(8,128)(2,1)S(1)}) custom-call(bf16[128,512]{1,0:T(8,128)(2,1)S(1)} %get-tuple-element.17.input_ref, bf16[128,512]{1,0:T(8,128)(2,1)S(1)} %collective-permute-done.2.input_other, bf16[128,512]{1,0:T(8,128)(2,1)S(1)} %get-tuple-element.16.layer_ref, ...), custom_call_target="tpu_custom_call" | custom-call | bytes 524288 | tf_op jit(solution)/shard_map/middle/pallas_call | solution.py:238
  48.8 5.0 %collective-permute-start.3 = (bf16[128,512]{1,0:T(8,128)(2,1)S(1)}, bf16[128,512]{1,0:T(8,128)(2,1)S(1)}, u32[]{:S(2)}, u32[]{:S(2)}) collective-permute-start(bf16[128,512]{1,0:T(8,128)(2,1)S(1)} %get-tuple-element.18.layer_ref), channel_id=1, source_target_pairs={{0,2},{1,3},{2,0},{3,1},{4,6},{5,7},{6,4},{7,5},{8,10},{9,11},{10,... | collective-permute-start | bytes 393224 | tf_op jit(solution)/shard_map/ppermute | solution.py:187
  53.8 2.8 %all-to-all-done.1 = bf16[32,16,512]{2,1,0:T(8,128)(2,1)S(1)} async-done(((bf16[32,16,512]{2,1,0:T(8,128)(2,1)}), bf16[32,16,512]{2,1,0:T(8,128)(2,1)S(1)}, u32[]{:S(2)}, u32[]{:S(2)}) %all-to-all-start.1) | async-done | bytes 524320 | tf_op jit(solution)/shard_map/all_to_all | solution.py:183
  56.6 6.9 %newton.1 = (f32[1,16,512]{2,1,0:T(8,128)S(1)}, f32[1,16,512]{2,1,0:T(8,128)S(1)}) custom-call(s32[1]{0:T(128)} %bitcast.2.place_ref, bf16[512,512]{1,0:T(8,128)(2,1)S(1)} %bitcast.6), custom_call_target="tpu_custom_call" | custom-call | bytes 65536 | tf_op jit(solution)/shard_map/newton/pallas_call | solution.py:250
  63.5 0.0 collective-permute-done.3.layer_other
  63.5 0.7 %last.1 = (bf16[128,512]{1,0:T(8,128)(2,1)}, f32[1,16,512]{2,1,0:T(8,128)}, f32[1,16,512]{2,1,0:T(8,128)}) custom-call(bf16[128,512]{1,0:T(8,128)(2,1)S(1)} %get-tuple-element.18.layer_ref, bf16[128,512]{1,0:T(8,128)(2,1)S(1)} %collective-permute-done.3.layer_other, f32[1,16,512]{2,1,0:T(8,128)S(1)} %get-tuple-element.20.left_ref, ...), custom_call_target="tpu_custom_call" | custom-call | bytes 262144 | tf_op jit(solution)/shard_map/last/pallas_call | solution.py:266
Async XLA Ops:
  2.7 13.9 %copy-start = (bf16[512,512]{1,0:T(8,128)(2,1)S(1)}, bf16[512,512]{1,0:T(8,128)(2,1)}, u32[]{:S(2)}) copy-start(bf16[512,512]{1,0:T(8,128)(2,1)} %w_any.1) | copy-start | bytes 1572868
  2.7 13.9 %copy-start.1 = (bf16[128,512]{1,0:T(8,128)(2,1)S(1)}, bf16[128,512]{1,0:T(8,128)(2,1)}, u32[]{:S(2)}) copy-start(bf16[128,512]{1,0:T(8,128)(2,1)} %x_any.3) | copy-start | bytes 393220
  2.8 13.9 %copy-start.2 = (bf16[128,512]{1,0:T(8,128)(2,1)S(1)}, bf16[128,512]{1,0:T(8,128)(2,1)}, u32[]{:S(2)}) copy-start(bf16[128,512]{1,0:T(8,128)(2,1)} %g_any.3) | copy-start | bytes 393220
  2.8 31.1 %all-to-all-start = ((bf16[32,16,512]{2,1,0:T(8,128)(2,1)}), bf16[32,16,512]{2,1,0:T(8,128)(2,1)S(1)}, u32[]{:S(2)}, u32[]{:S(2)}) async-start(bf16[32,16,512]{2,1,0:T(8,128)(2,1)} %bitcast), calls=%async_computation | async-start | bytes 1048576 | tf_op jit(solution)/shard_map/all_to_all | solution.py:183
  17.5 4.7 %collective-permute-start.1 = (bf16[128,512]{1,0:T(8,128)(2,1)S(1)}, bf16[128,512]{1,0:T(8,128)(2,1)S(1)}, u32[]{:S(2)}, u32[]{:S(2)}) collective-permute-start(bf16[128,512]{1,0:T(8,128)(2,1)S(1)} %get-tuple-element.16.layer_ref), channel_id=1, source_target_pairs={{0,1},{1,0},{2,3},{3,2},{4,5},{5,4},{6,7},{7,6},{8,9},{9,8},{10,11... | collective-permute-start | bytes 393224 | tf_op jit(solution)/shard_map/ppermute | solution.py:187
  19.4 7.8 %collective-permute-start = (bf16[128,512]{1,0:T(8,128)(2,1)S(1)}, bf16[128,512]{1,0:T(8,128)(2,1)S(1)}, u32[]{:S(2)}, u32[]{:S(2)}) collective-permute-start(bf16[128,512]{1,0:T(8,128)(2,1)S(1)} %get-tuple-element.15.input_ref), channel_id=1, source_target_pairs={{0,4},{4,0},{8,12},{12,8},{1,5},{5,1},{9,13},{13,9},{2,6},{6,2},{1... | collective-permute-start | bytes 393224 | tf_op jit(solution)/shard_map/ppermute | solution.py:187
  34.8 21.8 %all-to-all-start.1 = ((bf16[32,16,512]{2,1,0:T(8,128)(2,1)}), bf16[32,16,512]{2,1,0:T(8,128)(2,1)S(1)}, u32[]{:S(2)}, u32[]{:S(2)}) async-start(bf16[32,16,512]{2,1,0:T(8,128)(2,1)} %bitcast.3), calls=%async_computation.1 | async-start | bytes 1048576 | tf_op jit(solution)/shard_map/all_to_all | solution.py:183
  39.7 8.4 %collective-permute-start.2 = (bf16[128,512]{1,0:T(8,128)(2,1)S(1)}, bf16[128,512]{1,0:T(8,128)(2,1)S(1)}, u32[]{:S(2)}, u32[]{:S(2)}) collective-permute-start(bf16[128,512]{1,0:T(8,128)(2,1)S(1)} %get-tuple-element.17.input_ref), channel_id=1, source_target_pairs={{0,8},{4,12},{8,0},{12,4},{1,9},{5,13},{9,1},{13,5},{2,10},{6,14},... | collective-permute-start | bytes 393224 | tf_op jit(solution)/shard_map/ppermute | solution.py:187
  48.8 14.8 %collective-permute-start.3 = (bf16[128,512]{1,0:T(8,128)(2,1)S(1)}, bf16[128,512]{1,0:T(8,128)(2,1)S(1)}, u32[]{:S(2)}, u32[]{:S(2)}) collective-permute-start(bf16[128,512]{1,0:T(8,128)(2,1)S(1)} %get-tuple-element.18.layer_ref), channel_id=1, source_target_pairs={{0,2},{1,3},{2,0},{3,1},{4,6},{5,7},{6,4},{7,5},{8,10},{9,11},{10,... | collective-permute-start | bytes 393224 | tf_op jit(solution)/shard_map/ppermute | solution.py:187

commit v6 on v5

--- a/solution.py
+++ b/solution.py
@@ -8,6 +8,8 @@
 from jax.sharding import PartitionSpec as P
 
 ITERS = 6
+CHUNKS = 4
+Y_LO = 4
 VMEM = pl.BlockSpec(memory_space=pltpu.VMEM)
 HBM = pl.BlockSpec(memory_space=pltpu.HBM)
 ANY = pl.BlockSpec(memory_space=pl.ANY)
@@ -21,7 +23,12 @@
 
 
 def fetch(sources, targets, sems):
-    copies = [pltpu.make_async_copy(src, dst, sems.at[k]) for k, (src, dst) in enumerate(zip(sources, targets))]
+    copies = []
+    for source, target in zip(sources, targets):
+        size = source.shape[0] // CHUNKS
+        for k in range(CHUNKS):
+            rows = slice(k * size, (k + 1) * size)
+            copies.append(pltpu.make_async_copy(source.at[rows, :], target.at[rows, :], sems.at[len(copies)]))
     for copy in copies:
         copy.start()
     for copy in copies:
@@ -43,10 +50,15 @@
     total = parts_ref[:slab, :].astype(F32)
     for k in range(1, copies):
         total = total + parts_ref[k * slab : (k + 1) * slab, :].astype(F32)
-    total = total.astype(BF16)
-    for k in range(copies):
+    out_ref[...] = total.astype(BF16)
+    input_sum[...] = pair_sum(input_ref, input_other)
+
+
+def copies_kernel(half_ref, other_ref, out_ref):
+    slab = half_ref.shape[0]
+    total = pair_sum(half_ref, other_ref)
+    for k in range(out_ref.shape[0] // slab):
         out_ref[k * slab : (k + 1) * slab, :] = total
-    input_sum[...] = pair_sum(input_ref, input_other)
 
 
 def outputs_kernel(x_any, g_any, w_any, after_any, layer_ref, input_ref, x_ref, g_ref, w_ref, sems):
@@ -98,8 +110,9 @@
             ref[top, low] = values[half:].T
 
     def gram(side, cut):
-        left, right = (block_ref, turned) if side == 0 else (turned, block_ref)
-        return mm(left[cut.start :, :], right[:, cut])
+        if side == 0:
+            return mm(block_ref[cut.start :, :], block_ref[cut, :], ((1,), (1,)))
+        return mm(turned[cut.start :, :], block_ref[:, cut])
 
     def keep_gram(side, cut, product):
         corner = jnp.where(on_diagonal, product[:half] + 1e-06, product[:half])
@@ -179,8 +192,8 @@
     return pltpu.CompilerParams(vmem_limit_bytes=mebibytes * 2**20)
 
 
-def exchange(values, axis):
-    return lax.all_to_all(values, axis, 0, 0, tiled=True)
+def exchange(values, groups):
+    return lax.all_to_all(values, "dp", 0, 0, tiled=True, axis_index_groups=groups)
 
 
 def partner(values, axis, flip):
@@ -202,12 +215,16 @@
         out_shape=block,
         in_specs=[HBM, HBM],
         out_specs=VMEM,
-        scratch_shapes=[tokens_vmem, tokens_vmem, pltpu.SemaphoreType.DMA((2,))],
+        scratch_shapes=[tokens_vmem, tokens_vmem, pltpu.SemaphoreType.DMA((2 * CHUNKS,))],
         compiler_params=limit(8),
         cost_estimate=pl.CostEstimate(flops=2 * tokens * extent * extent, bytes_accessed=2**20, transcendentals=0),
         name="grad_part",
     )(in_hbm(x_in), in_hbm(grad_out))
-    received = exchange(grad_part, "dp")
+    z_size = groups // Y_LO
+    order = [list(range(z_size // 2)), list(range(z_size - 1, z_size // 2 - 1, -1))]
+    halves = [[z * Y_LO + y for z in zs for y in range(Y_LO)] for zs in order]
+    members = len(halves[0])
+    received = exchange(grad_part, halves)
     layer_part, input_part = pl.pallas_call(
         outputs_kernel,
         out_shape=[whole, whole],
@@ -217,23 +234,33 @@
             tokens_vmem,
             tokens_vmem,
             pltpu.VMEM((extent, extent), BF16),
-            pltpu.SemaphoreType.DMA((3,)),
+            pltpu.SemaphoreType.DMA((3 * CHUNKS,)),
         ],
         compiler_params=limit(8),
         cost_estimate=pl.CostEstimate(flops=4 * tokens * extent * extent, bytes_accessed=2**20, transcendentals=0),
         name="outputs_part",
     )(x_in, grad_out, weight, grad_part)
     layer_near = partner(layer_part, "precond", 1)
-    copies, input_sum = pl.pallas_call(
-        functools.partial(sum_kernel, groups),
-        out_shape=[block, whole],
+    half, input_sum = pl.pallas_call(
+        functools.partial(sum_kernel, members),
+        out_shape=[pltpu.VMEM((extent // members, extent), BF16), whole],
         in_specs=[VMEM, VMEM, VMEM, ANY],
         out_specs=[VMEM] * 2,
         compiler_params=limit(8),
         cost_estimate=pl.CostEstimate(flops=extent * extent, bytes_accessed=2**20, transcendentals=0),
         name="sums",
     )(received, input_part, partner(input_part, "tensor", 1), layer_near)
-    grad_low = exchange(copies, "dp")
+    across = [pair for a, b in zip(*halves) for pair in ((a, b), (b, a))]
+    copies = pl.pallas_call(
+        copies_kernel,
+        out_shape=block,
+        in_specs=[VMEM, VMEM],
+        out_specs=VMEM,
+        compiler_params=limit(8),
+        cost_estimate=pl.CostEstimate(flops=extent * extent, bytes_accessed=2**19, transcendentals=0),
+        name="copies",
+    )(half, lax.ppermute(half, "dp", across))
+    grad_low = exchange(copies, halves)
 
     grad_in, layer_sum = pl.pallas_call(
         middle_kernel,

time: 64.7 us -> 67.2 us (1.039)
  the two profiles are of different devices: /device:TPU:6 before, /device:TPU:36 now
where the time goes in v6:
time: 67.2 us; the launch traced here: 66.7 us
  starting transfers between devices  29.1 us (43%)
  waiting for transfers between devices  24 us (36%)
  Pallas kernels  12.8 us (19%)
  between operations  0.77 us (1%)
    all_to_all x2, waiting for transfers between devices, exchange(): lax.all_to_all(values, 'dp', 0, 0, tiled=True, axis_index_groups=groups)  14.4 us
    all_to_all x2, starting transfers between devices, exchange(): lax.all_to_all(values, 'dp', 0, 0, tiled=True, axis_index_groups=groups)  11.4 us
    ppermute x4, starting transfers between devices, partner(): return lax.ppermute(values, axis, [(i, i ^ flip) for i in range(4)])  10.6 us
    ppermute x4, waiting for transfers between devices, partner(): return lax.ppermute(values, axis, [(i, i ^ flip) for i in range(4)])  7.78 us
    ppermute x1, starting transfers between devices, shards(): lax.ppermute(half, 'dp', across)  7.06 us
    pallas_call x1, Pallas kernels, shards(): pl.pallas_call(functools.partial(newton_kernel, slab), out_shape=[pltpu.V...  6.83 us
    pallas_call x1, Pallas kernels, shards(): pl.pallas_call(functools.partial(grad_kernel, tokens * groups), out_shape...  2.06 us
    ppermute x1, waiting for transfers between devices, shards(): lax.ppermute(half, 'dp', across)  1.88 us
  transfers between devices with their start and end apart: 7, of which 5 were waited for; matrix products, arithmetic and copies ran while one was open for 0% of the time, Pallas kernels for 14%

profile of v6, /device:TPU:36, one launch (start us, length us, event | category | flops | bytes accessed | tf_op | source)
XLA Modules:
  0.0 66.7 jit_solution(14729854652203069272)
XLA Ops:
  0.6 2.1 %grad_part.1.after_any = bf16[512,512]{1,0:T(8,128)(2,1)} custom-call(bf16[128,512]{1,0:T(8,128)(2,1)} %x_any.3, bf16[128,512]{1,0:T(8,128)(2,1)} %g_any.3), custom_call_target="tpu_custom_call" | custom-call | flops 67108864 | bytes 1048576 | tf_op jit(solution)/shard_map/grad_part/pallas_call | solution.py:213
  2.7 0.0 copy-start
  2.7 0.0 copy-start.1
  2.7 0.0 copy-start.2
  2.7 7.8 %all-to-all-start = ((bf16[16,32,512]{2,1,0:T(8,128)(2,1)}), bf16[16,32,512]{2,1,0:T(8,128)(2,1)S(1)}, u32[]{:S(2)}, u32[]{:S(2)}) async-start(bf16[16,32,512]{2,1,0:T(8,128)(2,1)} %bitcast), calls=%async_computation | async-start | bytes 1048576 | tf_op jit(solution)/shard_map/all_to_all | solution.py:196
  10.6 0.0 copy-done
  10.6 0.0 copy-done.1
  10.6 0.0 copy-done.2
  10.6 1.5 %outputs_part.1 = (bf16[128,512]{1,0:T(8,128)(2,1)S(1)}, bf16[128,512]{1,0:T(8,128)(2,1)S(1)}) custom-call(bf16[128,512]{1,0:T(8,128)(2,1)S(1)} %copy-done.1, bf16[128,512]{1,0:T(8,128)(2,1)S(1)} %copy-done.2, bf16[512,512]{1,0:T(8,128)(2,1)S(1)} %copy-done, bf16[512,512]{1,0:T(8,128)(2,1)} %grad_part.1.after_any), custom_call_target="tpu_custom_call" | custom-call | flops 134217728 | bytes 1048576 | tf_op jit(solution)/shard_map/outputs_part/pallas_call | solution.py:228
  12.2 3.1 %collective-permute-start = (bf16[128,512]{1,0:T(8,128)(2,1)S(1)}, bf16[128,512]{1,0:T(8,128)(2,1)S(1)}, u32[]{:S(2)}, u32[]{:S(2)}) collective-permute-start(bf16[128,512]{1,0:T(8,128)(2,1)S(1)} %get-tuple-element.15.input_ref), channel_id=1, source_target_pairs={{0,4},{4,0},{8,12},{12,8},{1,5},{5,1},{9,13},{13,9},{2,6},{6,2},{1... | collective-permute-start | bytes 393224 | tf_op jit(solution)/shard_map/ppermute | solution.py:200
  15.3 1.9 %collective-permute-start.1 = (bf16[128,512]{1,0:T(8,128)(2,1)S(1)}, bf16[128,512]{1,0:T(8,128)(2,1)S(1)}, u32[]{:S(2)}, u32[]{:S(2)}) collective-permute-start(bf16[128,512]{1,0:T(8,128)(2,1)S(1)} %get-tuple-element.16.layer_ref), channel_id=1, source_target_pairs={{0,1},{1,0},{2,3},{3,2},{4,5},{5,4},{6,7},{7,6},{8,9},{9,8},{10,11... | collective-permute-start | bytes 393224 | tf_op jit(solution)/shard_map/ppermute | solution.py:200
  17.2 1.8 %collective-permute-done.input_other = bf16[128,512]{1,0:T(8,128)(2,1)S(1)} collective-permute-done((bf16[128,512]{1,0:T(8,128)(2,1)S(1)}, bf16[128,512]{1,0:T(8,128)(2,1)S(1)}, u32[]{:S(2)}, u32[]{:S(2)}) %collective-permute-start) | collective-permute-done | bytes 131104 | tf_op jit(solution)/shard_map/ppermute | solution.py:200
  19.0 0.0 collective-permute-done.1.layer_any.layer_other
  19.0 8.6 %all-to-all-done = bf16[16,32,512]{2,1,0:T(8,128)(2,1)S(1)} async-done(((bf16[16,32,512]{2,1,0:T(8,128)(2,1)}), bf16[16,32,512]{2,1,0:T(8,128)(2,1)S(1)}, u32[]{:S(2)}, u32[]{:S(2)}) %all-to-all-start) | async-done | bytes 524320 | tf_op jit(solution)/shard_map/all_to_all | solution.py:196
  27.7 0.1 sums.1
  27.8 7.1 %collective-permute-start.4 = (bf16[32,512]{1,0:T(8,128)(2,1)S(1)}, bf16[32,512]{1,0:T(8,128)(2,1)S(1)}, u32[]{:S(2)}, u32[]{:S(2)}) collective-permute-start(bf16[32,512]{1,0:T(8,128)(2,1)S(1)} %get-tuple-element.19.half_ref), channel_id=1, source_target_pairs={{0,448},{448,0},{16,464},{464,16},{32,480},{480,32},{48,496},{496,... | collective-permute-start | bytes 98312 | tf_op jit(solution)/shard_map/ppermute | solution.py:262
  34.8 1.9 %collective-permute-done.4.other_ref = bf16[32,512]{1,0:T(8,128)(2,1)S(1)} collective-permute-done((bf16[32,512]{1,0:T(8,128)(2,1)S(1)}, bf16[32,512]{1,0:T(8,128)(2,1)S(1)}, u32[]{:S(2)}, u32[]{:S(2)}) %collective-permute-start.4) | collective-permute-done | bytes 32800 | tf_op jit(solution)/shard_map/ppermute | solution.py:262
  36.7 0.8 %copies.1 = bf16[512,512]{1,0:T(8,128)(2,1)} custom-call(bf16[32,512]{1,0:T(8,128)(2,1)S(1)} %get-tuple-element.19.half_ref, bf16[32,512]{1,0:T(8,128)(2,1)S(1)} %collective-permute-done.4.other_ref), custom_call_target="tpu_custom_call" | custom-call | flops 262144 | bytes 524288 | tf_op jit(solution)/shard_map/copies/pallas_call | solution.py:254
  37.6 3.6 %all-to-all-start.1 = ((bf16[16,32,512]{2,1,0:T(8,128)(2,1)}), bf16[16,32,512]{2,1,0:T(8,128)(2,1)S(1)}, u32[]{:S(2)}, u32[]{:S(2)}) async-start(bf16[16,32,512]{2,1,0:T(8,128)(2,1)} %bitcast.3), calls=%async_computation.1 | async-start | bytes 1048576 | tf_op jit(solution)/shard_map/all_to_all | solution.py:196
  41.2 2.4 %collective-permute-start.2 = (bf16[128,512]{1,0:T(8,128)(2,1)S(1)}, bf16[128,512]{1,0:T(8,128)(2,1)S(1)}, u32[]{:S(2)}, u32[]{:S(2)}) collective-permute-start(bf16[128,512]{1,0:T(8,128)(2,1)S(1)} %get-tuple-element.17.input_ref), channel_id=1, source_target_pairs={{0,8},{4,12},{8,0},{12,4},{1,9},{5,13},{9,1},{13,5},{2,10},{6,14},... | collective-permute-start | bytes 393224 | tf_op jit(solution)/shard_map/ppermute | solution.py:200
  43.6 6.0 %collective-permute-done.2.input_other = bf16[128,512]{1,0:T(8,128)(2,1)S(1)} collective-permute-done((bf16[128,512]{1,0:T(8,128)(2,1)S(1)}, bf16[128,512]{1,0:T(8,128)(2,1)S(1)}, u32[]{:S(2)}, u32[]{:S(2)}) %collective-permute-start.2) | collective-permute-done | bytes 131104 | tf_op jit(solution)/shard_map/ppermute | solution.py:200
  49.5 0.7 %middle.1 = (bf16[128,512]{1,0:T(8,128)(2,1)}, bf16[128,512]{1,0:T(8,128)(2,1)S(1)}) custom-call(bf16[128,512]{1,0:T(8,128)(2,1)S(1)} %get-tuple-element.17.input_ref, bf16[128,512]{1,0:T(8,128)(2,1)S(1)} %collective-permute-done.2.input_other, bf16[128,512]{1,0:T(8,128)(2,1)S(1)} %get-tuple-element.16.layer_ref, ...), custom_call_target="tpu_custom_call" | custom-call | bytes 524288 | tf_op jit(solution)/shard_map/middle/pallas_call | solution.py:265
  50.2 3.2 %collective-permute-start.3 = (bf16[128,512]{1,0:T(8,128)(2,1)S(1)}, bf16[128,512]{1,0:T(8,128)(2,1)S(1)}, u32[]{:S(2)}, u32[]{:S(2)}) collective-permute-start(bf16[128,512]{1,0:T(8,128)(2,1)S(1)} %get-tuple-element.18.layer_ref), channel_id=1, source_target_pairs={{0,2},{1,3},{2,0},{3,1},{4,6},{5,7},{6,4},{7,5},{8,10},{9,11},{10,... | collective-permute-start | bytes 393224 | tf_op jit(solution)/shard_map/ppermute | solution.py:200
  53.4 5.7 %all-to-all-done.1 = bf16[16,32,512]{2,1,0:T(8,128)(2,1)S(1)} async-done(((bf16[16,32,512]{2,1,0:T(8,128)(2,1)}), bf16[16,32,512]{2,1,0:T(8,128)(2,1)S(1)}, u32[]{:S(2)}, u32[]{:S(2)}) %all-to-all-start.1) | async-done | bytes 524320 | tf_op jit(solution)/shard_map/all_to_all | solution.py:196
  59.1 6.8 %newton.1 = (f32[1,16,512]{2,1,0:T(8,128)S(1)}, f32[1,16,512]{2,1,0:T(8,128)S(1)}) custom-call(s32[1]{0:T(128)} %bitcast.2.place_ref, bf16[512,512]{1,0:T(8,128)(2,1)S(1)} %bitcast.6), custom_call_target="tpu_custom_call" | custom-call | bytes 65536 | tf_op jit(solution)/shard_map/newton/pallas_call | solution.py:277
  66.0 0.0 collective-permute-done.3.layer_other
  66.0 0.7 %last.1 = (bf16[128,512]{1,0:T(8,128)(2,1)}, f32[1,16,512]{2,1,0:T(8,128)}, f32[1,16,512]{2,1,0:T(8,128)}) custom-call(bf16[128,512]{1,0:T(8,128)(2,1)S(1)} %get-tuple-element.18.layer_ref, bf16[128,512]{1,0:T(8,128)(2,1)S(1)} %collective-permute-done.3.layer_other, f32[1,16,512]{2,1,0:T(8,128)S(1)} %get-tuple-element.20.left_ref, ...), custom_call_target="tpu_custom_call" | custom-call | bytes 262144 | tf_op jit(solution)/shard_map/last/pallas_call | solution.py:293
Async XLA Ops:
  2.7 7.9 %copy-start = (bf16[512,512]{1,0:T(8,128)(2,1)S(1)}, bf16[512,512]{1,0:T(8,128)(2,1)}, u32[]{:S(2)}) copy-start(bf16[512,512]{1,0:T(8,128)(2,1)} %w_any.1) | copy-start | bytes 1572868
  2.7 7.9 %copy-start.1 = (bf16[128,512]{1,0:T(8,128)(2,1)S(1)}, bf16[128,512]{1,0:T(8,128)(2,1)}, u32[]{:S(2)}) copy-start(bf16[128,512]{1,0:T(8,128)(2,1)} %x_any.3) | copy-start | bytes 393220
  2.7 7.9 %copy-start.2 = (bf16[128,512]{1,0:T(8,128)(2,1)S(1)}, bf16[128,512]{1,0:T(8,128)(2,1)}, u32[]{:S(2)}) copy-start(bf16[128,512]{1,0:T(8,128)(2,1)} %g_any.3) | copy-start | bytes 393220
  2.7 24.9 %all-to-all-start = ((bf16[16,32,512]{2,1,0:T(8,128)(2,1)}), bf16[16,32,512]{2,1,0:T(8,128)(2,1)S(1)}, u32[]{:S(2)}, u32[]{:S(2)}) async-start(bf16[16,32,512]{2,1,0:T(8,128)(2,1)} %bitcast), calls=%async_computation | async-start | bytes 1048576 | tf_op jit(solution)/shard_map/all_to_all | solution.py:196
  12.2 6.9 %collective-permute-start = (bf16[128,512]{1,0:T(8,128)(2,1)S(1)}, bf16[128,512]{1,0:T(8,128)(2,1)S(1)}, u32[]{:S(2)}, u32[]{:S(2)}) collective-permute-start(bf16[128,512]{1,0:T(8,128)(2,1)S(1)} %get-tuple-element.15.input_ref), channel_id=1, source_target_pairs={{0,4},{4,0},{8,12},{12,8},{1,5},{5,1},{9,13},{13,9},{2,6},{6,2},{1... | collective-permute-start | bytes 393224 | tf_op jit(solution)/shard_map/ppermute | solution.py:200
  15.3 3.7 %collective-permute-start.1 = (bf16[128,512]{1,0:T(8,128)(2,1)S(1)}, bf16[128,512]{1,0:T(8,128)(2,1)S(1)}, u32[]{:S(2)}, u32[]{:S(2)}) collective-permute-start(bf16[128,512]{1,0:T(8,128)(2,1)S(1)} %get-tuple-element.16.layer_ref), channel_id=1, source_target_pairs={{0,1},{1,0},{2,3},{3,2},{4,5},{5,4},{6,7},{7,6},{8,9},{9,8},{10,11... | collective-permute-start | bytes 393224 | tf_op jit(solution)/shard_map/ppermute | solution.py:200
  27.8 8.9 %collective-permute-start.4 = (bf16[32,512]{1,0:T(8,128)(2,1)S(1)}, bf16[32,512]{1,0:T(8,128)(2,1)S(1)}, u32[]{:S(2)}, u32[]{:S(2)}) collective-permute-start(bf16[32,512]{1,0:T(8,128)(2,1)S(1)} %get-tuple-element.19.half_ref), channel_id=1, source_target_pairs={{0,448},{448,0},{16,464},{464,16},{32,480},{480,32},{48,496},{496,... | collective-permute-start | bytes 98312 | tf_op jit(solution)/shard_map/ppermute | solution.py:262
  37.6 21.5 %all-to-all-start.1 = ((bf16[16,32,512]{2,1,0:T(8,128)(2,1)}), bf16[16,32,512]{2,1,0:T(8,128)(2,1)S(1)}, u32[]{:S(2)}, u32[]{:S(2)}) async-start(bf16[16,32,512]{2,1,0:T(8,128)(2,1)} %bitcast.3), calls=%async_computation.1 | async-start | bytes 1048576 | tf_op jit(solution)/shard_map/all_to_all | solution.py:196
  41.2 8.4 %collective-permute-start.2 = (bf16[128,512]{1,0:T(8,128)(2,1)S(1)}, bf16[128,512]{1,0:T(8,128)(2,1)S(1)}, u32[]{:S(2)}, u32[]{:S(2)}) collective-permute-start(bf16[128,512]{1,0:T(8,128)(2,1)S(1)} %get-tuple-element.17.input_ref), channel_id=1, source_target_pairs={{0,8},{4,12},{8,0},{12,4},{1,9},{5,13},{9,1},{13,5},{2,10},{6,14},... | collective-permute-start | bytes 393224 | tf_op jit(solution)/shard_map/ppermute | solution.py:200
  50.2 15.7 %collective-permute-start.3 = (bf16[128,512]{1,0:T(8,128)(2,1)S(1)}, bf16[128,512]{1,0:T(8,128)(2,1)S(1)}, u32[]{:S(2)}, u32[]{:S(2)}) collective-permute-start(bf16[128,512]{1,0:T(8,128)(2,1)S(1)} %get-tuple-element.18.layer_ref), channel_id=1, source_target_pairs={{0,2},{1,3},{2,0},{3,1},{4,6},{5,7},{6,4},{7,5},{8,10},{9,11},{10,... | collective-permute-start | bytes 393224 | tf_op jit(solution)/shard_map/ppermute | solution.py:200

commit v7 on v5

--- a/solution.py
+++ b/solution.py
@@ -67,13 +67,8 @@
 
 
 def staged(units):
-    waiting = None
     for product, use in units:
-        result = product()
-        if waiting is not None:
-            waiting[0](waiting[1])
-        waiting = (use, result)
-    waiting[0](waiting[1])
+        use(product())
 
 
 def newton_kernel(slab, place_ref, block_ref, left_ref, right_ref, wide, n_low, c_low, h_low, row):
@@ -98,8 +93,9 @@
             ref[top, low] = values[half:].T
 
     def gram(side, cut):
-        left, right = (block_ref, turned) if side == 0 else (turned, block_ref)
-        return mm(left[cut.start :, :], right[:, cut])
+        if side == 0:
+            return mm(block_ref[cut.start :, :], block_ref[cut, :], ((1,), (1,)))
+        return mm(turned[cut.start :, :], block_ref[:, cut])
 
     def keep_gram(side, cut, product):
         corner = jnp.where(on_diagonal, product[:half] + 1e-06, product[:half])

time: 64.7 us -> 64.6 us (level)
  no operation moved by 1% of the time
where the time goes in v7:
time: 64.6 us; the launch traced here: 64.2 us
  starting transfers between devices  31.8 us (49%)
  waiting for transfers between devices  19.6 us (30%)
  Pallas kernels  12 us (19%)
  between operations  0.76 us (1%)
    all_to_all x2, starting transfers between devices, exchange(): return lax.all_to_all(values, axis, 0, 0, tiled=True)  18.8 us
    ppermute x4, starting transfers between devices, partner(): return lax.ppermute(values, axis, [(i, i ^ flip) for i in range(4)])  13 us
    ppermute x4, waiting for transfers between devices, partner(): return lax.ppermute(values, axis, [(i, i ^ flip) for i in range(4)])  10.1 us
    all_to_all x2, waiting for transfers between devices, exchange(): return lax.all_to_all(values, axis, 0, 0, tiled=True)  9.49 us
    pallas_call x1, Pallas kernels, shards(): pl.pallas_call(functools.partial(newton_kernel, slab), out_shape=[pltpu.V...  6.83 us
    pallas_call x1, Pallas kernels, shards(): pl.pallas_call(functools.partial(grad_kernel, tokens * groups), out_shape...  2.09 us
  transfers between devices with their start and end apart: 6, of which 4 were waited for; matrix products, arithmetic and copies ran while one was open for 0% of the time, Pallas kernels for 13%

profile of v7, /device:TPU:6, one launch (start us, length us, event | category | flops | bytes accessed | tf_op | source)
XLA Modules:
  0.0 64.2 jit_solution(1511973982682192742)
XLA Ops:
  0.6 2.1 %grad_part.1.after_any = bf16[512,512]{1,0:T(8,128)(2,1)} custom-call(bf16[128,512]{1,0:T(8,128)(2,1)} %x_any.3, bf16[128,512]{1,0:T(8,128)(2,1)} %g_any.3), custom_call_target="tpu_custom_call" | custom-call | flops 67108864 | bytes 1048576 | tf_op jit(solution)/shard_map/grad_part/pallas_call | solution.py:196
  2.7 0.0 copy-start
  2.7 0.0 copy-start.1
  2.8 0.0 copy-start.2
  2.8 13.9 %all-to-all-start = ((bf16[32,16,512]{2,1,0:T(8,128)(2,1)}), bf16[32,16,512]{2,1,0:T(8,128)(2,1)S(1)}, u32[]{:S(2)}, u32[]{:S(2)}) async-start(bf16[32,16,512]{2,1,0:T(8,128)(2,1)} %bitcast), calls=%async_computation | async-start | bytes 1048576 | tf_op jit(solution)/shard_map/all_to_all | solution.py:179
  16.7 0.0 copy-done
  16.7 0.0 copy-done.1
  16.7 0.0 copy-done.2
  16.7 0.8 %outputs_part.1 = (bf16[128,512]{1,0:T(8,128)(2,1)S(1)}, bf16[128,512]{1,0:T(8,128)(2,1)S(1)}) custom-call(bf16[128,512]{1,0:T(8,128)(2,1)S(1)} %copy-done.1, bf16[128,512]{1,0:T(8,128)(2,1)S(1)} %copy-done.2, bf16[512,512]{1,0:T(8,128)(2,1)S(1)} %copy-done, bf16[512,512]{1,0:T(8,128)(2,1)} %grad_part.1.after_any), custom_call_target="tpu_custom_call" | custom-call | flops 134217728 | bytes 1048576 | tf_op jit(solution)/shard_map/outputs_part/pallas_call | solution.py:207
  17.5 1.9 %collective-permute-start.1 = (bf16[128,512]{1,0:T(8,128)(2,1)S(1)}, bf16[128,512]{1,0:T(8,128)(2,1)S(1)}, u32[]{:S(2)}, u32[]{:S(2)}) collective-permute-start(bf16[128,512]{1,0:T(8,128)(2,1)S(1)} %get-tuple-element.16.layer_ref), channel_id=1, source_target_pairs={{0,1},{1,0},{2,3},{3,2},{4,5},{5,4},{6,7},{7,6},{8,9},{9,8},{10,11... | collective-permute-start | bytes 393224 | tf_op jit(solution)/shard_map/ppermute | solution.py:183
  19.4 2.7 %collective-permute-start = (bf16[128,512]{1,0:T(8,128)(2,1)S(1)}, bf16[128,512]{1,0:T(8,128)(2,1)S(1)}, u32[]{:S(2)}, u32[]{:S(2)}) collective-permute-start(bf16[128,512]{1,0:T(8,128)(2,1)S(1)} %get-tuple-element.15.input_ref), channel_id=1, source_target_pairs={{0,4},{4,0},{8,12},{12,8},{1,5},{5,1},{9,13},{13,9},{2,6},{6,2},{1... | collective-permute-start | bytes 393224 | tf_op jit(solution)/shard_map/ppermute | solution.py:183
  22.2 0.0 collective-permute-done.1.layer_any.layer_other
  22.2 5.0 %collective-permute-done.input_other = bf16[128,512]{1,0:T(8,128)(2,1)S(1)} collective-permute-done((bf16[128,512]{1,0:T(8,128)(2,1)S(1)}, bf16[128,512]{1,0:T(8,128)(2,1)S(1)}, u32[]{:S(2)}, u32[]{:S(2)}) %collective-permute-start) | collective-permute-done | bytes 131104 | tf_op jit(solution)/shard_map/ppermute | solution.py:183
  27.2 6.6 %all-to-all-done = bf16[32,16,512]{2,1,0:T(8,128)(2,1)S(1)} async-done(((bf16[32,16,512]{2,1,0:T(8,128)(2,1)}), bf16[32,16,512]{2,1,0:T(8,128)(2,1)S(1)}, u32[]{:S(2)}, u32[]{:S(2)}) %all-to-all-start) | async-done | bytes 524320 | tf_op jit(solution)/shard_map/all_to_all | solution.py:179
  33.9 0.9 %sums.1 = (bf16[512,512]{1,0:T(8,128)(2,1)}, bf16[128,512]{1,0:T(8,128)(2,1)S(1)}) custom-call(bf16[512,512]{1,0:T(8,128)(2,1)S(1)} %bitcast.5, bf16[128,512]{1,0:T(8,128)(2,1)S(1)} %get-tuple-element.15.input_ref, bf16[128,512]{1,0:T(8,128)(2,1)S(1)} %collective-permute-done.input_other, bf16[128,512]{1,0:T(8,128)(2,1)S(1)} %collective-permute-done.1.layer_any.layer_other), custom_call_target="tpu_custom_call" | custom-call | flops 262144 | bytes 1048576 | tf_op jit(solution)/shard_map/sums/pallas_call | solution.py:223
  34.8 4.9 %all-to-all-start.1 = ((bf16[32,16,512]{2,1,0:T(8,128)(2,1)}), bf16[32,16,512]{2,1,0:T(8,128)(2,1)S(1)}, u32[]{:S(2)}, u32[]{:S(2)}) async-start(bf16[32,16,512]{2,1,0:T(8,128)(2,1)} %bitcast.3), calls=%async_computation.1 | async-start | bytes 1048576 | tf_op jit(solution)/shard_map/all_to_all | solution.py:179
  39.7 3.3 %collective-permute-start.2 = (bf16[128,512]{1,0:T(8,128)(2,1)S(1)}, bf16[128,512]{1,0:T(8,128)(2,1)S(1)}, u32[]{:S(2)}, u32[]{:S(2)}) collective-permute-start(bf16[128,512]{1,0:T(8,128)(2,1)S(1)} %get-tuple-element.17.input_ref), channel_id=1, source_target_pairs={{0,8},{4,12},{8,0},{12,4},{1,9},{5,13},{9,1},{13,5},{2,10},{6,14},... | collective-permute-start | bytes 393224 | tf_op jit(solution)/shard_map/ppermute | solution.py:183
  43.0 5.0 %collective-permute-done.2.input_other = bf16[128,512]{1,0:T(8,128)(2,1)S(1)} collective-permute-done((bf16[128,512]{1,0:T(8,128)(2,1)S(1)}, bf16[128,512]{1,0:T(8,128)(2,1)S(1)}, u32[]{:S(2)}, u32[]{:S(2)}) %collective-permute-start.2) | collective-permute-done | bytes 131104 | tf_op jit(solution)/shard_map/ppermute | solution.py:183
  48.1 0.7 %middle.1 = (bf16[128,512]{1,0:T(8,128)(2,1)}, bf16[128,512]{1,0:T(8,128)(2,1)S(1)}) custom-call(bf16[128,512]{1,0:T(8,128)(2,1)S(1)} %get-tuple-element.17.input_ref, bf16[128,512]{1,0:T(8,128)(2,1)S(1)} %collective-permute-done.2.input_other, bf16[128,512]{1,0:T(8,128)(2,1)S(1)} %get-tuple-element.16.layer_ref, ...), custom_call_target="tpu_custom_call" | custom-call | bytes 524288 | tf_op jit(solution)/shard_map/middle/pallas_call | solution.py:234
  48.8 5.0 %collective-permute-start.3 = (bf16[128,512]{1,0:T(8,128)(2,1)S(1)}, bf16[128,512]{1,0:T(8,128)(2,1)S(1)}, u32[]{:S(2)}, u32[]{:S(2)}) collective-permute-start(bf16[128,512]{1,0:T(8,128)(2,1)S(1)} %get-tuple-element.18.layer_ref), channel_id=1, source_target_pairs={{0,2},{1,3},{2,0},{3,1},{4,6},{5,7},{6,4},{7,5},{8,10},{9,11},{10,... | collective-permute-start | bytes 393224 | tf_op jit(solution)/shard_map/ppermute | solution.py:183
  53.8 2.8 %all-to-all-done.1 = bf16[32,16,512]{2,1,0:T(8,128)(2,1)S(1)} async-done(((bf16[32,16,512]{2,1,0:T(8,128)(2,1)}), bf16[32,16,512]{2,1,0:T(8,128)(2,1)S(1)}, u32[]{:S(2)}, u32[]{:S(2)}) %all-to-all-start.1) | async-done | bytes 524320 | tf_op jit(solution)/shard_map/all_to_all | solution.py:179
  56.6 6.8 %newton.1 = (f32[1,16,512]{2,1,0:T(8,128)S(1)}, f32[1,16,512]{2,1,0:T(8,128)S(1)}) custom-call(s32[1]{0:T(128)} %bitcast.2.place_ref, bf16[512,512]{1,0:T(8,128)(2,1)S(1)} %bitcast.6), custom_call_target="tpu_custom_call" | custom-call | bytes 65536 | tf_op jit(solution)/shard_map/newton/pallas_call | solution.py:246
  63.5 0.0 collective-permute-done.3.layer_other
  63.5 0.7 %last.1 = (bf16[128,512]{1,0:T(8,128)(2,1)}, f32[1,16,512]{2,1,0:T(8,128)}, f32[1,16,512]{2,1,0:T(8,128)}) custom-call(bf16[128,512]{1,0:T(8,128)(2,1)S(1)} %get-tuple-element.18.layer_ref, bf16[128,512]{1,0:T(8,128)(2,1)S(1)} %collective-permute-done.3.layer_other, f32[1,16,512]{2,1,0:T(8,128)S(1)} %get-tuple-element.20.left_ref, ...), custom_call_target="tpu_custom_call" | custom-call | bytes 262144 | tf_op jit(solution)/shard_map/last/pallas_call | solution.py:262
Async XLA Ops:
  2.7 13.9 %copy-start = (bf16[512,512]{1,0:T(8,128)(2,1)S(1)}, bf16[512,512]{1,0:T(8,128)(2,1)}, u32[]{:S(2)}) copy-start(bf16[512,512]{1,0:T(8,128)(2,1)} %w_any.1) | copy-start | bytes 1572868
  2.7 13.9 %copy-start.1 = (bf16[128,512]{1,0:T(8,128)(2,1)S(1)}, bf16[128,512]{1,0:T(8,128)(2,1)}, u32[]{:S(2)}) copy-start(bf16[128,512]{1,0:T(8,128)(2,1)} %x_any.3) | copy-start | bytes 393220
  2.8 13.9 %copy-start.2 = (bf16[128,512]{1,0:T(8,128)(2,1)S(1)}, bf16[128,512]{1,0:T(8,128)(2,1)}, u32[]{:S(2)}) copy-start(bf16[128,512]{1,0:T(8,128)(2,1)} %g_any.3) | copy-start | bytes 393220
  2.8 31.1 %all-to-all-start = ((bf16[32,16,512]{2,1,0:T(8,128)(2,1)}), bf16[32,16,512]{2,1,0:T(8,128)(2,1)S(1)}, u32[]{:S(2)}, u32[]{:S(2)}) async-start(bf16[32,16,512]{2,1,0:T(8,128)(2,1)} %bitcast), calls=%async_computation | async-start | bytes 1048576 | tf_op jit(solution)/shard_map/all_to_all | solution.py:179
  17.5 4.7 %collective-permute-start.1 = (bf16[128,512]{1,0:T(8,128)(2,1)S(1)}, bf16[128,512]{1,0:T(8,128)(2,1)S(1)}, u32[]{:S(2)}, u32[]{:S(2)}) collective-permute-start(bf16[128,512]{1,0:T(8,128)(2,1)S(1)} %get-tuple-element.16.layer_ref), channel_id=1, source_target_pairs={{0,1},{1,0},{2,3},{3,2},{4,5},{5,4},{6,7},{7,6},{8,9},{9,8},{10,11... | collective-permute-start | bytes 393224 | tf_op jit(solution)/shard_map/ppermute | solution.py:183
  19.4 7.8 %collective-permute-start = (bf16[128,512]{1,0:T(8,128)(2,1)S(1)}, bf16[128,512]{1,0:T(8,128)(2,1)S(1)}, u32[]{:S(2)}, u32[]{:S(2)}) collective-permute-start(bf16[128,512]{1,0:T(8,128)(2,1)S(1)} %get-tuple-element.15.input_ref), channel_id=1, source_target_pairs={{0,4},{4,0},{8,12},{12,8},{1,5},{5,1},{9,13},{13,9},{2,6},{6,2},{1... | collective-permute-start | bytes 393224 | tf_op jit(solution)/shard_map/ppermute | solution.py:183
  34.8 21.8 %all-to-all-start.1 = ((bf16[32,16,512]{2,1,0:T(8,128)(2,1)}), bf16[32,16,512]{2,1,0:T(8,128)(2,1)S(1)}, u32[]{:S(2)}, u32[]{:S(2)}) async-start(bf16[32,16,512]{2,1,0:T(8,128)(2,1)} %bitcast.3), calls=%async_computation.1 | async-start | bytes 1048576 | tf_op jit(solution)/shard_map/all_to_all | solution.py:179
  39.7 8.4 %collective-permute-start.2 = (bf16[128,512]{1,0:T(8,128)(2,1)S(1)}, bf16[128,512]{1,0:T(8,128)(2,1)S(1)}, u32[]{:S(2)}, u32[]{:S(2)}) collective-permute-start(bf16[128,512]{1,0:T(8,128)(2,1)S(1)} %get-tuple-element.17.input_ref), channel_id=1, source_target_pairs={{0,8},{4,12},{8,0},{12,4},{1,9},{5,13},{9,1},{13,5},{2,10},{6,14},... | collective-permute-start | bytes 393224 | tf_op jit(solution)/shard_map/ppermute | solution.py:183
  48.8 14.7 %collective-permute-start.3 = (bf16[128,512]{1,0:T(8,128)(2,1)S(1)}, bf16[128,512]{1,0:T(8,128)(2,1)S(1)}, u32[]{:S(2)}, u32[]{:S(2)}) collective-permute-start(bf16[128,512]{1,0:T(8,128)(2,1)S(1)} %get-tuple-element.18.layer_ref), channel_id=1, source_target_pairs={{0,2},{1,3},{2,0},{3,1},{4,6},{5,7},{6,4},{7,5},{8,10},{9,11},{10,... | collective-permute-start | bytes 393224 | tf_op jit(solution)/shard_map/ppermute | solution.py:183

commit v8 on v5

--- a/solution.py
+++ b/solution.py
@@ -28,17 +28,27 @@
         copy.wait()
 
 
-def grad_kernel(tokens_all, x_any, g_any, grad_ref, x_ref, g_ref, sems):
-    fetch((x_any, g_any), (x_ref, g_ref), sems)
+def products_kernel(
+    tokens_all, x_any, g_any, w_any, grad_ref, layer_ref, input_ref, x_ref, g_ref, w_ref, sems
+):
+    fetch((x_any, g_any, w_any), (x_ref, g_ref, w_ref), sems)
     grad = mm(x_ref[...], g_ref[...], ((0,), (0,)))
     grad_ref[...] = (grad * (1.0 / tokens_all)).astype(BF16)
+    layer_ref[...] = mm(x_ref[...], w_ref[...]).astype(BF16)
+    input_ref[...] = mm(g_ref[...], w_ref[...], ((1,), (1,))).astype(BF16)
+
+
+def hand_on_kernel(grad_ref, input_ref, layer_ref, after_ref, grad_out, input_out, layer_out):
+    grad_out[...] = grad_ref[...]
+    input_out[...] = input_ref[...]
+    layer_out[...] = layer_ref[...]
 
 
 def pair_sum(left_ref, right_ref):
     return (left_ref[...].astype(F32) + right_ref[...].astype(F32)).astype(BF16)
 
 
-def sum_kernel(copies, parts_ref, input_ref, input_other, layer_any, out_ref, input_sum):
+def sum_kernel(copies, parts_ref, input_ref, input_other, input_later, layer_any, out_ref, input_sum):
     slab = parts_ref.shape[0] // copies
     total = parts_ref[:slab, :].astype(F32)
     for k in range(1, copies):
@@ -46,13 +56,8 @@
     total = total.astype(BF16)
     for k in range(copies):
         out_ref[k * slab : (k + 1) * slab, :] = total
-    input_sum[...] = pair_sum(input_ref, input_other)
-
-
-def outputs_kernel(x_any, g_any, w_any, after_any, layer_ref, input_ref, x_ref, g_ref, w_ref, sems):
-    fetch((x_any, g_any, w_any), (x_ref, g_ref, w_ref), sems)
-    layer_ref[...] = mm(x_ref[...], w_ref[...]).astype(BF16)
-    input_ref[...] = mm(g_ref[...], w_ref[...], ((1,), (1,))).astype(BF16)
+    other = input_other[...].astype(F32) + input_later[...].astype(F32)
+    input_sum[...] = (input_ref[...].astype(F32) + other).astype(BF16)
 
 
 def middle_kernel(input_ref, input_other, layer_ref, layer_other, input_out, layer_sum):
@@ -187,6 +192,11 @@
     return lax.ppermute(values, axis, [(i, i ^ flip) for i in range(4)])
 
 
+def core_partner(values, core):
+    pairs = [(t * 4 + p, (t ^ 1) * 4 + p) for t in range(4) for p in (core, core + 2)]
+    return lax.ppermute(values, ("tensor", "precond"), pairs)
+
+
 def shards(x_in, grad_out, weight):
     extent = weight.shape[0]
     tokens = x_in.shape[0]
@@ -197,22 +207,11 @@
     whole = jax.ShapeDtypeStruct((tokens, extent), BF16)
     tokens_vmem = pltpu.VMEM((tokens, extent), BF16)
 
-    grad_part = pl.pallas_call(
-        functools.partial(grad_kernel, tokens * groups),
-        out_shape=block,
-        in_specs=[HBM, HBM],
-        out_specs=VMEM,
-        scratch_shapes=[tokens_vmem, tokens_vmem, pltpu.SemaphoreType.DMA((2,))],
-        compiler_params=limit(8),
-        cost_estimate=pl.CostEstimate(flops=2 * tokens * extent * extent, bytes_accessed=2**20, transcendentals=0),
-        name="grad_part",
-    )(in_hbm(x_in), in_hbm(grad_out))
-    received = exchange(grad_part, "dp")
-    layer_part, input_part = pl.pallas_call(
-        outputs_kernel,
-        out_shape=[whole, whole],
-        in_specs=[HBM, HBM, HBM, ANY],
-        out_specs=[VMEM, VMEM],
+    grad_near, layer_part, input_part = pl.pallas_call(
+        functools.partial(products_kernel, tokens * groups),
+        out_shape=[block, whole, whole],
+        in_specs=[HBM, HBM, HBM],
+        out_specs=[VMEM] * 3,
         scratch_shapes=[
             tokens_vmem,
             tokens_vmem,
@@ -220,19 +219,30 @@
             pltpu.SemaphoreType.DMA((3,)),
         ],
         compiler_params=limit(8),
-        cost_estimate=pl.CostEstimate(flops=4 * tokens * extent * extent, bytes_accessed=2**20, transcendentals=0),
-        name="outputs_part",
-    )(x_in, grad_out, weight, grad_part)
+        cost_estimate=pl.CostEstimate(flops=6 * tokens * extent * extent, bytes_accessed=2**20, transcendentals=0),
+        name="products",
+    )(in_hbm(x_in), in_hbm(grad_out), in_hbm(weight))
+    input_other = core_partner(input_part, 0)
+    grad_part, later_part, layer_part = pl.pallas_call(
+        hand_on_kernel,
+        out_shape=[jax.ShapeDtypeStruct((extent, extent), BF16), whole, whole],
+        in_specs=[VMEM] * 4,
+        out_specs=[VMEM] * 3,
+        compiler_params=limit(8),
+        cost_estimate=pl.CostEstimate(flops=0, bytes_accessed=2**20, transcendentals=0),
+        name="hand_on",
+    )(grad_near, input_part, layer_part, input_other)
+    received = exchange(grad_part, "dp")
     layer_near = partner(layer_part, "precond", 1)
     copies, input_sum = pl.pallas_call(
         functools.partial(sum_kernel, groups),
         out_shape=[block, whole],
-        in_specs=[VMEM, VMEM, VMEM, ANY],
+        in_specs=[VMEM, VMEM, VMEM, VMEM, ANY],
         out_specs=[VMEM] * 2,
         compiler_params=limit(8),
         cost_estimate=pl.CostEstimate(flops=extent * extent, bytes_accessed=2**20, transcendentals=0),
         name="sums",
-    )(received, input_part, partner(input_part, "tensor", 1), layer_near)
+    )(received, input_part, input_other, core_partner(later_part, 1), layer_near)
     grad_low = exchange(copies, "dp")
 
     grad_in, layer_sum = pl.pallas_call(

time: 64.7 us -> 68.4 us (1.057)
  waiting for transfers between devices: 19.6 us -> 24 us
    all_to_all x2, waiting for transfers between devices: 9.49 us -> 13.8 us  [exchange(): return lax.all_to_all(values, axis, 0, 0, tiled=True)]
    ppermute x0 -> x2, waiting for transfers between devices: none -> 4.12 us  [core_partner(): return lax.ppermute(values, ('tensor', 'precond'), pairs)]
    ppermute x4 -> x3, waiting for transfers between devices: 10.1 us -> 6.02 us  [partner(): return lax.ppermute(values, axis, [(i, i ^ flip) for i in range(4)])]
    ppermute x0 -> x2, starting transfers between devices: none -> 3.41 us  [core_partner(): return lax.ppermute(values, ('tensor', 'precond'), pairs)]
    ppermute x4 -> x3, starting transfers between devices: 13 us -> 10.3 us  [partner(): return lax.ppermute(values, axis, [(i, i ^ flip) for i in range(4)])]
    all_to_all x2, starting transfers between devices: 18.8 us -> 17.8 us  [exchange(): return lax.all_to_all(values, axis, 0, 0, tiled=True)]
  transfers between devices with their start and end apart: 6 -> 7, of which waited for: 4 -> 5; matrix products, arithmetic and copies ran while one was open for 0% -> 0% of each run, Pallas kernels for 13% -> 11%
where the time goes in v8:
time: 68.4 us; the launch traced here: 67.9 us
  starting transfers between devices  31.5 us (46%)
  waiting for transfers between devices  24 us (35%)
  Pallas kernels  11.8 us (17%)
  between operations  0.71 us (1%)
    all_to_all x2, starting transfers between devices, exchange(): return lax.all_to_all(values, axis, 0, 0, tiled=True)  17.8 us
    all_to_all x2, waiting for transfers between devices, exchange(): return lax.all_to_all(values, axis, 0, 0, tiled=True)  13.8 us
    ppermute x3, starting transfers between devices, partner(): return lax.ppermute(values, axis, [(i, i ^ flip) for i in range(4)])  10.3 us
    pallas_call x1, Pallas kernels, shards(): pl.pallas_call(functools.partial(newton_kernel, slab), out_shape=[pltpu.V...  6.86 us
    ppermute x3, waiting for transfers between devices, partner(): return lax.ppermute(values, axis, [(i, i ^ flip) for i in range(4)])  6.02 us
    ppermute x2, waiting for transfers between devices, core_partner(): return lax.ppermute(values, ('tensor', 'precond'), pairs)  4.12 us
    ppermute x2, starting transfers between devices, core_partner(): return lax.ppermute(values, ('tensor', 'precond'), pairs)  3.41 us
    pallas_call x1, Pallas kernels, shards(): pl.pallas_call(functools.partial(products_kernel, tokens * groups), out_s...  1.76 us
  transfers between devices with their start and end apart: 7, of which 5 were waited for; matrix products, arithmetic and copies ran while one was open for 0% of the time, Pallas kernels for 11%

profile of v8, /device:TPU:6, one launch (start us, length us, event | category | flops | bytes accessed | tf_op | source)
XLA Modules:
  0.0 67.9 jit_solution(17334354937609449075)
XLA Ops:
  0.6 1.8 %products.1 = (bf16[512,512]{1,0:T(8,128)(2,1)S(1)}, bf16[128,512]{1,0:T(8,128)(2,1)S(1)}, bf16[128,512]{1,0:T(8,128)(2,1)S(1)}) custom-call(bf16[128,512]{1,0:T(8,128)(2,1)} %x_any.1, bf16[128,512]{1,0:T(8,128)(2,1)} %g_any.1, bf16[512,512]{1,0:T(8,128)(2,1)} %w_any.1), custom_call_target="tpu_custom_call" | custom-call | flops 201326592 | bytes 1048576 | tf_op jit(solution)/shard_map/products/pallas_call | solution.py:210
  2.4 2.7 %collective-permute-start = (bf16[128,512]{1,0:T(8,128)(2,1)S(1)}, bf16[128,512]{1,0:T(8,128)(2,1)S(1)}, u32[]{:S(2)}, u32[]{:S(2)}) collective-permute-start(bf16[128,512]{1,0:T(8,128)(2,1)S(1)} %get-tuple-element.20.input_ref), channel_id=1, source_target_pairs={{0,4},{2,6},{4,0},{6,2},{8,12},{10,14},{12,8},{14,10},{16,20},{18,... | collective-permute-start | bytes 393224 | tf_op jit(solution)/shard_map/ppermute | solution.py:197
  5.1 4.1 %collective-permute-done.after_ref.input_other = bf16[128,512]{1,0:T(8,128)(2,1)S(1)} collective-permute-done((bf16[128,512]{1,0:T(8,128)(2,1)S(1)}, bf16[128,512]{1,0:T(8,128)(2,1)S(1)}, u32[]{:S(2)}, u32[]{:S(2)}) %collective-permute-start) | collective-permute-done | bytes 131104 | tf_op jit(solution)/shard_map/ppermute | solution.py:197
  9.3 0.8 %hand_on.1 = (bf16[512,512]{1,0:T(8,128)(2,1)}, bf16[128,512]{1,0:T(8,128)(2,1)S(1)}, bf16[128,512]{1,0:T(8,128)(2,1)S(1)}) custom-call(bf16[512,512]{1,0:T(8,128)(2,1)S(1)} %get-tuple-element.19.grad_ref, bf16[128,512]{1,0:T(8,128)(2,1)S(1)} %get-tuple-element.20.input_ref, bf16[128,512]{1,0:T(8,128)(2,1)S(1)} %get-tuple-element.21.layer_ref, ...), custom_call_target="tpu_custom_call" | custom-call | bytes 1048576 | tf_op jit(solution)/shard_map/hand_on/pallas_call | solution.py:226
  10.1 13.7 %all-to-all-start = ((bf16[32,16,512]{2,1,0:T(8,128)(2,1)}), bf16[32,16,512]{2,1,0:T(8,128)(2,1)S(1)}, u32[]{:S(2)}, u32[]{:S(2)}) async-start(bf16[32,16,512]{2,1,0:T(8,128)(2,1)} %bitcast), calls=%async_computation | async-start | bytes 1048576 | tf_op jit(solution)/shard_map/all_to_all | solution.py:188
  23.9 1.9 %collective-permute-start.2 = (bf16[128,512]{1,0:T(8,128)(2,1)S(1)}, bf16[128,512]{1,0:T(8,128)(2,1)S(1)}, u32[]{:S(2)}, u32[]{:S(2)}) collective-permute-start(bf16[128,512]{1,0:T(8,128)(2,1)S(1)} %get-tuple-element.24.layer_ref), channel_id=1, source_target_pairs={{0,1},{1,0},{2,3},{3,2},{4,5},{5,4},{6,7},{7,6},{8,9},{9,8},{10,11... | collective-permute-start | bytes 393224 | tf_op jit(solution)/shard_map/ppermute | solution.py:192
  25.8 0.7 collective-permute-start.1
  26.5 0.6 collective-permute-done.2.layer_any.layer_other
  27.1 0.0 collective-permute-done.1.input_later
  27.1 10.7 %all-to-all-done = bf16[32,16,512]{2,1,0:T(8,128)(2,1)S(1)} async-done(((bf16[32,16,512]{2,1,0:T(8,128)(2,1)}), bf16[32,16,512]{2,1,0:T(8,128)(2,1)S(1)}, u32[]{:S(2)}, u32[]{:S(2)}) %all-to-all-start) | async-done | bytes 524320 | tf_op jit(solution)/shard_map/all_to_all | solution.py:188
  37.8 0.9 %sums.1 = (bf16[512,512]{1,0:T(8,128)(2,1)}, bf16[128,512]{1,0:T(8,128)(2,1)S(1)}) custom-call(bf16[512,512]{1,0:T(8,128)(2,1)S(1)} %bitcast.6, bf16[128,512]{1,0:T(8,128)(2,1)S(1)} %get-tuple-element.20.input_ref, bf16[128,512]{1,0:T(8,128)(2,1)S(1)} %collective-permute-done.after_ref.input_other, bf16[128,512]{1,0:T(8,128)(2,1)S(1)} %collective-permute-done.1.input_later, ...), custom_call_target="tpu_custom_call" | custom-call | flops 262144 | bytes 1048576 | tf_op jit(solution)/shard_map/sums/pallas_call | solution.py:237
  38.7 4.1 %all-to-all-start.1 = ((bf16[32,16,512]{2,1,0:T(8,128)(2,1)}), bf16[32,16,512]{2,1,0:T(8,128)(2,1)S(1)}, u32[]{:S(2)}, u32[]{:S(2)}) async-start(bf16[32,16,512]{2,1,0:T(8,128)(2,1)} %bitcast.3), calls=%async_computation.1 | async-start | bytes 1048576 | tf_op jit(solution)/shard_map/all_to_all | solution.py:188
  42.8 3.3 %collective-permute-start.3 = (bf16[128,512]{1,0:T(8,128)(2,1)S(1)}, bf16[128,512]{1,0:T(8,128)(2,1)S(1)}, u32[]{:S(2)}, u32[]{:S(2)}) collective-permute-start(bf16[128,512]{1,0:T(8,128)(2,1)S(1)} %get-tuple-element.25.input_ref), channel_id=1, source_target_pairs={{0,8},{4,12},{8,0},{12,4},{1,9},{5,13},{9,1},{13,5},{2,10},{6,14},... | collective-permute-start | bytes 393224 | tf_op jit(solution)/shard_map/ppermute | solution.py:192
  46.1 5.4 %collective-permute-done.3.input_other = bf16[128,512]{1,0:T(8,128)(2,1)S(1)} collective-permute-done((bf16[128,512]{1,0:T(8,128)(2,1)S(1)}, bf16[128,512]{1,0:T(8,128)(2,1)S(1)}, u32[]{:S(2)}, u32[]{:S(2)}) %collective-permute-start.3) | collective-permute-done | bytes 131104 | tf_op jit(solution)/shard_map/ppermute | solution.py:192
  51.5 0.7 %middle.1 = (bf16[128,512]{1,0:T(8,128)(2,1)}, bf16[128,512]{1,0:T(8,128)(2,1)S(1)}) custom-call(bf16[128,512]{1,0:T(8,128)(2,1)S(1)} %get-tuple-element.25.input_ref, bf16[128,512]{1,0:T(8,128)(2,1)S(1)} %collective-permute-done.3.input_other, bf16[128,512]{1,0:T(8,128)(2,1)S(1)} %get-tuple-element.24.layer_ref, ...), custom_call_target="tpu_custom_call" | custom-call | bytes 524288 | tf_op jit(solution)/shard_map/middle/pallas_call | solution.py:248
  52.2 5.0 %collective-permute-start.4 = (bf16[128,512]{1,0:T(8,128)(2,1)S(1)}, bf16[128,512]{1,0:T(8,128)(2,1)S(1)}, u32[]{:S(2)}, u32[]{:S(2)}) collective-permute-start(bf16[128,512]{1,0:T(8,128)(2,1)S(1)} %get-tuple-element.26.layer_ref), channel_id=1, source_target_pairs={{0,2},{1,3},{2,0},{3,1},{4,6},{5,7},{6,4},{7,5},{8,10},{9,11},{10,... | collective-permute-start | bytes 393224 | tf_op jit(solution)/shard_map/ppermute | solution.py:192
  57.2 3.1 %all-to-all-done.1 = bf16[32,16,512]{2,1,0:T(8,128)(2,1)S(1)} async-done(((bf16[32,16,512]{2,1,0:T(8,128)(2,1)}), bf16[32,16,512]{2,1,0:T(8,128)(2,1)S(1)}, u32[]{:S(2)}, u32[]{:S(2)}) %all-to-all-start.1) | async-done | bytes 524320 | tf_op jit(solution)/shard_map/all_to_all | solution.py:188
  60.4 6.9 %newton.1 = (f32[1,16,512]{2,1,0:T(8,128)S(1)}, f32[1,16,512]{2,1,0:T(8,128)S(1)}) custom-call(s32[1]{0:T(128)} %bitcast.2.place_ref, bf16[512,512]{1,0:T(8,128)(2,1)S(1)} %bitcast.5), custom_call_target="tpu_custom_call" | custom-call | bytes 65536 | tf_op jit(solution)/shard_map/newton/pallas_call | solution.py:260
  67.2 0.0 collective-permute-done.4.layer_other
  67.3 0.7 %last.1 = (bf16[128,512]{1,0:T(8,128)(2,1)}, f32[1,16,512]{2,1,0:T(8,128)}, f32[1,16,512]{2,1,0:T(8,128)}) custom-call(bf16[128,512]{1,0:T(8,128)(2,1)S(1)} %get-tuple-element.26.layer_ref, bf16[128,512]{1,0:T(8,128)(2,1)S(1)} %collective-permute-done.4.layer_other, f32[1,16,512]{2,1,0:T(8,128)S(1)} %get-tuple-element.28.left_ref, ...), custom_call_target="tpu_custom_call" | custom-call | bytes 262144 | tf_op jit(solution)/shard_map/last/pallas_call | solution.py:276
Async XLA Ops:
  2.4 6.9 %collective-permute-start = (bf16[128,512]{1,0:T(8,128)(2,1)S(1)}, bf16[128,512]{1,0:T(8,128)(2,1)S(1)}, u32[]{:S(2)}, u32[]{:S(2)}) collective-permute-start(bf16[128,512]{1,0:T(8,128)(2,1)S(1)} %get-tuple-element.20.input_ref), channel_id=1, source_target_pairs={{0,4},{2,6},{4,0},{6,2},{8,12},{10,14},{12,8},{14,10},{16,20},{18,... | collective-permute-start | bytes 393224 | tf_op jit(solution)/shard_map/ppermute | solution.py:197
  10.1 27.7 %all-to-all-start = ((bf16[32,16,512]{2,1,0:T(8,128)(2,1)}), bf16[32,16,512]{2,1,0:T(8,128)(2,1)S(1)}, u32[]{:S(2)}, u32[]{:S(2)}) async-start(bf16[32,16,512]{2,1,0:T(8,128)(2,1)} %bitcast), calls=%async_computation | async-start | bytes 1048576 | tf_op jit(solution)/shard_map/all_to_all | solution.py:188
  23.9 3.2 %collective-permute-start.2 = (bf16[128,512]{1,0:T(8,128)(2,1)S(1)}, bf16[128,512]{1,0:T(8,128)(2,1)S(1)}, u32[]{:S(2)}, u32[]{:S(2)}) collective-permute-start(bf16[128,512]{1,0:T(8,128)(2,1)S(1)} %get-tuple-element.24.layer_ref), channel_id=1, source_target_pairs={{0,1},{1,0},{2,3},{3,2},{4,5},{5,4},{6,7},{7,6},{8,9},{9,8},{10,11... | collective-permute-start | bytes 393224 | tf_op jit(solution)/shard_map/ppermute | solution.py:192
  25.8 1.3 %collective-permute-start.1 = (bf16[128,512]{1,0:T(8,128)(2,1)S(1)}, bf16[128,512]{1,0:T(8,128)(2,1)S(1)}, u32[]{:S(2)}, u32[]{:S(2)}) collective-permute-start(bf16[128,512]{1,0:T(8,128)(2,1)S(1)} %get-tuple-element.23), channel_id=1, source_target_pairs={{1,5},{3,7},{5,1},{7,3},{9,13},{11,15},{13,9},{15,11},{17,21},{19,... | collective-permute-start | bytes 393224 | tf_op jit(solution)/shard_map/ppermute | solution.py:197
  38.7 21.6 %all-to-all-start.1 = ((bf16[32,16,512]{2,1,0:T(8,128)(2,1)}), bf16[32,16,512]{2,1,0:T(8,128)(2,1)S(1)}, u32[]{:S(2)}, u32[]{:S(2)}) async-start(bf16[32,16,512]{2,1,0:T(8,128)(2,1)} %bitcast.3), calls=%async_computation.1 | async-start | bytes 1048576 | tf_op jit(solution)/shard_map/all_to_all | solution.py:188
  42.8 8.7 %collective-permute-start.3 = (bf16[128,512]{1,0:T(8,128)(2,1)S(1)}, bf16[128,512]{1,0:T(8,128)(2,1)S(1)}, u32[]{:S(2)}, u32[]{:S(2)}) collective-permute-start(bf16[128,512]{1,0:T(8,128)(2,1)S(1)} %get-tuple-element.25.input_ref), channel_id=1, source_target_pairs={{0,8},{4,12},{8,0},{12,4},{1,9},{5,13},{9,1},{13,5},{2,10},{6,14},... | collective-permute-start | bytes 393224 | tf_op jit(solution)/shard_map/ppermute | solution.py:192
  52.2 15.0 %collective-permute-start.4 = (bf16[128,512]{1,0:T(8,128)(2,1)S(1)}, bf16[128,512]{1,0:T(8,128)(2,1)S(1)}, u32[]{:S(2)}, u32[]{:S(2)}) collective-permute-start(bf16[128,512]{1,0:T(8,128)(2,1)S(1)} %get-tuple-element.26.layer_ref), channel_id=1, source_target_pairs={{0,2},{1,3},{2,0},{3,1},{4,6},{5,7},{6,4},{7,5},{8,10},{9,11},{10,... | collective-permute-start | bytes 393224 | tf_op jit(solution)/shard_map/ppermute | solution.py:192

commit v9 on v5

--- a/solution.py
+++ b/solution.py
@@ -28,25 +28,52 @@
         copy.wait()
 
 
-def grad_kernel(tokens_all, x_any, g_any, grad_ref, x_ref, g_ref, sems):
-    fetch((x_any, g_any), (x_ref, g_ref), sems)
-    grad = mm(x_ref[...], g_ref[...], ((0,), (0,)))
-    grad_ref[...] = (grad * (1.0 / tokens_all)).astype(BF16)
+def grad_kernel(tokens_all, x_any, g_any, grad_any, x_ref, g_ref, grad_ref, sems, out_sems):
+    rows_in = x_ref.shape[0] // 4
+    copies = []
+    for source, target in ((x_any, x_ref), (g_any, g_ref)):
+        for k in range(4):
+            rows = slice(k * rows_in, (k + 1) * rows_in)
+            copies.append(pltpu.make_async_copy(source.at[rows, :], target.at[rows, :], sems.at[len(copies)]))
+    for copy in copies:
+        copy.start()
+    for copy in copies:
+        copy.wait()
+    outs = []
+    chunk = grad_ref.shape[0] // 4
+    for k in range(4):
+        grad = mm(x_ref[:, k * chunk : (k + 1) * chunk], g_ref[...], ((0,), (0,)))
+        grad_ref[k * chunk : (k + 1) * chunk, :] = (grad * (1.0 / tokens_all)).astype(BF16)
+        for start in (k * chunk, k * chunk + chunk // 2):
+            rows = slice(start, start + chunk // 2)
+            outs.append(pltpu.make_async_copy(grad_ref.at[rows, :], grad_any.at[rows, :], out_sems.at[len(outs)]))
+            outs[-1].start()
+    for copy in outs:
+        copy.wait()
 
 
 def pair_sum(left_ref, right_ref):
     return (left_ref[...].astype(F32) + right_ref[...].astype(F32)).astype(BF16)
 
 
-def sum_kernel(copies, parts_ref, input_ref, input_other, layer_any, out_ref, input_sum):
-    slab = parts_ref.shape[0] // copies
+def sum_kernel(groups, parts_ref, input_ref, input_other, layer_any, out_any, input_sum, total_ref, sems):
+    slab = parts_ref.shape[0] // groups
     total = parts_ref[:slab, :].astype(F32)
-    for k in range(1, copies):
+    for k in range(1, groups):
         total = total + parts_ref[k * slab : (k + 1) * slab, :].astype(F32)
     total = total.astype(BF16)
-    for k in range(copies):
-        out_ref[k * slab : (k + 1) * slab, :] = total
+    block = total_ref.shape[0]
+    for k in range(block // slab):
+        total_ref[k * slab : (k + 1) * slab, :] = total
+    copies = [
+        pltpu.make_async_copy(total_ref, out_any.at[k * block : (k + 1) * block, :], sems.at[k])
+        for k in range(out_any.shape[0] // block)
+    ]
+    for copy in copies:
+        copy.start()
     input_sum[...] = pair_sum(input_ref, input_other)
+    for copy in copies:
+        copy.wait()
 
 
 def outputs_kernel(x_any, g_any, w_any, after_any, layer_ref, input_ref, x_ref, g_ref, w_ref, sems):
@@ -193,16 +220,22 @@
     groups = lax.axis_size("dp")
     slab = extent // groups
     place = lax.axis_index("dp").astype(jnp.int32).reshape(1)
-    block = pltpu.VMEM((extent, extent), BF16)
+    in_hbm_block = jax.ShapeDtypeStruct((extent, extent), BF16)
     whole = jax.ShapeDtypeStruct((tokens, extent), BF16)
     tokens_vmem = pltpu.VMEM((tokens, extent), BF16)
 
     grad_part = pl.pallas_call(
         functools.partial(grad_kernel, tokens * groups),
-        out_shape=block,
+        out_shape=in_hbm_block,
         in_specs=[HBM, HBM],
-        out_specs=VMEM,
-        scratch_shapes=[tokens_vmem, tokens_vmem, pltpu.SemaphoreType.DMA((2,))],
+        out_specs=HBM,
+        scratch_shapes=[
+            tokens_vmem,
+            tokens_vmem,
+            pltpu.VMEM((extent, extent), BF16),
+            pltpu.SemaphoreType.DMA((8,)),
+            pltpu.SemaphoreType.DMA((8,)),
+        ],
         compiler_params=limit(8),
         cost_estimate=pl.CostEstimate(flops=2 * tokens * extent * extent, bytes_accessed=2**20, transcendentals=0),
         name="grad_part",
@@ -226,9 +259,10 @@
     layer_near = partner(layer_part, "precond", 1)
     copies, input_sum = pl.pallas_call(
         functools.partial(sum_kernel, groups),
-        out_shape=[block, whole],
+        out_shape=[in_hbm_block, whole],
         in_specs=[VMEM, VMEM, VMEM, ANY],
-        out_specs=[VMEM] * 2,
+        out_specs=[HBM, VMEM],
+        scratch_shapes=[pltpu.VMEM((extent // 8, extent), BF16), pltpu.SemaphoreType.DMA((8,))],
         compiler_params=limit(8),
         cost_estimate=pl.CostEstimate(flops=extent * extent, bytes_accessed=2**20, transcendentals=0),
         name="sums",

time: 64.7 us -> 64.7 us (level)
  no operation moved by 1% of the time
where the time goes in v9:
time: 64.7 us; the launch traced here: 64.2 us
  starting transfers between devices  31.8 us (49%)
  waiting for transfers between devices  19.6 us (30%)
  Pallas kernels  12 us (19%)
  between operations  0.77 us (1%)
    all_to_all x2, starting transfers between devices, exchange(): return lax.all_to_all(values, axis, 0, 0, tiled=True)  18.8 us
    ppermute x4, starting transfers between devices, partner(): return lax.ppermute(values, axis, [(i, i ^ flip) for i in range(4)])  13 us
    ppermute x4, waiting for transfers between devices, partner(): return lax.ppermute(values, axis, [(i, i ^ flip) for i in range(4)])  10.1 us
    all_to_all x2, waiting for transfers between devices, exchange(): return lax.all_to_all(values, axis, 0, 0, tiled=True)  9.48 us
    pallas_call x1, Pallas kernels, shards(): pl.pallas_call(functools.partial(newton_kernel, slab), out_shape=[pltpu.V...  6.87 us
    pallas_call x1, Pallas kernels, shards(): pl.pallas_call(functools.partial(grad_kernel, tokens * groups), out_shape...  2.02 us
  transfers between devices with their start and end apart: 6, of which 4 were waited for; matrix products, arithmetic and copies ran while one was open for 0% of the time, Pallas kernels for 13%

profile of v9, /device:TPU:6, one launch (start us, length us, event | category | flops | bytes accessed | tf_op | source)
XLA Modules:
  0.0 64.2 jit_solution(17480316086021115786)
XLA Ops:
  0.6 2.0 %grad_part.1.after_any = bf16[512,512]{1,0:T(8,128)(2,1)} custom-call(bf16[128,512]{1,0:T(8,128)(2,1)} %x_any.3, bf16[128,512]{1,0:T(8,128)(2,1)} %g_any.3), custom_call_target="tpu_custom_call" | custom-call | flops 67108864 | bytes 1048576 | tf_op jit(solution)/shard_map/grad_part/pallas_call | solution.py:227
  2.7 0.0 copy-start
  2.7 0.0 copy-start.1
  2.7 0.0 copy-start.2
  2.7 13.9 %all-to-all-start = ((bf16[32,16,512]{2,1,0:T(8,128)(2,1)}), bf16[32,16,512]{2,1,0:T(8,128)(2,1)S(1)}, u32[]{:S(2)}, u32[]{:S(2)}) async-start(bf16[32,16,512]{2,1,0:T(8,128)(2,1)} %bitcast), calls=%async_computation | async-start | bytes 1048576 | tf_op jit(solution)/shard_map/all_to_all | solution.py:210
  16.6 0.0 copy-done
  16.6 0.0 copy-done.1
  16.6 0.0 copy-done.2
  16.6 0.8 %outputs_part.1 = (bf16[128,512]{1,0:T(8,128)(2,1)S(1)}, bf16[128,512]{1,0:T(8,128)(2,1)S(1)}) custom-call(bf16[128,512]{1,0:T(8,128)(2,1)S(1)} %copy-done.1, bf16[128,512]{1,0:T(8,128)(2,1)S(1)} %copy-done.2, bf16[512,512]{1,0:T(8,128)(2,1)S(1)} %copy-done, bf16[512,512]{1,0:T(8,128)(2,1)} %grad_part.1.after_any), custom_call_target="tpu_custom_call" | custom-call | flops 134217728 | bytes 1048576 | tf_op jit(solution)/shard_map/outputs_part/pallas_call | solution.py:244
  17.4 1.9 %collective-permute-start.1 = (bf16[128,512]{1,0:T(8,128)(2,1)S(1)}, bf16[128,512]{1,0:T(8,128)(2,1)S(1)}, u32[]{:S(2)}, u32[]{:S(2)}) collective-permute-start(bf16[128,512]{1,0:T(8,128)(2,1)S(1)} %get-tuple-element.16.layer_ref), channel_id=1, source_target_pairs={{0,1},{1,0},{2,3},{3,2},{4,5},{5,4},{6,7},{7,6},{8,9},{9,8},{10,11... | collective-permute-start | bytes 393224 | tf_op jit(solution)/shard_map/ppermute | solution.py:214
  19.4 2.7 %collective-permute-start = (bf16[128,512]{1,0:T(8,128)(2,1)S(1)}, bf16[128,512]{1,0:T(8,128)(2,1)S(1)}, u32[]{:S(2)}, u32[]{:S(2)}) collective-permute-start(bf16[128,512]{1,0:T(8,128)(2,1)S(1)} %get-tuple-element.15.input_ref), channel_id=1, source_target_pairs={{0,4},{4,0},{8,12},{12,8},{1,5},{5,1},{9,13},{13,9},{2,6},{6,2},{1... | collective-permute-start | bytes 393224 | tf_op jit(solution)/shard_map/ppermute | solution.py:214
  22.1 0.0 collective-permute-done.1.layer_any.layer_other
  22.1 5.0 %collective-permute-done.input_other = bf16[128,512]{1,0:T(8,128)(2,1)S(1)} collective-permute-done((bf16[128,512]{1,0:T(8,128)(2,1)S(1)}, bf16[128,512]{1,0:T(8,128)(2,1)S(1)}, u32[]{:S(2)}, u32[]{:S(2)}) %collective-permute-start) | collective-permute-done | bytes 131104 | tf_op jit(solution)/shard_map/ppermute | solution.py:214
  27.2 6.6 %all-to-all-done = bf16[32,16,512]{2,1,0:T(8,128)(2,1)S(1)} async-done(((bf16[32,16,512]{2,1,0:T(8,128)(2,1)}), bf16[32,16,512]{2,1,0:T(8,128)(2,1)S(1)}, u32[]{:S(2)}, u32[]{:S(2)}) %all-to-all-start) | async-done | bytes 524320 | tf_op jit(solution)/shard_map/all_to_all | solution.py:210
  33.8 0.9 %sums.1 = (bf16[512,512]{1,0:T(8,128)(2,1)}, bf16[128,512]{1,0:T(8,128)(2,1)S(1)}) custom-call(bf16[512,512]{1,0:T(8,128)(2,1)S(1)} %bitcast.5, bf16[128,512]{1,0:T(8,128)(2,1)S(1)} %get-tuple-element.15.input_ref, bf16[128,512]{1,0:T(8,128)(2,1)S(1)} %collective-permute-done.input_other, bf16[128,512]{1,0:T(8,128)(2,1)S(1)} %collective-permute-done.1.layer_any.layer_other), custom_call_target="tpu_custom_call" | custom-call | flops 262144 | bytes 1048576 | tf_op jit(solution)/shard_map/sums/pallas_call | solution.py:260
  34.8 4.9 %all-to-all-start.1 = ((bf16[32,16,512]{2,1,0:T(8,128)(2,1)}), bf16[32,16,512]{2,1,0:T(8,128)(2,1)S(1)}, u32[]{:S(2)}, u32[]{:S(2)}) async-start(bf16[32,16,512]{2,1,0:T(8,128)(2,1)} %bitcast.3), calls=%async_computation.1 | async-start | bytes 1048576 | tf_op jit(solution)/shard_map/all_to_all | solution.py:210
  39.7 3.3 %collective-permute-start.2 = (bf16[128,512]{1,0:T(8,128)(2,1)S(1)}, bf16[128,512]{1,0:T(8,128)(2,1)S(1)}, u32[]{:S(2)}, u32[]{:S(2)}) collective-permute-start(bf16[128,512]{1,0:T(8,128)(2,1)S(1)} %get-tuple-element.17.input_ref), channel_id=1, source_target_pairs={{0,8},{4,12},{8,0},{12,4},{1,9},{5,13},{9,1},{13,5},{2,10},{6,14},... | collective-permute-start | bytes 393224 | tf_op jit(solution)/shard_map/ppermute | solution.py:214
  43.0 5.0 %collective-permute-done.2.input_other = bf16[128,512]{1,0:T(8,128)(2,1)S(1)} collective-permute-done((bf16[128,512]{1,0:T(8,128)(2,1)S(1)}, bf16[128,512]{1,0:T(8,128)(2,1)S(1)}, u32[]{:S(2)}, u32[]{:S(2)}) %collective-permute-start.2) | collective-permute-done | bytes 131104 | tf_op jit(solution)/shard_map/ppermute | solution.py:214
  48.0 0.7 %middle.1 = (bf16[128,512]{1,0:T(8,128)(2,1)}, bf16[128,512]{1,0:T(8,128)(2,1)S(1)}) custom-call(bf16[128,512]{1,0:T(8,128)(2,1)S(1)} %get-tuple-element.17.input_ref, bf16[128,512]{1,0:T(8,128)(2,1)S(1)} %collective-permute-done.2.input_other, bf16[128,512]{1,0:T(8,128)(2,1)S(1)} %get-tuple-element.16.layer_ref, ...), custom_call_target="tpu_custom_call" | custom-call | bytes 524288 | tf_op jit(solution)/shard_map/middle/pallas_call | solution.py:272
  48.7 5.0 %collective-permute-start.3 = (bf16[128,512]{1,0:T(8,128)(2,1)S(1)}, bf16[128,512]{1,0:T(8,128)(2,1)S(1)}, u32[]{:S(2)}, u32[]{:S(2)}) collective-permute-start(bf16[128,512]{1,0:T(8,128)(2,1)S(1)} %get-tuple-element.18.layer_ref), channel_id=1, source_target_pairs={{0,2},{1,3},{2,0},{3,1},{4,6},{5,7},{6,4},{7,5},{8,10},{9,11},{10,... | collective-permute-start | bytes 393224 | tf_op jit(solution)/shard_map/ppermute | solution.py:214
  53.8 2.8 %all-to-all-done.1 = bf16[32,16,512]{2,1,0:T(8,128)(2,1)S(1)} async-done(((bf16[32,16,512]{2,1,0:T(8,128)(2,1)}), bf16[32,16,512]{2,1,0:T(8,128)(2,1)S(1)}, u32[]{:S(2)}, u32[]{:S(2)}) %all-to-all-start.1) | async-done | bytes 524320 | tf_op jit(solution)/shard_map/all_to_all | solution.py:210
  56.6 6.9 %newton.1 = (f32[1,16,512]{2,1,0:T(8,128)S(1)}, f32[1,16,512]{2,1,0:T(8,128)S(1)}) custom-call(s32[1]{0:T(128)} %bitcast.2.place_ref, bf16[512,512]{1,0:T(8,128)(2,1)S(1)} %bitcast.6), custom_call_target="tpu_custom_call" | custom-call | bytes 65536 | tf_op jit(solution)/shard_map/newton/pallas_call | solution.py:284
  63.5 0.0 collective-permute-done.3.layer_other
  63.5 0.7 %last.1 = (bf16[128,512]{1,0:T(8,128)(2,1)}, f32[1,16,512]{2,1,0:T(8,128)}, f32[1,16,512]{2,1,0:T(8,128)}) custom-call(bf16[128,512]{1,0:T(8,128)(2,1)S(1)} %get-tuple-element.18.layer_ref, bf16[128,512]{1,0:T(8,128)(2,1)S(1)} %collective-permute-done.3.layer_other, f32[1,16,512]{2,1,0:T(8,128)S(1)} %get-tuple-element.20.left_ref, ...), custom_call_target="tpu_custom_call" | custom-call | bytes 262144 | tf_op jit(solution)/shard_map/last/pallas_call | solution.py:300
Async XLA Ops:
  2.7 13.9 %copy-start = (bf16[512,512]{1,0:T(8,128)(2,1)S(1)}, bf16[512,512]{1,0:T(8,128)(2,1)}, u32[]{:S(2)}) copy-start(bf16[512,512]{1,0:T(8,128)(2,1)} %w_any.1) | copy-start | bytes 1572868
  2.7 13.9 %copy-start.1 = (bf16[128,512]{1,0:T(8,128)(2,1)S(1)}, bf16[128,512]{1,0:T(8,128)(2,1)}, u32[]{:S(2)}) copy-start(bf16[128,512]{1,0:T(8,128)(2,1)} %x_any.3) | copy-start | bytes 393220
  2.7 13.9 %copy-start.2 = (bf16[128,512]{1,0:T(8,128)(2,1)S(1)}, bf16[128,512]{1,0:T(8,128)(2,1)}, u32[]{:S(2)}) copy-start(bf16[128,512]{1,0:T(8,128)(2,1)} %g_any.3) | copy-start | bytes 393220
  2.7 31.1 %all-to-all-start = ((bf16[32,16,512]{2,1,0:T(8,128)(2,1)}), bf16[32,16,512]{2,1,0:T(8,128)(2,1)S(1)}, u32[]{:S(2)}, u32[]{:S(2)}) async-start(bf16[32,16,512]{2,1,0:T(8,128)(2,1)} %bitcast), calls=%async_computation | async-start | bytes 1048576 | tf_op jit(solution)/shard_map/all_to_all | solution.py:210
  17.4 4.7 %collective-permute-start.1 = (bf16[128,512]{1,0:T(8,128)(2,1)S(1)}, bf16[128,512]{1,0:T(8,128)(2,1)S(1)}, u32[]{:S(2)}, u32[]{:S(2)}) collective-permute-start(bf16[128,512]{1,0:T(8,128)(2,1)S(1)} %get-tuple-element.16.layer_ref), channel_id=1, source_target_pairs={{0,1},{1,0},{2,3},{3,2},{4,5},{5,4},{6,7},{7,6},{8,9},{9,8},{10,11... | collective-permute-start | bytes 393224 | tf_op jit(solution)/shard_map/ppermute | solution.py:214
  19.4 7.8 %collective-permute-start = (bf16[128,512]{1,0:T(8,128)(2,1)S(1)}, bf16[128,512]{1,0:T(8,128)(2,1)S(1)}, u32[]{:S(2)}, u32[]{:S(2)}) collective-permute-start(bf16[128,512]{1,0:T(8,128)(2,1)S(1)} %get-tuple-element.15.input_ref), channel_id=1, source_target_pairs={{0,4},{4,0},{8,12},{12,8},{1,5},{5,1},{9,13},{13,9},{2,6},{6,2},{1... | collective-permute-start | bytes 393224 | tf_op jit(solution)/shard_map/ppermute | solution.py:214
  34.8 21.9 %all-to-all-start.1 = ((bf16[32,16,512]{2,1,0:T(8,128)(2,1)}), bf16[32,16,512]{2,1,0:T(8,128)(2,1)S(1)}, u32[]{:S(2)}, u32[]{:S(2)}) async-start(bf16[32,16,512]{2,1,0:T(8,128)(2,1)} %bitcast.3), calls=%async_computation.1 | async-start | bytes 1048576 | tf_op jit(solution)/shard_map/all_to_all | solution.py:210
  39.7 8.4 %collective-permute-start.2 = (bf16[128,512]{1,0:T(8,128)(2,1)S(1)}, bf16[128,512]{1,0:T(8,128)(2,1)S(1)}, u32[]{:S(2)}, u32[]{:S(2)}) collective-permute-start(bf16[128,512]{1,0:T(8,128)(2,1)S(1)} %get-tuple-element.17.input_ref), channel_id=1, source_target_pairs={{0,8},{4,12},{8,0},{12,4},{1,9},{5,13},{9,1},{13,5},{2,10},{6,14},... | collective-permute-start | bytes 393224 | tf_op jit(solution)/shard_map/ppermute | solution.py:214
  48.7 14.8 %collective-permute-start.3 = (bf16[128,512]{1,0:T(8,128)(2,1)S(1)}, bf16[128,512]{1,0:T(8,128)(2,1)S(1)}, u32[]{:S(2)}, u32[]{:S(2)}) collective-permute-start(bf16[128,512]{1,0:T(8,128)(2,1)S(1)} %get-tuple-element.18.layer_ref), channel_id=1, source_target_pairs={{0,2},{1,3},{2,0},{3,1},{4,6},{5,7},{6,4},{7,5},{8,10},{9,11},{10,... | collective-permute-start | bytes 393224 | tf_op jit(solution)/shard_map/ppermute | solution.py:214

commit v10 on v5

--- a/solution.py
+++ b/solution.py
@@ -8,6 +8,10 @@
 from jax.sharding import PartitionSpec as P
 
 ITERS = 6
+ORDER = (
+    (26, 6, 9, 23, 12, 28, 25, 22, 15, 31, 5, 24, 4, 17, 18, 27)
+    + (13, 20, 10, 7, 30, 16, 19, 8, 2, 1, 21, 3, 11, 29, 0, 14)
+)
 VMEM = pl.BlockSpec(memory_space=pltpu.VMEM)
 HBM = pl.BlockSpec(memory_space=pltpu.HBM)
 ANY = pl.BlockSpec(memory_space=pl.ANY)
@@ -179,8 +183,10 @@
     return pltpu.CompilerParams(vmem_limit_bytes=mebibytes * 2**20)
 
 
-def exchange(values, axis):
-    return lax.all_to_all(values, axis, 0, 0, tiled=True)
+def exchange(values):
+    size = lax.axis_size("dp")
+    order = ORDER if size == len(ORDER) else range(size)
+    return lax.all_to_all(values, "dp", 0, 0, tiled=True, axis_index_groups=[list(order)])
 
 
 def partner(values, axis, flip):
@@ -207,7 +213,7 @@
         cost_estimate=pl.CostEstimate(flops=2 * tokens * extent * extent, bytes_accessed=2**20, transcendentals=0),
         name="grad_part",
     )(in_hbm(x_in), in_hbm(grad_out))
-    received = exchange(grad_part, "dp")
+    received = exchange(grad_part)
     layer_part, input_part = pl.pallas_call(
         outputs_kernel,
         out_shape=[whole, whole],
@@ -233,7 +239,7 @@
         cost_estimate=pl.CostEstimate(flops=extent * extent, bytes_accessed=2**20, transcendentals=0),
         name="sums",
     )(received, input_part, partner(input_part, "tensor", 1), layer_near)
-    grad_low = exchange(copies, "dp")
+    grad_low = exchange(copies)
 
     grad_in, layer_sum = pl.pallas_call(
         middle_kernel,

time: 64.7 us -> 64 us (0.989)
  waiting for transfers between devices: 19.6 us -> 13.5 us
  starting transfers between devices: 31.8 us -> 37.1 us
    all_to_all x2, waiting for transfers between devices: 9.49 us -> 3.42 us  [exchange(): lax.all_to_all(values, 'dp', 0, 0, tiled=True, axis_index_groups=[list(or...]
    all_to_all x2, starting transfers between devices: 18.8 us -> 22.7 us  [exchange(): lax.all_to_all(values, 'dp', 0, 0, tiled=True, axis_index_groups=[list(or...]
    ppermute x4, starting transfers between devices: 13 us -> 14.4 us  [partner(): return lax.ppermute(values, axis, [(i, i ^ flip) for i in range(4)])]
  transfers between devices with their start and end apart: 6 -> 6, of which waited for: 4 -> 3; matrix products, arithmetic and copies ran while one was open for 0% -> 0% of each run, Pallas kernels for 13% -> 13%
where the time goes in v10:
time: 64 us; the launch traced here: 63.5 us
  starting transfers between devices  37.1 us (58%)
  waiting for transfers between devices  13.5 us (21%)
  Pallas kernels  12.1 us (19%)
  between operations  0.77 us (1%)
    all_to_all x2, starting transfers between devices, exchange(): lax.all_to_all(values, 'dp', 0, 0, tiled=True, axis_index_groups=[list(or...  22.7 us
    ppermute x4, starting transfers between devices, partner(): return lax.ppermute(values, axis, [(i, i ^ flip) for i in range(4)])  14.4 us
    ppermute x4, waiting for transfers between devices, partner(): return lax.ppermute(values, axis, [(i, i ^ flip) for i in range(4)])  10.1 us
    pallas_call x1, Pallas kernels, shards(): pl.pallas_call(functools.partial(newton_kernel, slab), out_shape=[pltpu.V...  6.87 us
    all_to_all x2, waiting for transfers between devices, exchange(): lax.all_to_all(values, 'dp', 0, 0, tiled=True, axis_index_groups=[list(or...  3.42 us
    pallas_call x1, Pallas kernels, shards(): pl.pallas_call(functools.partial(grad_kernel, tokens * groups), out_shape...  2.09 us
  transfers between devices with their start and end apart: 6, of which 3 were waited for; matrix products, arithmetic and copies ran while one was open for 0% of the time, Pallas kernels for 13%

profile of v10, /device:TPU:6, one launch (start us, length us, event | category | flops | bytes accessed | tf_op | source)
XLA Modules:
  0.0 63.5 jit_solution(6534684456866535039)
XLA Ops:
  0.6 2.1 %grad_part.1.after_any = bf16[512,512]{1,0:T(8,128)(2,1)} custom-call(bf16[128,512]{1,0:T(8,128)(2,1)} %x_any.3, bf16[128,512]{1,0:T(8,128)(2,1)} %g_any.3), custom_call_target="tpu_custom_call" | custom-call | flops 67108864 | bytes 1048576 | tf_op jit(solution)/shard_map/grad_part/pallas_call | solution.py:206
  2.7 0.0 copy-start
  2.7 0.0 copy-start.1
  2.8 0.0 copy-start.2
  2.8 15.2 %all-to-all-start = ((bf16[32,16,512]{2,1,0:T(8,128)(2,1)}), bf16[32,16,512]{2,1,0:T(8,128)(2,1)S(1)}, u32[]{:S(2)}, u32[]{:S(2)}) async-start(bf16[32,16,512]{2,1,0:T(8,128)(2,1)} %bitcast), calls=%async_computation | async-start | bytes 1048576 | tf_op jit(solution)/shard_map/all_to_all | solution.py:189
  18.0 0.0 copy-done
  18.0 0.0 copy-done.1
  18.0 0.0 copy-done.2
  18.0 0.8 %outputs_part.1 = (bf16[128,512]{1,0:T(8,128)(2,1)S(1)}, bf16[128,512]{1,0:T(8,128)(2,1)S(1)}) custom-call(bf16[128,512]{1,0:T(8,128)(2,1)S(1)} %copy-done.1, bf16[128,512]{1,0:T(8,128)(2,1)S(1)} %copy-done.2, bf16[512,512]{1,0:T(8,128)(2,1)S(1)} %copy-done, bf16[512,512]{1,0:T(8,128)(2,1)} %grad_part.1.after_any), custom_call_target="tpu_custom_call" | custom-call | flops 134217728 | bytes 1048576 | tf_op jit(solution)/shard_map/outputs_part/pallas_call | solution.py:217
  18.8 1.9 %collective-permute-start.1 = (bf16[128,512]{1,0:T(8,128)(2,1)S(1)}, bf16[128,512]{1,0:T(8,128)(2,1)S(1)}, u32[]{:S(2)}, u32[]{:S(2)}) collective-permute-start(bf16[128,512]{1,0:T(8,128)(2,1)S(1)} %get-tuple-element.16.layer_ref), channel_id=1, source_target_pairs={{0,1},{1,0},{2,3},{3,2},{4,5},{5,4},{6,7},{7,6},{8,9},{9,8},{10,11... | collective-permute-start | bytes 393224 | tf_op jit(solution)/shard_map/ppermute | solution.py:193
  20.7 2.7 %collective-permute-start = (bf16[128,512]{1,0:T(8,128)(2,1)S(1)}, bf16[128,512]{1,0:T(8,128)(2,1)S(1)}, u32[]{:S(2)}, u32[]{:S(2)}) collective-permute-start(bf16[128,512]{1,0:T(8,128)(2,1)S(1)} %get-tuple-element.15.input_ref), channel_id=1, source_target_pairs={{0,4},{4,0},{8,12},{12,8},{1,5},{5,1},{9,13},{13,9},{2,6},{6,2},{1... | collective-permute-start | bytes 393224 | tf_op jit(solution)/shard_map/ppermute | solution.py:193
  23.5 0.0 collective-permute-done.1.layer_any.layer_other
  23.5 5.0 %collective-permute-done.input_other = bf16[128,512]{1,0:T(8,128)(2,1)S(1)} collective-permute-done((bf16[128,512]{1,0:T(8,128)(2,1)S(1)}, bf16[128,512]{1,0:T(8,128)(2,1)S(1)}, u32[]{:S(2)}, u32[]{:S(2)}) %collective-permute-start) | collective-permute-done | bytes 131104 | tf_op jit(solution)/shard_map/ppermute | solution.py:193
  28.5 3.4 %all-to-all-done = bf16[32,16,512]{2,1,0:T(8,128)(2,1)S(1)} async-done(((bf16[32,16,512]{2,1,0:T(8,128)(2,1)}), bf16[32,16,512]{2,1,0:T(8,128)(2,1)S(1)}, u32[]{:S(2)}, u32[]{:S(2)}) %all-to-all-start) | async-done | bytes 524320 | tf_op jit(solution)/shard_map/all_to_all | solution.py:189
  32.0 0.9 %sums.1 = (bf16[512,512]{1,0:T(8,128)(2,1)}, bf16[128,512]{1,0:T(8,128)(2,1)S(1)}) custom-call(bf16[512,512]{1,0:T(8,128)(2,1)S(1)} %bitcast.5, bf16[128,512]{1,0:T(8,128)(2,1)S(1)} %get-tuple-element.15.input_ref, bf16[128,512]{1,0:T(8,128)(2,1)S(1)} %collective-permute-done.input_other, bf16[128,512]{1,0:T(8,128)(2,1)S(1)} %collective-permute-done.1.layer_any.layer_other), custom_call_target="tpu_custom_call" | custom-call | flops 262144 | bytes 1048576 | tf_op jit(solution)/shard_map/sums/pallas_call | solution.py:233
  32.9 7.5 %all-to-all-start.1 = ((bf16[32,16,512]{2,1,0:T(8,128)(2,1)}), bf16[32,16,512]{2,1,0:T(8,128)(2,1)S(1)}, u32[]{:S(2)}, u32[]{:S(2)}) async-start(bf16[32,16,512]{2,1,0:T(8,128)(2,1)} %bitcast.3), calls=%async_computation.1 | async-start | bytes 1048576 | tf_op jit(solution)/shard_map/all_to_all | solution.py:189
  40.4 3.3 %collective-permute-start.2 = (bf16[128,512]{1,0:T(8,128)(2,1)S(1)}, bf16[128,512]{1,0:T(8,128)(2,1)S(1)}, u32[]{:S(2)}, u32[]{:S(2)}) collective-permute-start(bf16[128,512]{1,0:T(8,128)(2,1)S(1)} %get-tuple-element.17.input_ref), channel_id=1, source_target_pairs={{0,8},{4,12},{8,0},{12,4},{1,9},{5,13},{9,1},{13,5},{2,10},{6,14},... | collective-permute-start | bytes 393224 | tf_op jit(solution)/shard_map/ppermute | solution.py:193
  43.7 5.1 %collective-permute-done.2.input_other = bf16[128,512]{1,0:T(8,128)(2,1)S(1)} collective-permute-done((bf16[128,512]{1,0:T(8,128)(2,1)S(1)}, bf16[128,512]{1,0:T(8,128)(2,1)S(1)}, u32[]{:S(2)}, u32[]{:S(2)}) %collective-permute-start.2) | collective-permute-done | bytes 131104 | tf_op jit(solution)/shard_map/ppermute | solution.py:193
  48.7 0.7 %middle.1 = (bf16[128,512]{1,0:T(8,128)(2,1)}, bf16[128,512]{1,0:T(8,128)(2,1)S(1)}) custom-call(bf16[128,512]{1,0:T(8,128)(2,1)S(1)} %get-tuple-element.17.input_ref, bf16[128,512]{1,0:T(8,128)(2,1)S(1)} %collective-permute-done.2.input_other, bf16[128,512]{1,0:T(8,128)(2,1)S(1)} %get-tuple-element.16.layer_ref, ...), custom_call_target="tpu_custom_call" | custom-call | bytes 524288 | tf_op jit(solution)/shard_map/middle/pallas_call | solution.py:244
  49.4 6.4 %collective-permute-start.3 = (bf16[128,512]{1,0:T(8,128)(2,1)S(1)}, bf16[128,512]{1,0:T(8,128)(2,1)S(1)}, u32[]{:S(2)}, u32[]{:S(2)}) collective-permute-start(bf16[128,512]{1,0:T(8,128)(2,1)S(1)} %get-tuple-element.18.layer_ref), channel_id=1, source_target_pairs={{0,2},{1,3},{2,0},{3,1},{4,6},{5,7},{6,4},{7,5},{8,10},{9,11},{10,... | collective-permute-start | bytes 393224 | tf_op jit(solution)/shard_map/ppermute | solution.py:193
  55.9 0.0 all-to-all-done.1
  55.9 6.9 %newton.1 = (f32[1,16,512]{2,1,0:T(8,128)S(1)}, f32[1,16,512]{2,1,0:T(8,128)S(1)}) custom-call(s32[1]{0:T(128)} %bitcast.2.place_ref, bf16[512,512]{1,0:T(8,128)(2,1)S(1)} %bitcast.6), custom_call_target="tpu_custom_call" | custom-call | bytes 65536 | tf_op jit(solution)/shard_map/newton/pallas_call | solution.py:256
  62.8 0.0 collective-permute-done.3.layer_other
  62.8 0.7 %last.1 = (bf16[128,512]{1,0:T(8,128)(2,1)}, f32[1,16,512]{2,1,0:T(8,128)}, f32[1,16,512]{2,1,0:T(8,128)}) custom-call(bf16[128,512]{1,0:T(8,128)(2,1)S(1)} %get-tuple-element.18.layer_ref, bf16[128,512]{1,0:T(8,128)(2,1)S(1)} %collective-permute-done.3.layer_other, f32[1,16,512]{2,1,0:T(8,128)S(1)} %get-tuple-element.20.left_ref, ...), custom_call_target="tpu_custom_call" | custom-call | bytes 262144 | tf_op jit(solution)/shard_map/last/pallas_call | solution.py:272
Async XLA Ops:
  2.7 15.2 %copy-start = (bf16[512,512]{1,0:T(8,128)(2,1)S(1)}, bf16[512,512]{1,0:T(8,128)(2,1)}, u32[]{:S(2)}) copy-start(bf16[512,512]{1,0:T(8,128)(2,1)} %w_any.1) | copy-start | bytes 1572868
  2.7 15.2 %copy-start.1 = (bf16[128,512]{1,0:T(8,128)(2,1)S(1)}, bf16[128,512]{1,0:T(8,128)(2,1)}, u32[]{:S(2)}) copy-start(bf16[128,512]{1,0:T(8,128)(2,1)} %x_any.3) | copy-start | bytes 393220
  2.8 15.2 %copy-start.2 = (bf16[128,512]{1,0:T(8,128)(2,1)S(1)}, bf16[128,512]{1,0:T(8,128)(2,1)}, u32[]{:S(2)}) copy-start(bf16[128,512]{1,0:T(8,128)(2,1)} %g_any.3) | copy-start | bytes 393220
  2.8 29.2 %all-to-all-start = ((bf16[32,16,512]{2,1,0:T(8,128)(2,1)}), bf16[32,16,512]{2,1,0:T(8,128)(2,1)S(1)}, u32[]{:S(2)}, u32[]{:S(2)}) async-start(bf16[32,16,512]{2,1,0:T(8,128)(2,1)} %bitcast), calls=%async_computation | async-start | bytes 1048576 | tf_op jit(solution)/shard_map/all_to_all | solution.py:189
  18.8 4.7 %collective-permute-start.1 = (bf16[128,512]{1,0:T(8,128)(2,1)S(1)}, bf16[128,512]{1,0:T(8,128)(2,1)S(1)}, u32[]{:S(2)}, u32[]{:S(2)}) collective-permute-start(bf16[128,512]{1,0:T(8,128)(2,1)S(1)} %get-tuple-element.16.layer_ref), channel_id=1, source_target_pairs={{0,1},{1,0},{2,3},{3,2},{4,5},{5,4},{6,7},{7,6},{8,9},{9,8},{10,11... | collective-permute-start | bytes 393224 | tf_op jit(solution)/shard_map/ppermute | solution.py:193
  20.7 7.8 %collective-permute-start = (bf16[128,512]{1,0:T(8,128)(2,1)S(1)}, bf16[128,512]{1,0:T(8,128)(2,1)S(1)}, u32[]{:S(2)}, u32[]{:S(2)}) collective-permute-start(bf16[128,512]{1,0:T(8,128)(2,1)S(1)} %get-tuple-element.15.input_ref), channel_id=1, source_target_pairs={{0,4},{4,0},{8,12},{12,8},{1,5},{5,1},{9,13},{13,9},{2,6},{6,2},{1... | collective-permute-start | bytes 393224 | tf_op jit(solution)/shard_map/ppermute | solution.py:193
  32.9 23.0 %all-to-all-start.1 = ((bf16[32,16,512]{2,1,0:T(8,128)(2,1)}), bf16[32,16,512]{2,1,0:T(8,128)(2,1)S(1)}, u32[]{:S(2)}, u32[]{:S(2)}) async-start(bf16[32,16,512]{2,1,0:T(8,128)(2,1)} %bitcast.3), calls=%async_computation.1 | async-start | bytes 1048576 | tf_op jit(solution)/shard_map/all_to_all | solution.py:189
  40.4 8.4 %collective-permute-start.2 = (bf16[128,512]{1,0:T(8,128)(2,1)S(1)}, bf16[128,512]{1,0:T(8,128)(2,1)S(1)}, u32[]{:S(2)}, u32[]{:S(2)}) collective-permute-start(bf16[128,512]{1,0:T(8,128)(2,1)S(1)} %get-tuple-element.17.input_ref), channel_id=1, source_target_pairs={{0,8},{4,12},{8,0},{12,4},{1,9},{5,13},{9,1},{13,5},{2,10},{6,14},... | collective-permute-start | bytes 393224 | tf_op jit(solution)/shard_map/ppermute | solution.py:193
  49.4 13.3 %collective-permute-start.3 = (bf16[128,512]{1,0:T(8,128)(2,1)S(1)}, bf16[128,512]{1,0:T(8,128)(2,1)S(1)}, u32[]{:S(2)}, u32[]{:S(2)}) collective-permute-start(bf16[128,512]{1,0:T(8,128)(2,1)S(1)} %get-tuple-element.18.layer_ref), channel_id=1, source_target_pairs={{0,2},{1,3},{2,0},{3,1},{4,6},{5,7},{6,4},{7,5},{8,10},{9,11},{10,... | collective-permute-start | bytes 393224 | tf_op jit(solution)/shard_map/ppermute | solution.py:193

commit v11 on v10

--- a/solution.py
+++ b/solution.py
@@ -42,7 +42,7 @@
     return (left_ref[...].astype(F32) + right_ref[...].astype(F32)).astype(BF16)
 
 
-def sum_kernel(copies, parts_ref, input_ref, input_other, layer_any, out_ref, input_sum):
+def sum_kernel(copies, parts_ref, input_ref, input_other, layer_ref, layer_other, out_ref, input_sum, layer_sum):
     slab = parts_ref.shape[0] // copies
     total = parts_ref[:slab, :].astype(F32)
     for k in range(1, copies):
@@ -51,6 +51,7 @@
     for k in range(copies):
         out_ref[k * slab : (k + 1) * slab, :] = total
     input_sum[...] = pair_sum(input_ref, input_other)
+    layer_sum[...] = pair_sum(layer_ref, layer_other)
 
 
 def outputs_kernel(x_any, g_any, w_any, after_any, layer_ref, input_ref, x_ref, g_ref, w_ref, sems):
@@ -59,8 +60,7 @@
     input_ref[...] = mm(g_ref[...], w_ref[...], ((1,), (1,))).astype(BF16)
 
 
-def middle_kernel(input_ref, input_other, layer_ref, layer_other, input_out, layer_sum):
-    layer_sum[...] = pair_sum(layer_ref, layer_other)
+def middle_kernel(input_ref, input_other, input_out):
     input_out[...] = pair_sum(input_ref, input_other)
 
 
@@ -230,26 +230,26 @@
         name="outputs_part",
     )(x_in, grad_out, weight, grad_part)
     layer_near = partner(layer_part, "precond", 1)
-    copies, input_sum = pl.pallas_call(
+    copies, input_sum, layer_sum = pl.pallas_call(
         functools.partial(sum_kernel, groups),
-        out_shape=[block, whole],
-        in_specs=[VMEM, VMEM, VMEM, ANY],
-        out_specs=[VMEM] * 2,
+        out_shape=[block, whole, whole],
+        in_specs=[VMEM] * 5,
+        out_specs=[VMEM] * 3,
         compiler_params=limit(8),
         cost_estimate=pl.CostEstimate(flops=extent * extent, bytes_accessed=2**20, transcendentals=0),
         name="sums",
-    )(received, input_part, partner(input_part, "tensor", 1), layer_near)
+    )(received, input_part, partner(input_part, "tensor", 1), layer_part, layer_near)
     grad_low = exchange(copies)
 
-    grad_in, layer_sum = pl.pallas_call(
+    grad_in = pl.pallas_call(
         middle_kernel,
-        out_shape=[whole, whole],
-        in_specs=[VMEM] * 4,
-        out_specs=[VMEM] * 2,
+        out_shape=whole,
+        in_specs=[VMEM] * 2,
+        out_specs=VMEM,
         compiler_params=limit(8),
         cost_estimate=pl.CostEstimate(flops=0, bytes_accessed=2**19, transcendentals=0),
         name="middle",
-    )(input_sum, partner(input_sum, "tensor", 2), layer_part, layer_near)
+    )(input_sum, partner(input_sum, "tensor", 2))
     layer_other = partner(layer_sum, "precond", 2)
 
     root = jax.ShapeDtypeStruct((1, slab, extent), F32)

time: 64 us -> 67.8 us (1.059)
  waiting for transfers between devices: 13.5 us -> 17.3 us
    all_to_all x2, waiting for transfers between devices: 3.42 us -> 15.2 us  [exchange(): lax.all_to_all(values, 'dp', 0, 0, tiled=True, axis_index_groups=[list(or...]
    ppermute x4, waiting for transfers between devices: 10.1 us -> 2.19 us  [partner(): return lax.ppermute(values, axis, [(i, i ^ flip) for i in range(4)])]
  transfers between devices with their start and end apart: 6 -> 6, of which waited for: 3 -> 3; matrix products, arithmetic and copies ran while one was open for 0% -> 0% of each run, Pallas kernels for 13% -> 12%
where the time goes in v11:
time: 67.8 us; the launch traced here: 67.3 us
  starting transfers between devices  37.1 us (55%)
  waiting for transfers between devices  17.3 us (26%)
  Pallas kernels  12.1 us (18%)
  between operations  0.76 us (1%)
    all_to_all x2, starting transfers between devices, exchange(): lax.all_to_all(values, 'dp', 0, 0, tiled=True, axis_index_groups=[list(or...  22.7 us
    all_to_all x2, waiting for transfers between devices, exchange(): lax.all_to_all(values, 'dp', 0, 0, tiled=True, axis_index_groups=[list(or...  15.2 us
    ppermute x4, starting transfers between devices, partner(): return lax.ppermute(values, axis, [(i, i ^ flip) for i in range(4)])  14.4 us
    pallas_call x1, Pallas kernels, shards(): pl.pallas_call(functools.partial(newton_kernel, slab), out_shape=[pltpu.V...  6.87 us
    ppermute x4, waiting for transfers between devices, partner(): return lax.ppermute(values, axis, [(i, i ^ flip) for i in range(4)])  2.19 us
    pallas_call x1, Pallas kernels, shards(): pl.pallas_call(functools.partial(grad_kernel, tokens * groups), out_shape...  2.09 us
  transfers between devices with their start and end apart: 6, of which 3 were waited for; matrix products, arithmetic and copies ran while one was open for 0% of the time, Pallas kernels for 12%

profile of v11, /device:TPU:6, one launch (start us, length us, event | category | flops | bytes accessed | tf_op | source)
XLA Modules:
  0.0 67.3 jit_solution(6542559446498501074)
XLA Ops:
  0.6 2.1 %grad_part.1.after_any = bf16[512,512]{1,0:T(8,128)(2,1)} custom-call(bf16[128,512]{1,0:T(8,128)(2,1)} %x_any.3, bf16[128,512]{1,0:T(8,128)(2,1)} %g_any.3), custom_call_target="tpu_custom_call" | custom-call | flops 67108864 | bytes 1048576 | tf_op jit(solution)/shard_map/grad_part/pallas_call | solution.py:206
  2.7 0.0 copy-start
  2.7 0.0 copy-start.1
  2.8 0.0 copy-start.2
  2.8 15.2 %all-to-all-start = ((bf16[32,16,512]{2,1,0:T(8,128)(2,1)}), bf16[32,16,512]{2,1,0:T(8,128)(2,1)S(1)}, u32[]{:S(2)}, u32[]{:S(2)}) async-start(bf16[32,16,512]{2,1,0:T(8,128)(2,1)} %bitcast), calls=%async_computation | async-start | bytes 1048576 | tf_op jit(solution)/shard_map/all_to_all | solution.py:189
  18.0 0.0 copy-done
  18.0 0.0 copy-done.1
  18.0 0.0 copy-done.2
  18.0 0.8 %outputs_part.1 = (bf16[128,512]{1,0:T(8,128)(2,1)S(1)}, bf16[128,512]{1,0:T(8,128)(2,1)S(1)}) custom-call(bf16[128,512]{1,0:T(8,128)(2,1)S(1)} %copy-done.1, bf16[128,512]{1,0:T(8,128)(2,1)S(1)} %copy-done.2, bf16[512,512]{1,0:T(8,128)(2,1)S(1)} %copy-done, bf16[512,512]{1,0:T(8,128)(2,1)} %grad_part.1.after_any), custom_call_target="tpu_custom_call" | custom-call | flops 134217728 | bytes 1048576 | tf_op jit(solution)/shard_map/outputs_part/pallas_call | solution.py:217
  18.8 2.7 %collective-permute-start = (bf16[128,512]{1,0:T(8,128)(2,1)S(1)}, bf16[128,512]{1,0:T(8,128)(2,1)S(1)}, u32[]{:S(2)}, u32[]{:S(2)}) collective-permute-start(bf16[128,512]{1,0:T(8,128)(2,1)S(1)} %get-tuple-element.14.input_ref), channel_id=1, source_target_pairs={{0,4},{4,0},{8,12},{12,8},{1,5},{5,1},{9,13},{13,9},{2,6},{6,2},{1... | collective-permute-start | bytes 393224 | tf_op jit(solution)/shard_map/ppermute | solution.py:193
  21.6 1.9 %collective-permute-start.1 = (bf16[128,512]{1,0:T(8,128)(2,1)S(1)}, bf16[128,512]{1,0:T(8,128)(2,1)S(1)}, u32[]{:S(2)}, u32[]{:S(2)}) collective-permute-start(bf16[128,512]{1,0:T(8,128)(2,1)S(1)} %get-tuple-element.15.layer_ref), channel_id=1, source_target_pairs={{0,1},{1,0},{2,3},{3,2},{4,5},{5,4},{6,7},{7,6},{8,9},{9,8},{10,11... | collective-permute-start | bytes 393224 | tf_op jit(solution)/shard_map/ppermute | solution.py:193
  23.5 2.2 %collective-permute-done.input_other = bf16[128,512]{1,0:T(8,128)(2,1)S(1)} collective-permute-done((bf16[128,512]{1,0:T(8,128)(2,1)S(1)}, bf16[128,512]{1,0:T(8,128)(2,1)S(1)}, u32[]{:S(2)}, u32[]{:S(2)}) %collective-permute-start) | collective-permute-done | bytes 131104 | tf_op jit(solution)/shard_map/ppermute | solution.py:193
  25.7 0.0 collective-permute-done.1.layer_other
  25.7 6.3 %all-to-all-done = bf16[32,16,512]{2,1,0:T(8,128)(2,1)S(1)} async-done(((bf16[32,16,512]{2,1,0:T(8,128)(2,1)}), bf16[32,16,512]{2,1,0:T(8,128)(2,1)S(1)}, u32[]{:S(2)}, u32[]{:S(2)}) %all-to-all-start) | async-done | bytes 524320 | tf_op jit(solution)/shard_map/all_to_all | solution.py:189
  32.0 0.9 %sums.1 = (bf16[512,512]{1,0:T(8,128)(2,1)}, bf16[128,512]{1,0:T(8,128)(2,1)S(1)}, bf16[128,512]{1,0:T(8,128)(2,1)S(1)}) custom-call(bf16[512,512]{1,0:T(8,128)(2,1)S(1)} %bitcast.6, bf16[128,512]{1,0:T(8,128)(2,1)S(1)} %get-tuple-element.14.input_ref, bf16[128,512]{1,0:T(8,128)(2,1)S(1)} %collective-permute-done.input_other, ...), custom_call_target="tpu_custom_call" | custom-call | flops 262144 | bytes 1048576 | tf_op jit(solution)/shard_map/sums/pallas_call | solution.py:233
  32.9 7.5 %all-to-all-start.1 = ((bf16[32,16,512]{2,1,0:T(8,128)(2,1)}), bf16[32,16,512]{2,1,0:T(8,128)(2,1)S(1)}, u32[]{:S(2)}, u32[]{:S(2)}) async-start(bf16[32,16,512]{2,1,0:T(8,128)(2,1)} %bitcast.3), calls=%async_computation.1 | async-start | bytes 1048576 | tf_op jit(solution)/shard_map/all_to_all | solution.py:189
  40.4 3.3 %collective-permute-start.3 = (bf16[128,512]{1,0:T(8,128)(2,1)S(1)}, bf16[128,512]{1,0:T(8,128)(2,1)S(1)}, u32[]{:S(2)}, u32[]{:S(2)}) collective-permute-start(bf16[128,512]{1,0:T(8,128)(2,1)S(1)} %get-tuple-element.21.input_ref), channel_id=1, source_target_pairs={{0,8},{4,12},{8,0},{12,4},{1,9},{5,13},{9,1},{13,5},{2,10},{6,14},... | collective-permute-start | bytes 393224 | tf_op jit(solution)/shard_map/ppermute | solution.py:193
  43.7 6.5 %collective-permute-start.2 = (bf16[128,512]{1,0:T(8,128)(2,1)S(1)}, bf16[128,512]{1,0:T(8,128)(2,1)S(1)}, u32[]{:S(2)}, u32[]{:S(2)}) collective-permute-start(bf16[128,512]{1,0:T(8,128)(2,1)S(1)} %get-tuple-element.16.layer_ref), channel_id=1, source_target_pairs={{0,2},{1,3},{2,0},{3,1},{4,6},{5,7},{6,4},{7,5},{8,10},{9,11},{10,... | collective-permute-start | bytes 393224 | tf_op jit(solution)/shard_map/ppermute | solution.py:193
  50.2 0.0 collective-permute-done.3.input_other
  50.2 0.7 %middle.1 = bf16[128,512]{1,0:T(8,128)(2,1)} custom-call(bf16[128,512]{1,0:T(8,128)(2,1)S(1)} %get-tuple-element.21.input_ref, bf16[128,512]{1,0:T(8,128)(2,1)S(1)} %collective-permute-done.3.input_other), custom_call_target="tpu_custom_call" | custom-call | bytes 524288 | tf_op jit(solution)/shard_map/middle/pallas_call | solution.py:244
  50.9 8.9 %all-to-all-done.1 = bf16[32,16,512]{2,1,0:T(8,128)(2,1)S(1)} async-done(((bf16[32,16,512]{2,1,0:T(8,128)(2,1)}), bf16[32,16,512]{2,1,0:T(8,128)(2,1)S(1)}, u32[]{:S(2)}, u32[]{:S(2)}) %all-to-all-start.1) | async-done | bytes 524320 | tf_op jit(solution)/shard_map/all_to_all | solution.py:189
  59.8 6.9 %newton.1 = (f32[1,16,512]{2,1,0:T(8,128)S(1)}, f32[1,16,512]{2,1,0:T(8,128)S(1)}) custom-call(s32[1]{0:T(128)} %bitcast.2.place_ref, bf16[512,512]{1,0:T(8,128)(2,1)S(1)} %bitcast.5), custom_call_target="tpu_custom_call" | custom-call | bytes 65536 | tf_op jit(solution)/shard_map/newton/pallas_call | solution.py:256
  66.6 0.0 collective-permute-done.2.layer_other
  66.6 0.7 %last.1 = (bf16[128,512]{1,0:T(8,128)(2,1)}, f32[1,16,512]{2,1,0:T(8,128)}, f32[1,16,512]{2,1,0:T(8,128)}) custom-call(bf16[128,512]{1,0:T(8,128)(2,1)S(1)} %get-tuple-element.16.layer_ref, bf16[128,512]{1,0:T(8,128)(2,1)S(1)} %collective-permute-done.2.layer_other, f32[1,16,512]{2,1,0:T(8,128)S(1)} %get-tuple-element.18.left_ref, ...), custom_call_target="tpu_custom_call" | custom-call | bytes 262144 | tf_op jit(solution)/shard_map/last/pallas_call | solution.py:272
Async XLA Ops:
  2.7 15.2 %copy-start = (bf16[512,512]{1,0:T(8,128)(2,1)S(1)}, bf16[512,512]{1,0:T(8,128)(2,1)}, u32[]{:S(2)}) copy-start(bf16[512,512]{1,0:T(8,128)(2,1)} %w_any.1) | copy-start | bytes 1572868
  2.7 15.2 %copy-start.1 = (bf16[128,512]{1,0:T(8,128)(2,1)S(1)}, bf16[128,512]{1,0:T(8,128)(2,1)}, u32[]{:S(2)}) copy-start(bf16[128,512]{1,0:T(8,128)(2,1)} %x_any.3) | copy-start | bytes 393220
  2.8 15.2 %copy-start.2 = (bf16[128,512]{1,0:T(8,128)(2,1)S(1)}, bf16[128,512]{1,0:T(8,128)(2,1)}, u32[]{:S(2)}) copy-start(bf16[128,512]{1,0:T(8,128)(2,1)} %g_any.3) | copy-start | bytes 393220
  2.8 29.2 %all-to-all-start = ((bf16[32,16,512]{2,1,0:T(8,128)(2,1)}), bf16[32,16,512]{2,1,0:T(8,128)(2,1)S(1)}, u32[]{:S(2)}, u32[]{:S(2)}) async-start(bf16[32,16,512]{2,1,0:T(8,128)(2,1)} %bitcast), calls=%async_computation | async-start | bytes 1048576 | tf_op jit(solution)/shard_map/all_to_all | solution.py:189
  18.8 6.9 %collective-permute-start = (bf16[128,512]{1,0:T(8,128)(2,1)S(1)}, bf16[128,512]{1,0:T(8,128)(2,1)S(1)}, u32[]{:S(2)}, u32[]{:S(2)}) collective-permute-start(bf16[128,512]{1,0:T(8,128)(2,1)S(1)} %get-tuple-element.14.input_ref), channel_id=1, source_target_pairs={{0,4},{4,0},{8,12},{12,8},{1,5},{5,1},{9,13},{13,9},{2,6},{6,2},{1... | collective-permute-start | bytes 393224 | tf_op jit(solution)/shard_map/ppermute | solution.py:193
  21.6 4.1 %collective-permute-start.1 = (bf16[128,512]{1,0:T(8,128)(2,1)S(1)}, bf16[128,512]{1,0:T(8,128)(2,1)S(1)}, u32[]{:S(2)}, u32[]{:S(2)}) collective-permute-start(bf16[128,512]{1,0:T(8,128)(2,1)S(1)} %get-tuple-element.15.layer_ref), channel_id=1, source_target_pairs={{0,1},{1,0},{2,3},{3,2},{4,5},{5,4},{6,7},{7,6},{8,9},{9,8},{10,11... | collective-permute-start | bytes 393224 | tf_op jit(solution)/shard_map/ppermute | solution.py:193
  32.9 26.9 %all-to-all-start.1 = ((bf16[32,16,512]{2,1,0:T(8,128)(2,1)}), bf16[32,16,512]{2,1,0:T(8,128)(2,1)S(1)}, u32[]{:S(2)}, u32[]{:S(2)}) async-start(bf16[32,16,512]{2,1,0:T(8,128)(2,1)} %bitcast.3), calls=%async_computation.1 | async-start | bytes 1048576 | tf_op jit(solution)/shard_map/all_to_all | solution.py:189
  40.4 9.8 %collective-permute-start.3 = (bf16[128,512]{1,0:T(8,128)(2,1)S(1)}, bf16[128,512]{1,0:T(8,128)(2,1)S(1)}, u32[]{:S(2)}, u32[]{:S(2)}) collective-permute-start(bf16[128,512]{1,0:T(8,128)(2,1)S(1)} %get-tuple-element.21.input_ref), channel_id=1, source_target_pairs={{0,8},{4,12},{8,0},{12,4},{1,9},{5,13},{9,1},{13,5},{2,10},{6,14},... | collective-permute-start | bytes 393224 | tf_op jit(solution)/shard_map/ppermute | solution.py:193
  43.7 22.9 %collective-permute-start.2 = (bf16[128,512]{1,0:T(8,128)(2,1)S(1)}, bf16[128,512]{1,0:T(8,128)(2,1)S(1)}, u32[]{:S(2)}, u32[]{:S(2)}) collective-permute-start(bf16[128,512]{1,0:T(8,128)(2,1)S(1)} %get-tuple-element.16.layer_ref), channel_id=1, source_target_pairs={{0,2},{1,3},{2,0},{3,1},{4,6},{5,7},{6,4},{7,5},{8,10},{9,11},{10,... | collective-permute-start | bytes 393224 | tf_op jit(solution)/shard_map/ppermute | solution.py:193

commit v12 on v10

--- a/solution.py
+++ b/solution.py
@@ -32,10 +32,13 @@
         copy.wait()
 
 
-def grad_kernel(tokens_all, x_any, g_any, grad_ref, x_ref, g_ref, sems):
+def grad_kernel(tokens_all, order, x_any, g_any, grad_ref, x_ref, g_ref, sems):
     fetch((x_any, g_any), (x_ref, g_ref), sems)
     grad = mm(x_ref[...], g_ref[...], ((0,), (0,)))
-    grad_ref[...] = (grad * (1.0 / tokens_all)).astype(BF16)
+    low = (grad * (1.0 / tokens_all)).astype(BF16)
+    slab = low.shape[0] // len(order)
+    for j, owner in enumerate(order):
+        grad_ref[j * slab : (j + 1) * slab, :] = low[owner * slab : (owner + 1) * slab, :]
 
 
 def pair_sum(left_ref, right_ref):
@@ -183,10 +186,9 @@
     return pltpu.CompilerParams(vmem_limit_bytes=mebibytes * 2**20)
 
 
-def exchange(values):
-    size = lax.axis_size("dp")
-    order = ORDER if size == len(ORDER) else range(size)
-    return lax.all_to_all(values, "dp", 0, 0, tiled=True, axis_index_groups=[list(order)])
+def exchange(values, order=None):
+    groups = None if order is None else [list(order)]
+    return lax.all_to_all(values, "dp", 0, 0, tiled=True, axis_index_groups=groups)
 
 
 def partner(values, axis, flip):
@@ -203,8 +205,9 @@
     whole = jax.ShapeDtypeStruct((tokens, extent), BF16)
     tokens_vmem = pltpu.VMEM((tokens, extent), BF16)
 
+    order = ORDER if groups == len(ORDER) else tuple(range(groups))
     grad_part = pl.pallas_call(
-        functools.partial(grad_kernel, tokens * groups),
+        functools.partial(grad_kernel, tokens * groups, order),
         out_shape=block,
         in_specs=[HBM, HBM],
         out_specs=VMEM,
@@ -213,7 +216,7 @@
         cost_estimate=pl.CostEstimate(flops=2 * tokens * extent * extent, bytes_accessed=2**20, transcendentals=0),
         name="grad_part",
     )(in_hbm(x_in), in_hbm(grad_out))
-    received = exchange(grad_part)
+    received = exchange(grad_part, order)
     layer_part, input_part = pl.pallas_call(
         outputs_kernel,
         out_shape=[whole, whole],

time: 64 us -> 64.3 us (level)
  the two profiles are of different devices: /device:TPU:6 before, /device:TPU:58 now
where the time goes in v12:
time: 64.3 us; the launch traced here: 63.9 us
  starting transfers between devices  35.6 us (55%)
  waiting for transfers between devices  15.4 us (24%)
  Pallas kernels  12.1 us (19%)
  between operations  0.76 us (1%)
    all_to_all x2, starting transfers between devices, exchange(): lax.all_to_all(values, 'dp', 0, 0, tiled=True, axis_index_groups=groups)  23.9 us
    ppermute x4, starting transfers between devices, partner(): return lax.ppermute(values, axis, [(i, i ^ flip) for i in range(4)])  11.7 us
    ppermute x4, waiting for transfers between devices, partner(): return lax.ppermute(values, axis, [(i, i ^ flip) for i in range(4)])  9.67 us
    pallas_call x1, Pallas kernels, shards(): pl.pallas_call(functools.partial(newton_kernel, slab), out_shape=[pltpu.V...  6.87 us
    all_to_all x2, waiting for transfers between devices, exchange(): lax.all_to_all(values, 'dp', 0, 0, tiled=True, axis_index_groups=groups)  5.77 us
    pallas_call x1, Pallas kernels, shards(): pl.pallas_call(functools.partial(grad_kernel, tokens * groups, order), ou...  2.09 us
  transfers between devices with their start and end apart: 6, of which 4 were waited for; matrix products, arithmetic and copies ran while one was open for 0% of the time, Pallas kernels for 13%

profile of v12, /device:TPU:58, one launch (start us, length us, event | category | flops | bytes accessed | tf_op | source)
XLA Modules:
  0.0 63.9 jit_solution(6160216072777916324)
XLA Ops:
  0.6 2.1 %grad_part.1.after_any = bf16[512,512]{1,0:T(8,128)(2,1)} custom-call(bf16[128,512]{1,0:T(8,128)(2,1)} %x_any.3, bf16[128,512]{1,0:T(8,128)(2,1)} %g_any.3), custom_call_target="tpu_custom_call" | custom-call | flops 67108864 | bytes 1048576 | tf_op jit(solution)/shard_map/grad_part/pallas_call | solution.py:209
  2.7 0.0 copy-start
  2.7 0.0 copy-start.1
  2.8 0.0 copy-start.2
  2.8 14.5 %all-to-all-start = ((bf16[32,16,512]{2,1,0:T(8,128)(2,1)}), bf16[32,16,512]{2,1,0:T(8,128)(2,1)S(1)}, u32[]{:S(2)}, u32[]{:S(2)}) async-start(bf16[32,16,512]{2,1,0:T(8,128)(2,1)} %bitcast), calls=%async_computation | async-start | bytes 1048576 | tf_op jit(solution)/shard_map/all_to_all | solution.py:191
  17.3 0.0 copy-done
  17.3 0.0 copy-done.1
  17.3 0.0 copy-done.2
  17.3 0.8 %outputs_part.1 = (bf16[128,512]{1,0:T(8,128)(2,1)S(1)}, bf16[128,512]{1,0:T(8,128)(2,1)S(1)}) custom-call(bf16[128,512]{1,0:T(8,128)(2,1)S(1)} %copy-done.1, bf16[128,512]{1,0:T(8,128)(2,1)S(1)} %copy-done.2, bf16[512,512]{1,0:T(8,128)(2,1)S(1)} %copy-done, bf16[512,512]{1,0:T(8,128)(2,1)} %grad_part.1.after_any), custom_call_target="tpu_custom_call" | custom-call | flops 134217728 | bytes 1048576 | tf_op jit(solution)/shard_map/outputs_part/pallas_call | solution.py:220
  18.1 1.9 %collective-permute-start.1 = (bf16[128,512]{1,0:T(8,128)(2,1)S(1)}, bf16[128,512]{1,0:T(8,128)(2,1)S(1)}, u32[]{:S(2)}, u32[]{:S(2)}) collective-permute-start(bf16[128,512]{1,0:T(8,128)(2,1)S(1)} %get-tuple-element.16.layer_ref), channel_id=1, source_target_pairs={{0,1},{1,0},{2,3},{3,2},{4,5},{5,4},{6,7},{7,6},{8,9},{9,8},{10,11... | collective-permute-start | bytes 393224 | tf_op jit(solution)/shard_map/ppermute | solution.py:195
  20.0 2.4 %collective-permute-start = (bf16[128,512]{1,0:T(8,128)(2,1)S(1)}, bf16[128,512]{1,0:T(8,128)(2,1)S(1)}, u32[]{:S(2)}, u32[]{:S(2)}) collective-permute-start(bf16[128,512]{1,0:T(8,128)(2,1)S(1)} %get-tuple-element.15.input_ref), channel_id=1, source_target_pairs={{0,4},{4,0},{8,12},{12,8},{1,5},{5,1},{9,13},{13,9},{2,6},{6,2},{1... | collective-permute-start | bytes 393224 | tf_op jit(solution)/shard_map/ppermute | solution.py:195
  22.5 0.0 collective-permute-done.1.layer_any.layer_other
  22.5 5.3 %collective-permute-done.input_other = bf16[128,512]{1,0:T(8,128)(2,1)S(1)} collective-permute-done((bf16[128,512]{1,0:T(8,128)(2,1)S(1)}, bf16[128,512]{1,0:T(8,128)(2,1)S(1)}, u32[]{:S(2)}, u32[]{:S(2)}) %collective-permute-start) | collective-permute-done | bytes 131104 | tf_op jit(solution)/shard_map/ppermute | solution.py:195
  27.8 2.6 %all-to-all-done = bf16[32,16,512]{2,1,0:T(8,128)(2,1)S(1)} async-done(((bf16[32,16,512]{2,1,0:T(8,128)(2,1)}), bf16[32,16,512]{2,1,0:T(8,128)(2,1)S(1)}, u32[]{:S(2)}, u32[]{:S(2)}) %all-to-all-start) | async-done | bytes 524320 | tf_op jit(solution)/shard_map/all_to_all | solution.py:191
  30.4 0.9 %sums.1 = (bf16[512,512]{1,0:T(8,128)(2,1)}, bf16[128,512]{1,0:T(8,128)(2,1)S(1)}) custom-call(bf16[512,512]{1,0:T(8,128)(2,1)S(1)} %bitcast.5, bf16[128,512]{1,0:T(8,128)(2,1)S(1)} %get-tuple-element.15.input_ref, bf16[128,512]{1,0:T(8,128)(2,1)S(1)} %collective-permute-done.input_other, bf16[128,512]{1,0:T(8,128)(2,1)S(1)} %collective-permute-done.1.layer_any.layer_other), custom_call_target="tpu_custom_call" | custom-call | flops 262144 | bytes 1048576 | tf_op jit(solution)/shard_map/sums/pallas_call | solution.py:236
  31.3 9.4 %all-to-all-start.1 = ((bf16[32,16,512]{2,1,0:T(8,128)(2,1)}), bf16[32,16,512]{2,1,0:T(8,128)(2,1)S(1)}, u32[]{:S(2)}, u32[]{:S(2)}) async-start(bf16[32,16,512]{2,1,0:T(8,128)(2,1)} %bitcast.3), calls=%async_computation.1 | async-start | bytes 1048576 | tf_op jit(solution)/shard_map/all_to_all | solution.py:191
  40.8 4.0 %collective-permute-start.2 = (bf16[128,512]{1,0:T(8,128)(2,1)S(1)}, bf16[128,512]{1,0:T(8,128)(2,1)S(1)}, u32[]{:S(2)}, u32[]{:S(2)}) collective-permute-start(bf16[128,512]{1,0:T(8,128)(2,1)S(1)} %get-tuple-element.17.input_ref), channel_id=1, source_target_pairs={{0,8},{4,12},{8,0},{12,4},{1,9},{5,13},{9,1},{13,5},{2,10},{6,14},... | collective-permute-start | bytes 393224 | tf_op jit(solution)/shard_map/ppermute | solution.py:195
  44.8 4.3 %collective-permute-done.2.input_other = bf16[128,512]{1,0:T(8,128)(2,1)S(1)} collective-permute-done((bf16[128,512]{1,0:T(8,128)(2,1)S(1)}, bf16[128,512]{1,0:T(8,128)(2,1)S(1)}, u32[]{:S(2)}, u32[]{:S(2)}) %collective-permute-start.2) | collective-permute-done | bytes 131104 | tf_op jit(solution)/shard_map/ppermute | solution.py:195
  49.1 0.7 %middle.1 = (bf16[128,512]{1,0:T(8,128)(2,1)}, bf16[128,512]{1,0:T(8,128)(2,1)S(1)}) custom-call(bf16[128,512]{1,0:T(8,128)(2,1)S(1)} %get-tuple-element.17.input_ref, bf16[128,512]{1,0:T(8,128)(2,1)S(1)} %collective-permute-done.2.input_other, bf16[128,512]{1,0:T(8,128)(2,1)S(1)} %get-tuple-element.16.layer_ref, ...), custom_call_target="tpu_custom_call" | custom-call | bytes 524288 | tf_op jit(solution)/shard_map/middle/pallas_call | solution.py:247
  49.8 3.3 %collective-permute-start.3 = (bf16[128,512]{1,0:T(8,128)(2,1)S(1)}, bf16[128,512]{1,0:T(8,128)(2,1)S(1)}, u32[]{:S(2)}, u32[]{:S(2)}) collective-permute-start(bf16[128,512]{1,0:T(8,128)(2,1)S(1)} %get-tuple-element.18.layer_ref), channel_id=1, source_target_pairs={{0,2},{1,3},{2,0},{3,1},{4,6},{5,7},{6,4},{7,5},{8,10},{9,11},{10,... | collective-permute-start | bytes 393224 | tf_op jit(solution)/shard_map/ppermute | solution.py:195
  53.1 3.2 %all-to-all-done.1 = bf16[32,16,512]{2,1,0:T(8,128)(2,1)S(1)} async-done(((bf16[32,16,512]{2,1,0:T(8,128)(2,1)}), bf16[32,16,512]{2,1,0:T(8,128)(2,1)S(1)}, u32[]{:S(2)}, u32[]{:S(2)}) %all-to-all-start.1) | async-done | bytes 524320 | tf_op jit(solution)/shard_map/all_to_all | solution.py:191
  56.3 6.9 %newton.1 = (f32[1,16,512]{2,1,0:T(8,128)S(1)}, f32[1,16,512]{2,1,0:T(8,128)S(1)}) custom-call(s32[1]{0:T(128)} %bitcast.2.place_ref, bf16[512,512]{1,0:T(8,128)(2,1)S(1)} %bitcast.6), custom_call_target="tpu_custom_call" | custom-call | bytes 65536 | tf_op jit(solution)/shard_map/newton/pallas_call | solution.py:259
  63.2 0.0 collective-permute-done.3.layer_other
  63.2 0.7 %last.1 = (bf16[128,512]{1,0:T(8,128)(2,1)}, f32[1,16,512]{2,1,0:T(8,128)}, f32[1,16,512]{2,1,0:T(8,128)}) custom-call(bf16[128,512]{1,0:T(8,128)(2,1)S(1)} %get-tuple-element.18.layer_ref, bf16[128,512]{1,0:T(8,128)(2,1)S(1)} %collective-permute-done.3.layer_other, f32[1,16,512]{2,1,0:T(8,128)S(1)} %get-tuple-element.20.left_ref, ...), custom_call_target="tpu_custom_call" | custom-call | bytes 262144 | tf_op jit(solution)/shard_map/last/pallas_call | solution.py:275
Async XLA Ops:
  2.7 14.5 %copy-start = (bf16[512,512]{1,0:T(8,128)(2,1)S(1)}, bf16[512,512]{1,0:T(8,128)(2,1)}, u32[]{:S(2)}) copy-start(bf16[512,512]{1,0:T(8,128)(2,1)} %w_any.1) | copy-start | bytes 1572868
  2.7 14.5 %copy-start.1 = (bf16[128,512]{1,0:T(8,128)(2,1)S(1)}, bf16[128,512]{1,0:T(8,128)(2,1)}, u32[]{:S(2)}) copy-start(bf16[128,512]{1,0:T(8,128)(2,1)} %x_any.3) | copy-start | bytes 393220
  2.8 14.5 %copy-start.2 = (bf16[128,512]{1,0:T(8,128)(2,1)S(1)}, bf16[128,512]{1,0:T(8,128)(2,1)}, u32[]{:S(2)}) copy-start(bf16[128,512]{1,0:T(8,128)(2,1)} %g_any.3) | copy-start | bytes 393220
  2.8 27.7 %all-to-all-start = ((bf16[32,16,512]{2,1,0:T(8,128)(2,1)}), bf16[32,16,512]{2,1,0:T(8,128)(2,1)S(1)}, u32[]{:S(2)}, u32[]{:S(2)}) async-start(bf16[32,16,512]{2,1,0:T(8,128)(2,1)} %bitcast), calls=%async_computation | async-start | bytes 1048576 | tf_op jit(solution)/shard_map/all_to_all | solution.py:191
  18.1 4.4 %collective-permute-start.1 = (bf16[128,512]{1,0:T(8,128)(2,1)S(1)}, bf16[128,512]{1,0:T(8,128)(2,1)S(1)}, u32[]{:S(2)}, u32[]{:S(2)}) collective-permute-start(bf16[128,512]{1,0:T(8,128)(2,1)S(1)} %get-tuple-element.16.layer_ref), channel_id=1, source_target_pairs={{0,1},{1,0},{2,3},{3,2},{4,5},{5,4},{6,7},{7,6},{8,9},{9,8},{10,11... | collective-permute-start | bytes 393224 | tf_op jit(solution)/shard_map/ppermute | solution.py:195
  20.0 7.8 %collective-permute-start = (bf16[128,512]{1,0:T(8,128)(2,1)S(1)}, bf16[128,512]{1,0:T(8,128)(2,1)S(1)}, u32[]{:S(2)}, u32[]{:S(2)}) collective-permute-start(bf16[128,512]{1,0:T(8,128)(2,1)S(1)} %get-tuple-element.15.input_ref), channel_id=1, source_target_pairs={{0,4},{4,0},{8,12},{12,8},{1,5},{5,1},{9,13},{13,9},{2,6},{6,2},{1... | collective-permute-start | bytes 393224 | tf_op jit(solution)/shard_map/ppermute | solution.py:195
  31.3 24.9 %all-to-all-start.1 = ((bf16[32,16,512]{2,1,0:T(8,128)(2,1)}), bf16[32,16,512]{2,1,0:T(8,128)(2,1)S(1)}, u32[]{:S(2)}, u32[]{:S(2)}) async-start(bf16[32,16,512]{2,1,0:T(8,128)(2,1)} %bitcast.3), calls=%async_computation.1 | async-start | bytes 1048576 | tf_op jit(solution)/shard_map/all_to_all | solution.py:191
  40.8 8.4 %collective-permute-start.2 = (bf16[128,512]{1,0:T(8,128)(2,1)S(1)}, bf16[128,512]{1,0:T(8,128)(2,1)S(1)}, u32[]{:S(2)}, u32[]{:S(2)}) collective-permute-start(bf16[128,512]{1,0:T(8,128)(2,1)S(1)} %get-tuple-element.17.input_ref), channel_id=1, source_target_pairs={{0,8},{4,12},{8,0},{12,4},{1,9},{5,13},{9,1},{13,5},{2,10},{6,14},... | collective-permute-start | bytes 393224 | tf_op jit(solution)/shard_map/ppermute | solution.py:195
  49.8 13.4 %collective-permute-start.3 = (bf16[128,512]{1,0:T(8,128)(2,1)S(1)}, bf16[128,512]{1,0:T(8,128)(2,1)S(1)}, u32[]{:S(2)}, u32[]{:S(2)}) collective-permute-start(bf16[128,512]{1,0:T(8,128)(2,1)S(1)} %get-tuple-element.18.layer_ref), channel_id=1, source_target_pairs={{0,2},{1,3},{2,0},{3,1},{4,6},{5,7},{6,4},{7,5},{8,10},{9,11},{10,... | collective-permute-start | bytes 393224 | tf_op jit(solution)/shard_map/ppermute | solution.py:195
